TPU v7x, 256 devices: a whole 4x4x8 slice. The times are simulated.
256 devices in a mesh: ctx: 128 (over z, y_lo, x, core), head: 2 (over y_hi).
Axes of the slice: x: 4, y: 4 (y_hi: 2, y_lo: 2; y = y_hi * 2 + y_lo), z: 8, core: 2. Of those that a mesh axis runs over, the one named last changes fastest.
Arguments:
- index_queries: bfloat16 [64, 64, 128], P(None, 'head'), may hold values from -310 to 310
- head_weights: float32 [64, 64], P(None, 'head'), may hold values from -4 to 4
- index_keys: bfloat16 [131072, 128], P('ctx'), may hold values from -6 to 6
- main_target: float32 [64, 131072], P(None, 'ctx'), may hold values from 0.01 to 1
Outputs:
- grad_queries: float32 [64, 64, 128], P(None, 'head')
- grad_weights: float32 [64, 64], P(None, 'head')
- grad_keys: float32 [131072, 128], P('ctx')
- loss_rows: float32 [64], replicated
All inputs are finite; a program needn't handle non-finite values.
Results may differ from a plain program's by a relative error of at most 0.007.
Values sent between devices are 32-bit elements; how exact they have to be, the bound alone decides.
No kernel may reach another device: no remote copies, remote signals or barrier semaphores. Data moves between devices by JAX's collectives and lax.ppermute only.
A program may use at most 64 MiB of HBM per device.

v0:
```python
import jax
import jax.numpy as jnp
from jax import lax
from jax.sharding import PartitionSpec as P

H = 64


def on_device(index_queries, head_weights, index_keys, main_target):
    highest = lax.Precision.HIGHEST
    query_rows, local_heads, head_width = index_queries.shape
    key_rows = index_keys.shape[0]
    cycle_size = lax.axis_size("ctx")
    scale_width = head_width ** (-0.5)
    scale_heads = H ** (-0.5)
    group_size = min(8, local_heads)
    group_count = local_heads // group_size
    query_groups = index_queries.reshape(query_rows, group_count, group_size, head_width).transpose(
        1, 0, 2, 3
    )
    weight_groups = head_weights.reshape(query_rows, group_count, group_size).transpose(1, 0, 2)

    def head_logits(queries_part):
        return (
            jnp.einsum("tjd,sd->tjs", queries_part, index_keys, preferred_element_type=jnp.float32)
            * scale_width
        )

    def score_step(running, inputs):
        queries_part, weights_part = inputs
        relu_part = jnp.maximum(head_logits(queries_part), 0.0)
        added = jnp.einsum("tj,tjs->ts", weights_part, relu_part, precision=highest) * scale_heads
        return (running + added, None)

    partial_index, _ = lax.scan(
        score_step, jnp.zeros((query_rows, key_rows), jnp.float32), (query_groups, weight_groups)
    )
    index = lax.psum(partial_index, "head")
    key_pos = lax.axis_index("ctx") * key_rows + jnp.arange(key_rows, dtype=jnp.int32)
    query_pos = key_rows * cycle_size - query_rows + jnp.arange(query_rows, dtype=jnp.int32)
    valid = key_pos[None, :] <= query_pos[:, None]
    masked = jnp.where(valid, main_target, 0.0)
    local_mass = jnp.sum(masked, axis=1)
    local_ent = jnp.sum(masked * jnp.log(main_target), axis=1)
    local_cross = jnp.sum(masked * index, axis=1)
    local_max = jnp.max(jnp.where(valid, index, -jnp.inf), axis=1)
    row_max = lax.pmax(local_max, "ctx")
    expo = jnp.where(valid, jnp.exp(index - row_max[:, None]), 0.0)
    denom, mass, entropy_sum, cross = lax.psum(
        (jnp.sum(expo, axis=1), local_mass, local_ent, local_cross), "ctx"
    )
    loss_rows = entropy_sum / mass - jnp.log(mass) - cross / mass + row_max + jnp.log(denom)
    grad_index = (expo / denom[:, None] - masked / mass[:, None]) / query_rows

    def back_step(key_grad, inputs):
        queries_part, weights_part = inputs
        logits = head_logits(queries_part)
        weight_grad = (
            jnp.einsum("ts,tjs->tj", grad_index, jnp.maximum(logits, 0.0), precision=highest)
            * scale_heads
        )
        logit_grad = (
            grad_index[:, None, :]
            * weights_part[:, :, None]
            * scale_heads
            * jnp.where(logits > 0, 1.0, 0.0)
        ).astype(jnp.bfloat16)
        query_grad = (
            jnp.einsum("tjs,sd->tjd", logit_grad, index_keys, preferred_element_type=jnp.float32)
            * scale_width
        )
        key_grad = (
            key_grad
            + jnp.einsum(
                "tjs,tjd->sd", logit_grad, queries_part, preferred_element_type=jnp.float32
            )
            * scale_width
        )
        return (key_grad, (query_grad, weight_grad))

    local_keys_grad, (query_parts, weight_parts) = lax.scan(
        back_step, jnp.zeros((key_rows, head_width), jnp.float32), (query_groups, weight_groups)
    )
    grad_keys = lax.psum(local_keys_grad, "head")
    partial_queries = query_parts.transpose(1, 0, 2, 3).reshape(query_rows, local_heads, head_width)
    partial_weights = weight_parts.transpose(1, 0, 2).reshape(query_rows, local_heads)
    grad_queries, grad_weights = lax.psum((partial_queries, partial_weights), "ctx")
    return (grad_queries, grad_weights, grad_keys, loss_rows)


def solution(mesh):
    placed = (P(None, "head", None), P(None, "head"), P("ctx", None), P(None, "ctx"))
    return jax.shard_map(
        on_device,
        mesh=mesh,
        in_specs=placed,
        out_specs=(P(None, "head", None), P(None, "head"), P("ctx", None), P()),
        check_vma=False,
    )
```

profile of v0, /device:TPU:1, one launch (start us, length us, event | category | flops | bytes accessed | tf_op | source)
XLA Modules:
  0.0 1797.9 jit_solution(8390644732494685221)
XLA Ops:
  8.4 16.9 while.26
  10.6 1.9 fusion.61
  14.8 1.9 fusion.61
  19.0 1.9 fusion.61
  23.3 1.9 fusion.61
  26.1 39.8 %all-reduce.6.cloned.1.call-done = f32[64,1024]{1,0:T(8,128)} async-done(((f32[64,1024]{1,0:T(8,128)}), f32[64,1024]{1,0:T(8,128)}) %all-reduce.6.cloned.1.call-update) | async-done | bytes 262160 | tf_op jit(solution)/shard_map/psum | solution.py:38
  67.1 276.1 %pmax.7 = f32[64]{0:T(128)S(1)} all-reduce(f32[64]{0:T(128)S(1)} %fusion.34), channel_id=1, replica_groups=mesh['ctx'=128,'head'=2] {'ctx'}, use_global_device_ids=true, to_apply=%region_4.5 | all-reduce | flops 64 | bytes 512 | tf_op jit(solution)/shard_map/pmax | solution.py:47
  344.4 280.0 %all-reduce.1 = (f32[64]{0:T(128)S(1)}, f32[64]{0:T(128)S(1)}) all-reduce(f32[64]{0:T(128)S(1)} %get-tuple-element.145, f32[64]{0:T(128)S(1)} %get-tuple-element.144), channel_id=1, replica_groups=mesh['ctx'=128,'head'=2] {'ctx'}, use_global_device_ids=true, to_apply=%region_8.9 | all-reduce | flops 128 | bytes 1024 | tf_op jit(solution)/shard_map/psum | solution.py:49
  626.3 43.3 %while.27 = (s32[]{:T(128)}, f32[1024,128]{1,0:T(8,128)S(1)}, f32[4,64,8,128]{3,2,1,0:T(8,128)}, f32[4,64,8]{1,2,0:T(8,128)S(1)}, f32[64,1024]{1,0:T(8,128)}, /*...) while((s32[]{:T(128)}, f32[1024,128]{1,0:T(8,128)S(1)}, ...), condition=%wide.region_10.11_spmd.clone, body=%wide.region_9.10_spmd.clone.sunk | while | flops 417792512 | bytes 13429427 | solution.py:81
  627.8 4.3 fusion.70
  633.0 2.2 fusion.72
  635.2 1.9 fusion.71
  638.6 4.3 fusion.70
  643.8 2.2 fusion.72
  646.0 1.9 fusion.71
  649.4 4.3 fusion.70
  654.6 2.2 fusion.72
  660.2 4.3 fusion.70
  665.4 2.2 fusion.72
  667.7 1.9 fusion.71
  670.4 2.4 copy_bitcast_fusion
  672.8 542.9 %all-reduce = (f32[64,32]{0,1:T(8,128)}, f32[64]{0:T(128)S(1)}, f32[64]{0:T(128)S(1)}) all-reduce(f32[64,32]{0,1:T(8,128)S(1)} %bitcast.91, f32[64]{0:T(128)S(1)} %get-tuple-element.143, f32[64]{0:T(128)S(1)} %get-tuple-element.142), channel_id=1, replica_groups=mesh['ctx'=128,'head'=2] {'ctx'}, use_global_device_ids=true, to_apply=%region_12.13 | all-reduce | flops 2176 | bytes 17408 | tf_op jit(solution)/shard_map/psum | solution.py:87
  1216.3 572.0 %all-reduce.8.cloned.1.call-done = f32[64,32,128]{2,1,0:T(8,128)} async-done(((f32[64,32,128]{2,1,0:T(8,128)}), f32[64,32,128]{2,1,0:T(8,128)}) %all-reduce.8.cloned.1.call-update) | async-done | bytes 1048592 | tf_op jit(solution)/shard_map/psum | solution.py:87
  1788.3 2.3 copy.62
  (76 shorter events, 28.8 us)
Async XLA Ops:
  7.2 58.8 %all-reduce.6.cloned.1.call-start = ((), (), s32[]{:S(2)}) async-start(), calls=%async_computation | async-start | bytes 524288 | tf_op jit(solution)/shard_map/psum | solution.py:38
  8.4 334.8 %copy-start.2 = (f32[64,1024]{1,0:T(8,128)S(1)}, f32[64,1024]{1,0:T(8,128)}, u32[]{:S(2)}) copy-start(f32[64,1024]{1,0:T(8,128)} %param.11) | copy-start | bytes 786436
  25.3 0.7 copy-start.1
  26.0 1190.2 %all-reduce.10.cloned.1.call-start = ((), (), s32[]{:S(2)}) async-start(), calls=%async_computation.2 | async-start | bytes 1048576 | tf_op jit(solution)/shard_map/psum | solution.py:84
  626.3 1.5 copy-start.5
  626.3 6.7 copy-start
  637.1 1.5 copy-start.5
  637.1 6.7 copy-start
  647.9 1.5 copy-start.5
  647.9 6.7 copy-start
  658.7 1.5 copy-start.5
  658.7 6.7 copy-start
  669.5 0.8 copy-start.3
  670.4 1117.9 %all-reduce.8.cloned.1.call-start = ((), (), s32[]{:S(2)}) async-start(), calls=%async_computation.1 | async-start | bytes 2097152 | tf_op jit(solution)/shard_map/psum | solution.py:87
  1216.3 574.3 %copy-start.4 = (f32[1024,128]{1,0:T(8,128)S(1)}, f32[1024,128]{1,0:T(8,128)}, u32[]{:S(2)}) copy-start(f32[1024,128]{1,0:T(8,128)} %all-reduce.10.cloned.1.call-done) | copy-start | bytes 1572868
Sparse Core Ops, SparseCore 0:
  26.1 39.7 all-reduce.5
  670.5 36.9 all-reduce.9
  710.1 1078.1 all-reduce.7
where the time goes:
time: 1800 us
  blocking collectives  1100 us (61%)
  waiting for transfers between devices  612 us (34%)
  matrix products  52.7 us (3%)
    psum x1, waiting for transfers between devices, on_device(): lax.psum((partial_queries, partial_weights), 'ctx')  572 us
    psum x1, blocking collectives, on_device(): lax.psum((partial_queries, partial_weights), 'ctx')  543 us
    psum x1, blocking collectives, on_device(): lax.psum((jnp.sum(expo, axis=1), local_mass, local_ent, local_cross), 'ctx')  280 us
    pmax x1, blocking collectives, on_device(): row_max = lax.pmax(local_max, 'ctx')  276 us
    psum x1, waiting for transfers between devices, on_device(): index = lax.psum(partial_index, 'head')  39.8 us
  transfers between devices with their start and end apart: 3, of which 2 were waited for; matrix products, arithmetic and copies ran while one was open for 0% of the time, Pallas kernels for 0%

commit v1 on v0

v1 whole, which is shorter than its diff:
```python
import functools

import jax
import jax.numpy as jnp
from jax import lax
from jax.experimental import pallas as pl
from jax.experimental.pallas import tpu as pltpu
from jax.sharding import Mesh, PartitionSpec as P

H = 64
T = 64
JL = 32
D = 128
S = 1024
ROWS = T * JL
POS = 131072 - T
SCALE = (D**-0.5) * (H**-0.5)
CTX = ("z", "yl", "x", "c")
CHIPS = ("z", "yl", "x")
N_CHIPS = 64
VMEM = 48 * 1024 * 1024
NT = (((1,), (1,)), ((), ()))


def params():
    return pltpu.CompilerParams(vmem_limit_bytes=VMEM)


def whole(shape):
    return pl.BlockSpec(shape, lambda *_: (0,) * len(shape))


def score_kernel(q_ref, w_ref, k_ref, out_ref):
    width = out_ref.shape[1]
    acc = jnp.zeros((T, width), jnp.float32)
    w = w_ref[...]
    step = 8
    for j0 in range(0, JL, step):
        logits = lax.dot_general(
            q_ref[j0 * T : (j0 + step) * T, :], k_ref[...], NT, preferred_element_type=jnp.float32
        )
        for j in range(step):
            part = jnp.maximum(logits[j * T : (j + 1) * T, :], 0.0)
            acc = acc + w[:, j0 + j : j0 + j + 1] * part
    out_ref[...] = acc * SCALE


def score(q, w, k):
    tile = 256
    return pl.pallas_call(
        score_kernel,
        grid=(S // tile,),
        in_specs=[whole((ROWS, D)), whole((T, JL)), pl.BlockSpec((tile, D), lambda i: (i, 0))],
        out_specs=pl.BlockSpec((T, tile), lambda i: (0, i)),
        out_shape=jax.ShapeDtypeStruct((T, S), jnp.float32),
        compiler_params=params(),
        name="score",
    )(q, w, k)


def valid_mask(ctx):
    key = ctx * S + lax.broadcasted_iota(jnp.int32, (T, S), 1)
    query = POS + lax.broadcasted_iota(jnp.int32, (T, S), 0)
    return key <= query


def stats_kernel(ctx_ref, mine_ref, other_ref, target_ref, index_ref, stats_ref):
    index = mine_ref[...] + other_ref[...]
    index_ref[...] = index
    valid = valid_mask(ctx_ref[0])
    target = target_ref[...]
    masked = jnp.where(valid, target, 0.0)
    row_max = jnp.max(jnp.where(valid, index, -jnp.inf), axis=1, keepdims=True)
    denom = jnp.sum(jnp.where(valid, jnp.exp(index - row_max), 0.0), axis=1, keepdims=True)
    mass = jnp.sum(masked, axis=1, keepdims=True)
    entropy = jnp.sum(masked * jnp.log(target), axis=1, keepdims=True)
    cross = jnp.sum(masked * index, axis=1, keepdims=True)
    lane = lax.broadcasted_iota(jnp.int32, (T, 128), 1)
    packed = jnp.zeros((T, 128), jnp.float32)
    for i, column in enumerate((row_max, denom, mass, entropy, cross)):
        packed = jnp.where(lane == i, column, packed)
    packed = jnp.concatenate([packed, jnp.zeros((128 - T, 128), jnp.float32)], axis=0)
    stats_ref[...] = jnp.transpose(packed)[:8, :]


def local_stats(ctx, mine, other, target):
    return pl.pallas_call(
        stats_kernel,
        in_specs=[pl.BlockSpec(memory_space=pltpu.SMEM)] + [pl.BlockSpec(memory_space=pltpu.VMEM)] * 3,
        out_specs=[pl.BlockSpec(memory_space=pltpu.VMEM)] * 2,
        out_shape=[
            jax.ShapeDtypeStruct((T, S), jnp.float32),
            jax.ShapeDtypeStruct((8, 128), jnp.float32),
        ],
        compiler_params=params(),
        name="stats",
    )(ctx, mine, other, target)


def grad_index_of(ctx, index, target, stats):
    columns = jnp.transpose(jnp.concatenate([stats, jnp.zeros((120, 128), jnp.float32)], axis=0))[:T, :]
    row_max, denom, mass = columns[:, 0:1], columns[:, 1:2], columns[:, 2:3]
    gap = jnp.exp(index - row_max) / denom - target / mass
    return jnp.where(valid_mask(ctx), gap, 0.0) * (SCALE / T)


def query_kernel(who_ref, index_ref, target_ref, stats_ref, q_ref, k_ref, out_ref, g_ref):
    @pl.when(pl.program_id(0) == 0)
    def _():
        g_ref[...] = grad_index_of(who_ref[0], index_ref[...], target_ref[...], stats_ref[...])

    heads = q_ref.shape[0] // T
    logits = lax.dot_general(q_ref[...], k_ref[...], NT, preferred_element_type=jnp.float32)
    g = jnp.concatenate([g_ref[...]] * heads, axis=0)
    picked = jnp.where(logits > 0.0, g, 0.0).astype(jnp.bfloat16)
    out_ref[...] = jnp.dot(picked, k_ref[...], preferred_element_type=jnp.float32)


def query_grads(who, index, target, stats, q, k):
    block = 4 * T
    steps = ROWS // block
    grid_spec = pltpu.PrefetchScalarGridSpec(
        num_scalar_prefetch=1,
        grid=(steps,),
        in_specs=[
            whole((T, S)),
            whole((T, S)),
            whole((8, 128)),
            pl.BlockSpec((block, D), lambda i, who: ((i + who[1] * (steps // 2)) % steps, 0)),
            whole((S, D)),
        ],
        out_specs=pl.BlockSpec((block, D), lambda i, who: (i, 0)),
        scratch_shapes=[pltpu.VMEM((T, S), jnp.float32)],
    )
    return pl.pallas_call(
        query_kernel,
        grid_spec=grid_spec,
        out_shape=jax.ShapeDtypeStruct((ROWS, D), jnp.float32),
        compiler_params=params(),
        name="query_grads",
    )(who, index, target, stats, q, k)


def key_kernel(who_ref, index_ref, target_ref, stats_ref, q_ref, qw_ref, k_ref, out_ref, g_ref):
    @pl.when(pl.program_id(0) == 0)
    def _():
        g = grad_index_of(who_ref[0], index_ref[...], target_ref[...], stats_ref[...])
        g_ref[...] = jnp.transpose(jnp.concatenate([g, g], axis=0))

    tile = k_ref.shape[0]
    g = g_ref[pl.ds(pl.program_id(0) * tile, tile), :]
    acc = jnp.zeros((tile, D), jnp.float32)
    span = 1024
    for r in range(0, ROWS, span):
        logits = lax.dot_general(
            k_ref[...], q_ref[r : r + span, :], NT, preferred_element_type=jnp.float32
        )
        picked = jnp.where(logits > 0.0, jnp.concatenate([g] * (span // 128), axis=1), 0.0)
        acc = acc + jnp.dot(
            picked.astype(jnp.bfloat16), qw_ref[r : r + span, :], preferred_element_type=jnp.float32
        )
    out_ref[...] = acc


def key_grads(who, index, target, stats, q, qw, k):
    tile = 256
    return pl.pallas_call(
        key_kernel,
        grid=(S // tile,),
        in_specs=[
            pl.BlockSpec(memory_space=pltpu.SMEM),
            whole((T, S)),
            whole((T, S)),
            whole((8, 128)),
            whole((ROWS, D)),
            whole((ROWS, D)),
            pl.BlockSpec((tile, D), lambda i: (i, 0)),
        ],
        out_specs=pl.BlockSpec((tile, D), lambda i: (i, 0)),
        out_shape=jax.ShapeDtypeStruct((S, D), jnp.float32),
        scratch_shapes=[pltpu.VMEM((S, 128), jnp.float32)],
        compiler_params=params(),
        name="key_grads",
    )(who, index, target, stats, q, qw, k)


def merge(stats):
    row_max = jnp.max(stats[:, 0], axis=0)
    denom = jnp.sum(stats[:, 1] * jnp.exp(stats[:, 0] - row_max), axis=0)
    rest = jnp.sum(stats[:, 2:], axis=0)
    return jnp.concatenate([row_max[None], denom[None], rest], axis=0)


def on_device(index_queries, head_weights, index_keys, main_target):
    swap = [(0, 1), (1, 0)]
    core = lax.axis_index("c")
    ctx = lax.axis_index(CTX)
    who = jnp.stack([ctx, core]).astype(jnp.int32)
    q = index_queries.transpose(1, 0, 2).reshape(ROWS, D)
    partial_index = score(q, head_weights, index_keys)
    other_index = lax.ppermute(partial_index, "yh", swap)
    index, stats = local_stats(who, partial_index, other_index, main_target)

    pair = jnp.stack([stats, lax.ppermute(stats, "c", swap)])
    pair = merge(pair)
    spread = jnp.broadcast_to(pair[None], (N_CHIPS, 8, 128))
    stats = merge(lax.all_to_all(spread, CHIPS, 0, 0, tiled=True))
    row_max, denom, mass, entropy, cross = (stats[i, :T] for i in range(5))
    loss_rows = entropy / mass - jnp.log(mass) - cross / mass + row_max + jnp.log(denom)

    part = query_grads(who, index, main_target, stats, q, index_keys)
    half = ROWS // 2
    mine = part[:half] + lax.ppermute(part[half:], "c", swap)
    chunks = lax.all_to_all(mine.reshape(N_CHIPS, half // N_CHIPS, D), CHIPS, 0, 0, tiled=True)
    chunk = jnp.sum(chunks, axis=0)

    weighted = (head_weights.T.reshape(ROWS, 1) * q.astype(jnp.float32)).astype(jnp.bfloat16)
    key_part = key_grads(who, index, main_target, stats, q, weighted, index_keys)
    grad_keys = key_part + lax.ppermute(key_part, "yh", swap)

    spread = jnp.broadcast_to(chunk[None], (N_CHIPS,) + chunk.shape)
    mine = lax.all_to_all(spread, CHIPS, 0, 0, tiled=True).reshape(half, D)
    other = lax.ppermute(mine, "c", swap)
    first = jnp.where(core == 0, mine, other)
    second = jnp.where(core == 0, other, mine)
    total = jnp.concatenate([first, second], axis=0).reshape(JL, T, D).transpose(1, 0, 2)
    grad_queries = total * head_weights[:, :, None]
    grad_weights = jnp.sum(total * index_queries.astype(jnp.float32), axis=2)
    return grad_queries, grad_weights, grad_keys, loss_rows


def solution(mesh):
    fine = Mesh(mesh.devices.reshape(8, 2, 4, 2, 2), CTX + ("yh",))
    return jax.shard_map(
        on_device,
        mesh=fine,
        in_specs=(P(None, "yh", None), P(None, "yh"), P(CTX, None), P(None, CTX)),
        out_specs=(P(None, "yh", None), P(None, "yh"), P(CTX, None), P()),
        check_vma=False,
    )
```

time: 1800 us -> 106 us (0.06)
  blocking collectives: 1100 us -> 44.4 us
  waiting for transfers between devices: 612 us -> 18.3 us
  matrix products: 52.7 us -> 0 us
  starting transfers between devices: 0.12 us -> 22.7 us
    psum x2 -> x0, blocking collectives: 823 us -> none  [the longest x1 543 us: on_device(): lax.psum((partial_queries, partial_weights), 'ctx')]
    psum x3 -> x0, waiting for transfers between devices: 612 us -> none  [the longest x1 572 us: on_device(): lax.psum((partial_queries, partial_weights), 'ctx')]
    pmax x1 -> x0, blocking collectives: 276 us -> none  [on_device(): row_max = lax.pmax(local_max, 'ctx')]
    dot_general x24 -> x0, matrix products: 52.7 us -> none  [the longest x4 17.4 us: back_step(): jnp.einsum('ts,tjs->tj', grad_index, jnp.maximum(logits, 0.0), precision=...]
    all_to_all x0 -> x2, blocking collectives: none -> 44.4 us  [the longest x1 24 us: on_device(): stats = merge(lax.all_to_all(spread, CHIPS, 0, 0, tiled=True))]
  transfers between devices with their start and end apart: 3 -> 6, of which waited for: 2 -> 5; matrix products, arithmetic and copies ran while one was open for 0% -> 2% of each run, Pallas kernels for 0% -> 4%
where the time goes in v1:
time: 106 us; the launch traced here: 105 us
  blocking collectives  44.4 us (42%)
  starting transfers between devices  22.7 us (21%)
  waiting for transfers between devices  18.3 us (17%)
  Pallas kernels  11 us (10%)
  local copies, waits for them, and re-layouts  4.66 us (4%)
  other arithmetic  3.63 us (3%)
    all_to_all x1, blocking collectives, on_device(): stats = merge(lax.all_to_all(spread, CHIPS, 0, 0, tiled=True))  24 us
    all_to_all x1, blocking collectives, on_device(): lax.all_to_all(mine.reshape(N_CHIPS, half // N_CHIPS, D), CHIPS, 0, 0, ti...  20.4 us
    all_to_all x1, waiting for transfers between devices, on_device(): mine = lax.all_to_all(spread, CHIPS, 0, 0, tiled=True).reshape(half, D)  7.85 us
    all_to_all x1, starting transfers between devices, on_device(): mine = lax.all_to_all(spread, CHIPS, 0, 0, tiled=True).reshape(half, D)  6.82 us
    ppermute x1, waiting for transfers between devices, on_device(): other_index = lax.ppermute(partial_index, 'yh', swap)  4.89 us
    pallas_call x1, Pallas kernels, query_grads(): pl.pallas_call(query_kernel, grid_spec=grid_spec, out_shape=jax.ShapeDtyp...  4.38 us
    ppermute x1, starting transfers between devices, on_device(): other = lax.ppermute(mine, 'c', swap)  4.24 us
    pallas_call x1, Pallas kernels, key_grads(): pl.pallas_call(key_kernel, grid=(S // tile,), in_specs=[pl.BlockSpec(memo...  3.85 us
  transfers between devices with their start and end apart: 6, of which 5 were waited for; matrix products, arithmetic and copies ran while one was open for 2% of the time, Pallas kernels for 4%

profile of v1, /device:TPU:1, one launch (start us, length us, event | category | flops | bytes accessed | tf_op | source)
XLA Modules:
  0.0 105.4 jit_solution(9048259378302237065)
XLA Ops:
  0.7 1.3 %copy.24 = bf16[32,64,128]{2,1,0:T(8,128)(2,1)S(1)} copy(bf16[32,64,128]{2,0,1:T(8,128)(2,1)} %bitcast.36) | data formatting | bytes 1048576 | tf_op jit(solution)/shard_map/transpose | solution.py:199
  2.1 2.0 %score.1.mine_ref = f32[64,1024]{1,0:T(8,128)S(1)} custom-call(bf16[2048,128]{1,0:T(8,128)(2,1)S(1)} %bitcast.30, f32[64,32]{1,0:T(8,128)S(1)} %copy.25.w_ref, bf16[1024,128]{1,0:T(8,128)(2,1)S(1)} %copy-done), custom_call_target="tpu_custom_call" | custom-call | tf_op jit(solution)/shard_map/score/pallas_call | solution.py:50
  4.0 3.8 %collective-permute-start = (f32[64,1024]{1,0:T(8,128)S(1)}, f32[64,1024]{1,0:T(8,128)S(1)}, u32[]{:S(2)}, u32[]{:S(2)}) collective-permute-start(f32[64,1024]{1,0:T(8,128)S(1)} %score.1.mine_ref), channel_id=1, source_target_pairs={{0,1},{1,0},{2,3},{3,2},{4,5},{5,4},{6,7},{7,6},{8,9},{9,8},{10,11... | collective-permute-start | bytes 786440 | tf_op jit(solution)/shard_map/ppermute | solution.py:201
  7.9 4.9 %collective-permute-done.other_ref = f32[64,1024]{1,0:T(8,128)S(1)} collective-permute-done((f32[64,1024]{1,0:T(8,128)S(1)}, f32[64,1024]{1,0:T(8,128)S(1)}, u32[]{:S(2)}, u32[]{:S(2)}) %collective-permute-start) | collective-permute-done | bytes 262176 | tf_op jit(solution)/shard_map/ppermute | solution.py:201
  12.8 0.8 stats.1
  13.6 2.4 %collective-permute-start.1 = (f32[8,128]{1,0:T(8,128)S(1)}, f32[8,128]{1,0:T(8,128)S(1)}, u32[]{:S(2)}, u32[]{:S(2)}) collective-permute-start(f32[8,128]{1,0:T(8,128)S(1)} %get-tuple-element.7), channel_id=1, source_target_pairs={{0,2},{2,0},{1,3},{3,1},{4,6},{6,4},{5,7},{7,5},{8,10},{10,8},{9,1... | collective-permute-start | bytes 12296 | tf_op jit(solution)/shard_map/ppermute | solution.py:204
  16.1 0.8 collective-permute-done.1
  17.0 24.0 %all_to_all.15 = f32[64,8,128]{2,1,0:T(8,128)S(1)} all-to-all(f32[64,8,128]{2,1,0:T(8,128)S(1)} %broadcast_in_dim.14), channel_id=1, replica_groups=mesh['z'=8,'yl'=2,'x'=4,'c'=2,'yh'=2] {'z','yl','x'}, dimensions={0} | all-to-all | bytes 524288 | tf_op jit(solution)/shard_map/all_to_all | solution.py:207
  41.2 4.4 %query_grads.1 = f32[2048,128]{1,0:T(8,128)S(1)} custom-call(s32[2]{0:T(128)S(1)} %pad_add_fusion.ctx_ref.who_ref, f32[64,1024]{1,0:T(8,128)S(1)} %get-tuple-element.6.index_ref, f32[64,1024]{1,0:T(8,128)S(1)} %copy-done.1, f32[8,128]{1,0:T(8,128)S(1)} %pad_maximum_fusion.3.stats_ref, bf16[2048,128]{1,0:T(8,128)(2,1)S(1)} %bitcast.31, ...), custom_call_target="tpu_custom_call" | custom-call | tf_op jit(solution)/shard_map/query_grads/pallas_call | solution.py:135
  45.6 2.6 %collective-permute-start.2 = (f32[1024,128]{1,0:T(8,128)S(1)}, f32[1024,128]{1,0:T(8,128)S(1)}, u32[]{:S(2)}, u32[]{:S(2)}) collective-permute-start(f32[1024,128]{1,0:T(8,128)S(1)} %slice.58), channel_id=1, source_target_pairs={{0,2},{2,0},{1,3},{3,1},{4,6},{6,4},{5,7},{7,5},{8,10},{10,8},{9,1... | collective-permute-start | bytes 1572872 | tf_op jit(solution)/shard_map/ppermute | solution.py:213
  48.3 1.5 %collective-permute-done.2 = f32[1024,128]{1,0:T(8,128)S(1)} collective-permute-done((f32[1024,128]{1,0:T(8,128)S(1)}, f32[1024,128]{1,0:T(8,128)S(1)}, u32[]{:S(2)}, u32[]{:S(2)}) %collective-permute-start.2) | collective-permute-done | bytes 524320 | tf_op jit(solution)/shard_map/ppermute | solution.py:213
  49.9 20.4 %all_to_all.16 = f32[64,16,128]{2,1,0:T(8,128)S(1)} all-to-all(f32[64,16,128]{2,1,0:T(8,128)S(1)} %bitcast.38), channel_id=1, replica_groups=mesh['z'=8,'yl'=2,'x'=4,'c'=2,'yh'=2] {'z','yl','x'}, dimensions={0} | all-to-all | bytes 1048576 | tf_op jit(solution)/shard_map/all_to_all | solution.py:214
  70.3 0.8 broadcast_in_dim.32
  71.2 6.8 %all-to-all-start.2 = ((f32[64,16,128]{2,1,0:T(8,128)}), f32[64,16,128]{2,1,0:T(8,128)S(1)}, u32[]{:S(2)}, u32[]{:S(2)}) async-start(f32[64,16,128]{2,1,0:T(8,128)} %broadcast_in_dim.32), calls=%async_computation.2 | async-start | bytes 1048576 | tf_op jit(solution)/shard_map/all_to_all | solution.py:222
  78.4 3.8 %key_grads.1 = f32[1024,128]{1,0:T(8,128)S(1)} custom-call(s32[2]{0:T(128)S(1)} %pad_add_fusion.ctx_ref.who_ref, f32[64,1024]{1,0:T(8,128)S(1)} %get-tuple-element.6.index_ref, f32[64,1024]{1,0:T(8,128)S(1)} %copy-done.1, f32[8,128]{1,0:T(8,128)S(1)} %pad_maximum_fusion.3.stats_ref, bf16[2048,128]{1,0:T(8,128)(2,1)S(1)} %bitcast.32, ...), custom_call_target="tpu_custom_call" | custom-call | tf_op jit(solution)/shard_map/key_grads/pallas_call | solution.py:167
  82.3 2.7 %collective-permute-start.4 = (f32[1024,128]{1,0:T(8,128)S(1)}, f32[1024,128]{1,0:T(8,128)S(1)}, u32[]{:S(2)}, u32[]{:S(2)}) collective-permute-start(f32[1024,128]{1,0:T(8,128)S(1)} %key_grads.1), channel_id=1, source_target_pairs={{0,1},{1,0},{2,3},{3,2},{4,5},{5,4},{6,7},{7,6},{8,9},{9,8},{10,11... | collective-permute-start | bytes 1572872 | tf_op jit(solution)/shard_map/ppermute | solution.py:219
  85.0 7.8 %all-to-all-done.2 = f32[64,16,128]{2,1,0:T(8,128)S(1)} async-done(((f32[64,16,128]{2,1,0:T(8,128)}), f32[64,16,128]{2,1,0:T(8,128)S(1)}, u32[]{:S(2)}, u32[]{:S(2)}) %all-to-all-start.2) | async-done | bytes 524320 | tf_op jit(solution)/shard_map/all_to_all | solution.py:222
  92.8 4.2 %collective-permute-start.3 = (f32[1024,128]{1,0:T(8,128)S(1)}, f32[1024,128]{1,0:T(8,128)S(1)}, u32[]{:S(2)}, u32[]{:S(2)}) collective-permute-start(f32[1024,128]{1,0:T(8,128)S(1)} %bitcast.37), channel_id=1, source_target_pairs={{0,2},{2,0},{1,3},{3,1},{4,6},{6,4},{5,7},{7,5},{8,10},{10,8},{9,1... | collective-permute-start | bytes 1572872 | tf_op jit(solution)/shard_map/ppermute | solution.py:223
  97.0 0.5 add_bitcast_fusion
  97.6 3.2 %collective-permute-done.4 = f32[1024,128]{1,0:T(8,128)S(1)} collective-permute-done((f32[1024,128]{1,0:T(8,128)S(1)}, f32[1024,128]{1,0:T(8,128)S(1)}, u32[]{:S(2)}, u32[]{:S(2)}) %collective-permute-start.4) | collective-permute-done | bytes 524320 | tf_op jit(solution)/shard_map/ppermute | solution.py:219
  100.7 0.8 add.28
  102.1 0.7 copy-done.2
  102.8 1.0 multiply_reduce_fusion
  103.8 1.6 %copy.30 = f32[64,32,128]{2,1,0:T(8,128)} copy(f32[64,32,128]{2,0,1:T(8,128)S(1)} %broadcast_multiply_fusion) | data formatting | bytes 2097152
  (29 shorter events, 1.5 us)
Async XLA Ops:
  0.6 1.3 %copy-start.3 = (f32[64,32]{0,1:T(8,128)S(1)}, f32[64,32]{0,1:T(8,128)}, u32[]{:S(2)}) copy-start(f32[64,32]{0,1:T(8,128)} %param.5) | copy-start | bytes 24580
  0.6 1.4 %copy-start = (bf16[1024,128]{1,0:T(8,128)(2,1)S(1)}, bf16[1024,128]{1,0:T(8,128)(2,1)}, u32[]{:S(2)}) copy-start(bf16[1024,128]{1,0:T(8,128)(2,1)} %k_ref.5) | copy-start | bytes 786436
  2.0 10.8 %copy-start.1 = (f32[64,1024]{1,0:T(8,128)S(1)}, f32[64,1024]{1,0:T(8,128)}, u32[]{:S(2)}) copy-start(f32[64,1024]{1,0:T(8,128)} %target_ref.5) | copy-start | bytes 786436
  4.0 8.8 %collective-permute-start = (f32[64,1024]{1,0:T(8,128)S(1)}, f32[64,1024]{1,0:T(8,128)S(1)}, u32[]{:S(2)}, u32[]{:S(2)}) collective-permute-start(f32[64,1024]{1,0:T(8,128)S(1)} %score.1.mine_ref), channel_id=1, source_target_pairs={{0,1},{1,0},{2,3},{3,2},{4,5},{5,4},{6,7},{7,6},{8,9},{9,8},{10,11... | collective-permute-start | bytes 786440 | tf_op jit(solution)/shard_map/ppermute | solution.py:201
  13.6 3.3 %collective-permute-start.1 = (f32[8,128]{1,0:T(8,128)S(1)}, f32[8,128]{1,0:T(8,128)S(1)}, u32[]{:S(2)}, u32[]{:S(2)}) collective-permute-start(f32[8,128]{1,0:T(8,128)S(1)} %get-tuple-element.7), channel_id=1, source_target_pairs={{0,2},{2,0},{1,3},{3,1},{4,6},{6,4},{5,7},{7,5},{8,10},{10,8},{9,1... | collective-permute-start | bytes 12296 | tf_op jit(solution)/shard_map/ppermute | solution.py:204
  45.6 4.2 %collective-permute-start.2 = (f32[1024,128]{1,0:T(8,128)S(1)}, f32[1024,128]{1,0:T(8,128)S(1)}, u32[]{:S(2)}, u32[]{:S(2)}) collective-permute-start(f32[1024,128]{1,0:T(8,128)S(1)} %slice.58), channel_id=1, source_target_pairs={{0,2},{2,0},{1,3},{3,1},{4,6},{6,4},{5,7},{7,5},{8,10},{10,8},{9,1... | collective-permute-start | bytes 1572872 | tf_op jit(solution)/shard_map/ppermute | solution.py:213
  71.2 21.6 %all-to-all-start.2 = ((f32[64,16,128]{2,1,0:T(8,128)}), f32[64,16,128]{2,1,0:T(8,128)S(1)}, u32[]{:S(2)}, u32[]{:S(2)}) async-start(f32[64,16,128]{2,1,0:T(8,128)} %broadcast_in_dim.32), calls=%async_computation.2 | async-start | bytes 1048576 | tf_op jit(solution)/shard_map/all_to_all | solution.py:222
  82.3 18.5 %collective-permute-start.4 = (f32[1024,128]{1,0:T(8,128)S(1)}, f32[1024,128]{1,0:T(8,128)S(1)}, u32[]{:S(2)}, u32[]{:S(2)}) collective-permute-start(f32[1024,128]{1,0:T(8,128)S(1)} %key_grads.1), channel_id=1, source_target_pairs={{0,1},{1,0},{2,3},{3,2},{4,5},{5,4},{6,7},{7,6},{8,9},{9,8},{10,11... | collective-permute-start | bytes 1572872 | tf_op jit(solution)/shard_map/ppermute | solution.py:219
  92.8 8.8 %collective-permute-start.3 = (f32[1024,128]{1,0:T(8,128)S(1)}, f32[1024,128]{1,0:T(8,128)S(1)}, u32[]{:S(2)}, u32[]{:S(2)}) collective-permute-start(f32[1024,128]{1,0:T(8,128)S(1)} %bitcast.37), channel_id=1, source_target_pairs={{0,2},{2,0},{1,3},{3,1},{4,6},{6,4},{5,7},{7,5},{8,10},{10,8},{9,1... | collective-permute-start | bytes 1572872 | tf_op jit(solution)/shard_map/ppermute | solution.py:223
  101.7 1.0 copy-start.2

commit v2 on v0

v2 whole, which is shorter than its diff:
```python
import jax
import jax.numpy as jnp
from jax import lax
from jax.experimental import pallas as pl
from jax.experimental.pallas import tpu as pltpu
from jax.sharding import Mesh, PartitionSpec as P

H = 64
T = 64
JL = 32
D = 128
S = 1024
ROWS = T * JL
HALF = ROWS // 2
POS = 131072 - T
SCALE = (D**-0.5) * (H**-0.5)
CTX = ("zh", "zl", "yl", "x", "c")
NEAR = ("zl", "yl", "x")
PLANE = ("zl", "x")
FAR = "zh"
N_NEAR = 16
N_PLANE = 8
N_X = 4
N_FAR = 4
CHUNK = HALF // N_NEAR
KEY_ROWS = S
VMEM = 48 * 1024 * 1024
SCORE_VMEM = 60 * 1024 * 1024
NT = (((1,), (1,)), ((), ()))
IN_VMEM = pl.BlockSpec(memory_space=pltpu.VMEM)
IN_HBM = pl.BlockSpec(memory_space=pltpu.HBM)
IN_SMEM = pl.BlockSpec(memory_space=pltpu.SMEM)


def params(limit=VMEM):
    return pltpu.CompilerParams(vmem_limit_bytes=limit)


def f32(*shape):
    return jax.ShapeDtypeStruct(shape, jnp.float32)


def whole(shape):
    return pl.BlockSpec(shape, lambda *_: (0,) * len(shape))


def cost(flops, nbytes):
    return pl.CostEstimate(flops=flops, bytes_accessed=nbytes, transcendentals=0)


def columns_of(rows):
    width = rows[0].shape[1]
    filled = jnp.concatenate(rows + [jnp.zeros((128 - len(rows), width), jnp.float32)], axis=0)
    if width < 128:
        filled = jnp.concatenate([filled, jnp.zeros((128, 128 - width), jnp.float32)], axis=1)
    turned = jnp.transpose(filled)
    return [turned[:T, i : i + 1] for i in range(len(rows))]


def score_kernel(q_hbm, w_ref, k_hbm, out_ref, by_head_ref, q_ref, k_ref, q_f32, sems):
    heads, tile, step = JL // 2, 512, 4
    k_copy = pltpu.make_async_copy(k_hbm, k_ref, sems.at[2])
    copies = [
        pltpu.make_async_copy(q_hbm.at[:, h * heads : (h + 1) * heads, :], q_ref.at[h], sems.at[h])
        for h in range(2)
    ]
    copies[0].start()
    k_copy.start()
    copies[1].start()
    w = columns_of([w_ref[j : j + 1, :] * SCALE for j in range(JL)])
    for h in range(2):
        copies[h].wait()
        q_f32[...] = q_ref[h].astype(jnp.float32).reshape(HALF, D)
        for j in range(heads):
            at = h * HALF + j * T
            by_head_ref[at : at + T, :] = q_f32[pl.ds(j, T, stride=heads), :].astype(jnp.bfloat16)
        if h == 0:
            k_copy.wait()
        for s in range(0, S, tile):
            acc = jnp.zeros((T, tile), jnp.float32) if h == 0 else out_ref[:, s : s + tile]
            for j0 in range(h * heads, (h + 1) * heads, step):
                logits = lax.dot_general(
                    by_head_ref[j0 * T : (j0 + step) * T, :],
                    k_ref[s : s + tile, :],
                    NT,
                    preferred_element_type=jnp.float32,
                )
                for j in range(step):
                    acc = acc + w[j0 + j] * jnp.maximum(logits[j * T : (j + 1) * T, :], 0.0)
            out_ref[:, s : s + tile] = acc


def score(q, w, k):
    return pl.pallas_call(
        score_kernel,
        in_specs=[IN_HBM, IN_VMEM, IN_HBM],
        out_specs=[IN_VMEM] * 2,
        out_shape=[f32(T, S), jax.ShapeDtypeStruct((ROWS, D), jnp.bfloat16)],
        scratch_shapes=[
            pltpu.VMEM((2, T, JL // 2, D), jnp.bfloat16),
            pltpu.VMEM((S, D), jnp.bfloat16),
            pltpu.VMEM((HALF, D), jnp.float32),
            pltpu.SemaphoreType.DMA((3,)),
        ],
        compiler_params=params(SCORE_VMEM),
        name="score",
    )(q, w, k)


def valid_mask(ctx):
    key = ctx * S + lax.broadcasted_iota(jnp.int32, (T, S), 1)
    query = POS + lax.broadcasted_iota(jnp.int32, (T, S), 0)
    return key <= query


def target_kernel(who_ref, target_ref, index_ref, w_ref, q_ref, normal_ref, sums_ref, held_ref, weighted_ref):
    held_ref[...] = index_ref[...]
    w = columns_of([w_ref[j : j + 1, :] for j in range(JL)])
    for j in range(JL):
        at = slice(j * T, (j + 1) * T)
        weighted_ref[at, :] = (q_ref[at, :].astype(jnp.float32) * w[j]).astype(jnp.bfloat16)
    valid = valid_mask(who_ref[0])
    target = target_ref[...]
    masked = jnp.where(valid, target, 0.0)
    mass = jnp.sum(masked, axis=1, keepdims=True)
    entropy = jnp.sum(masked * jnp.log(target), axis=1, keepdims=True)
    normal_ref[...] = masked * (1.0 / mass)
    lane = lax.broadcasted_iota(jnp.int32, (T, 128), 1)
    sums_ref[...] = jnp.where(lane == 0, mass, entropy)


def target_sums(who, target, partial_index, w, q):
    return pl.pallas_call(
        target_kernel,
        in_specs=[IN_SMEM] + [IN_VMEM] * 4,
        out_specs=[IN_VMEM] * 4,
        out_shape=[f32(T, S), f32(T, 128), f32(T, S), jax.ShapeDtypeStruct((ROWS, D), jnp.bfloat16)],
        compiler_params=params(),
        name="target",
    )(who, target, partial_index, w, q)


def stats_kernel(who_ref, mine_ref, other_ref, target_ref, sums_ref, index_ref, stats_ref, parts_ref):
    index = mine_ref[...] + other_ref[...]
    index_ref[...] = index
    valid = valid_mask(who_ref[0])
    target = target_ref[...]
    row_max = jnp.max(jnp.where(valid, index, -jnp.inf), axis=1, keepdims=True)
    expo = jnp.where(valid, jnp.exp(index - row_max), 0.0)
    denom = jnp.sum(expo, axis=1, keepdims=True)
    mass, entropy = sums_ref[:, 0:1], sums_ref[:, 1:2]
    cross = mass * jnp.sum(target * index, axis=1, keepdims=True)
    lane = lax.broadcasted_iota(jnp.int32, (T, 128), 1)
    packed = jnp.zeros((T, 128), jnp.float32)
    soft = expo * (1.0 / denom)
    peaks = (jnp.sum(x * x, axis=1, keepdims=True) for x in (soft, target))
    mixed = jnp.where(next(peaks) <= 4.0 * next(peaks), 1.0, 0.0)
    for i, column in enumerate((row_max, denom, mass, entropy, cross, mixed)):
        packed = jnp.where(lane == i, column, packed)
    packed = jnp.concatenate([packed, jnp.zeros((128 - T, 128), jnp.float32)], axis=0)
    stats_ref[...] = jnp.transpose(packed)[:8, :]
    parts_ref[0] = soft.astype(jnp.bfloat16)
    parts_ref[1] = (mixed * soft - target).astype(jnp.bfloat16)


def local_stats(who, mine, other, target, sums):
    return pl.pallas_call(
        stats_kernel,
        in_specs=[IN_SMEM] + [IN_VMEM] * 4,
        out_specs=[IN_VMEM] * 3,
        out_shape=[f32(T, S), f32(8, 128), jax.ShapeDtypeStruct((2, T, S), jnp.bfloat16)],
        compiler_params=params(),
        name="stats",
    )(who, mine, other, target, sums)


def query_kernel(who_ref, parts_ref, stats_ref, q_ref, k_ref, out_ref):
    block = 4 * T
    for r in range(0, HALF, block):
        at = pl.multiple_of(who_ref[0] * HALF + r, block)
        logits = lax.dot_general(
            q_ref[pl.ds(at, block), :], k_ref[...], NT, preferred_element_type=jnp.float32
        )
        positive = logits.astype(jnp.bfloat16) > 0.0
        for i in range(2):
            part = jnp.concatenate([parts_ref[i]] * (block // T), axis=0)
            picked = jnp.where(positive, part, jnp.zeros_like(part))
            at = slice(i * HALF + r, i * HALF + r + block)
            out_ref[at, :] = jnp.dot(picked, k_ref[...], preferred_element_type=jnp.float32)
    out_ref[ROWS:, :] = stats_ref[...]


def query_sums(half, parts, stats, q, k, name):
    return pl.pallas_call(
        query_kernel,
        in_specs=[IN_SMEM] + [IN_VMEM] * 4,
        out_specs=IN_VMEM,
        out_shape=f32(ROWS + 8, D),
        compiler_params=params(),
        cost_estimate=cost(6 * HALF * S * D, 4 << 20),
        name=name,
    )(half, parts, stats, q, k)


def merge(stats):
    row_max = stats[0][0:1]
    for s in stats[1:]:
        row_max = jnp.maximum(row_max, s[0:1])
    denom, rest = 0.0, 0.0
    for s in stats:
        denom = denom + s[1:2] * jnp.exp(s[0:1] - row_max)
        rest = rest + s[2:8]
    return jnp.concatenate([row_max, denom, rest], axis=0)


def shares(part, total):
    return part[1:2] * jnp.exp(part[0:1] - total[0:1]) / total[1:2], part[2:3] / total[2:3]


def pack_kernel(keep_ref, recv_ref, out_ref):
    mine, other = keep_ref[ROWS:, :], recv_ref[ROWS:, :]
    chip = merge([mine, other])
    rows = [*shares(mine, chip), mine[5:6], *shares(other, chip), other[5:6]]
    soft_a, target_a, mixed_a, soft_b, target_b, mixed_b = columns_of(rows)
    gap_a, gap_b = soft_a - mixed_a * target_a, soft_b - mixed_b * target_b
    for i in range(N_NEAR):
        at, too = slice(i * CHUNK, (i + 1) * CHUNK), slice(HALF + i * CHUNK, HALF + (i + 1) * CHUNK)
        a, b = keep_ref[at, :], recv_ref[at, :]
        out_ref[i, :CHUNK, :] = soft_a * a + soft_b * b
        gap = gap_a * a + gap_b * b + target_a * keep_ref[too, :] + target_b * recv_ref[too, :]
        out_ref[i, CHUNK : 2 * CHUNK, :] = gap
        out_ref[i, 2 * CHUNK :, :] = chip


def pack(keep, recv):
    return pl.pallas_call(
        pack_kernel,
        in_specs=[IN_VMEM] * 2,
        out_specs=IN_VMEM,
        out_shape=f32(N_NEAR, 2 * CHUNK + 8, 128),
        compiler_params=params(),
        name="pack",
    )(keep, recv)


def combine_parts(refs):
    parts = [ref[2 * CHUNK :, :] for ref in refs]
    total = merge(parts)
    columns = columns_of([row for part in parts for row in shares(part, total)])
    soft_sum, gap_sum = 0.0, 0.0
    for i, ref in enumerate(refs):
        soft, target = columns[2 * i], columns[2 * i + 1]
        a = ref[:CHUNK, :]
        soft_sum = soft_sum + soft * a
        gap_sum = gap_sum + (soft - target) * a + target * ref[CHUNK : 2 * CHUNK, :]
    return total, soft_sum, gap_sum


def near_kernel(in_ref, out_ref):
    total, soft_sum, gap_sum = combine_parts([in_ref.at[i] for i in range(N_NEAR)])
    out_ref[:CHUNK, :] = soft_sum
    out_ref[CHUNK : 2 * CHUNK, :] = gap_sum
    out_ref[2 * CHUNK :, :] = total


def combine_near(received):
    return pl.pallas_call(
        near_kernel,
        in_specs=[IN_VMEM],
        out_specs=IN_VMEM,
        out_shape=f32(2 * CHUNK + 8, D),
        compiler_params=params(),
        name="combine_near",
    )(received)


def far_kernel(who_ref, a_ref, b_ref, c_ref, d_ref, w_ref, q_ref, out_ref, stats_ref, loss_ref):
    total, _, gap_sum = combine_parts([a_ref, b_ref, c_ref, d_ref])
    row_max, denom, mass, entropy, cross = (total[i : i + 1] for i in range(5))
    stats_ref[...] = total
    loss = entropy / mass - jnp.log(mass) - cross / mass + row_max + jnp.log(denom)
    loss_ref[...] = jnp.broadcast_to(loss, loss_ref.shape)
    gap_sum = gap_sum * (SCALE / T)
    head = who_ref[2]
    scaled = gap_sum * columns_of([w_ref[pl.ds(head, 1), :]])[0]
    q = q_ref[pl.ds(pl.multiple_of(head * T, T), T), :].astype(jnp.float32)
    grads = jnp.broadcast_to(jnp.sum(gap_sum * q, axis=1, keepdims=True), (T, 128))
    grads = jnp.transpose(jnp.concatenate([grads, grads], axis=0))[:8]
    out_ref[:CHUNK, :] = scaled
    out_ref[CHUNK:, :] = grads


def combine_far(who, own, far, w, q):
    return pl.pallas_call(
        far_kernel,
        in_specs=[IN_SMEM] + [IN_VMEM] * 6,
        out_specs=[IN_VMEM] * 3,
        out_shape=[f32(CHUNK + 8, D), f32(8, 128), f32(8, 128)],
        compiler_params=params(),
        name="combine_far",
    )(who, own, *far, w, q)


def spread_kernel(who_ref, mine_ref, other_ref, out_ref):
    size = CHUNK + 8
    first = who_ref[3] == 0
    for p in range(N_PLANE):
        out_ref[p, :size, :] = jnp.where(first, mine_ref[...], other_ref[...])
        out_ref[p, size:, :] = jnp.where(first, other_ref[...], mine_ref[...])


def spread(who, mine, other):
    return pl.pallas_call(
        spread_kernel,
        in_specs=[IN_SMEM] + [IN_VMEM] * 2,
        out_specs=IN_VMEM,
        out_shape=f32(N_PLANE, 2 * (CHUNK + 8), D),
        compiler_params=params(),
        name="spread",
    )(who, mine, other)


def chunks_of():
    for p in range(N_PLANE):
        for y in range(2):
            yield (p // N_X * 2 + y) * N_X + p % N_X, p, y * (CHUNK + 8)


def place_half(half, at, out_hbm, rows_ref, sem):
    for j, p, r in chunks_of():
        ref, i = at(p)
        rows_ref[pl.ds(j, T, stride=N_NEAR), :] = ref[i, r : r + CHUNK, :]
    to = out_hbm.at[:, pl.ds(pl.multiple_of(half * N_NEAR, N_NEAR), N_NEAR), :]
    copy = pltpu.make_async_copy(rows_ref.reshape(T, N_NEAR, D), to, sem)
    copy.start()
    return copy


def first_kernel(who_ref, mine_ref, out_hbm, rows_ref, sem):
    place_half(who_ref[1], lambda p: (mine_ref, p), out_hbm, rows_ref, sem).wait()


def last_kernel(who_ref, mine_ref, lower_ref, upper_ref, begun_hbm, out_hbm, weights_ref, rows_ref, sem):
    def mine_at(p):
        return mine_ref, p

    def other_at(p):
        return (lower_ref, p) if p < N_PLANE // 2 else (upper_ref, p - N_PLANE // 2)

    copy = place_half(1 - who_ref[1], other_at, out_hbm, rows_ref, sem)

    def emit(first, second):
        for half, at in enumerate((first, second)):
            for j, p, r in chunks_of():
                ref, i = at(p)
                row = half * N_NEAR + j
                weights_ref[row : row + 1, :] = ref[i, r + CHUNK : r + CHUNK + 1, :T]

    pl.when(who_ref[1] == 0)(lambda: emit(mine_at, other_at))
    pl.when(who_ref[1] == 1)(lambda: emit(other_at, mine_at))
    copy.wait()


HALF_SCRATCH = [pltpu.VMEM((HALF, D), jnp.float32), pltpu.SemaphoreType.DMA(())]


def place_mine(who, mine):
    return pl.pallas_call(
        first_kernel,
        in_specs=[IN_SMEM, IN_VMEM],
        out_specs=IN_HBM,
        out_shape=f32(T, JL, D),
        scratch_shapes=HALF_SCRATCH,
        compiler_params=params(),
        name="place_mine",
    )(who, mine)


def place_other(who, mine, other, begun):
    return pl.pallas_call(
        last_kernel,
        in_specs=[IN_SMEM, IN_VMEM, IN_VMEM, IN_VMEM, IN_HBM],
        out_specs=[IN_HBM, IN_VMEM],
        out_shape=[f32(T, JL, D), f32(JL, T)],
        scratch_shapes=HALF_SCRATCH,
        input_output_aliases={4: 0},
        compiler_params=params(),
        name="place_other",
    )(who, mine, *other, begun)


def key_kernel(who_ref, index_ref, target_ref, stats_ref, q_ref, weighted_ref, k_ref, out_ref):
    row_max, denom, mass = columns_of([stats_ref[i : i + 1, :] for i in range(3)])
    gap = jnp.exp(index_ref[...] - row_max) * (1.0 / denom) - target_ref[...] * (1.0 / mass)
    gap = jnp.where(valid_mask(who_ref[0]), gap, 0.0) * (SCALE / T)
    tile, span = 256, 1024
    for s in range(0, S, tile):
        g = gap[:, s : s + tile]
        g = jnp.transpose(jnp.concatenate([g, g], axis=0))
        acc = jnp.zeros((tile, D), jnp.float32)
        for r in range(0, ROWS, span):
            logits = lax.dot_general(
                k_ref[s : s + tile, :], q_ref[r : r + span, :], NT, preferred_element_type=jnp.float32
            )
            picked = jnp.where(logits > 0.0, jnp.concatenate([g] * (span // 128), axis=1), 0.0)
            acc = acc + jnp.dot(
                picked.astype(jnp.bfloat16), weighted_ref[r : r + span, :], preferred_element_type=jnp.float32
            )
        out_ref[s : s + tile, :] = acc


def key_grads(who, index, target, stats, q, weighted, k):
    return pl.pallas_call(
        key_kernel,
        in_specs=[IN_SMEM] + [IN_VMEM] * 6,
        out_specs=IN_VMEM,
        out_shape=f32(KEY_ROWS, D),
        compiler_params=params(),
        cost_estimate=cost(4 * ROWS * S * D, 4 << 20),
        name="key_grads",
    )(who, index, target, stats, q, weighted, k)


def on_device(index_queries, head_weights, index_keys, main_target):
    swap = [(0, 1), (1, 0)]
    core = lax.axis_index("c")
    head = core * N_NEAR + lax.axis_index(NEAR)
    who = jnp.stack([lax.axis_index(CTX), core, head, lax.axis_index("yl")]).astype(jnp.int32)
    w = head_weights.T
    partial_index, q = score(index_queries, w, index_keys)
    other_index = lax.ppermute(partial_index, "yh", swap)
    target, target_sum, held_index, weighted = target_sums(who, main_target, partial_index, w, q)
    index, stats, parts = local_stats(who, held_index, other_index, target, target_sum)

    send = query_sums(1 - who[1:2], parts, stats, q, index_keys, "query_sums_send")
    recv = lax.ppermute(send, "c", swap)
    keep = query_sums(who[1:2], parts, stats, q, index_keys, "query_sums_keep")
    near = lax.all_to_all(pack(keep, recv), NEAR, 0, 0, tiled=True)
    own = combine_near(near)
    far = [lax.ppermute(own, FAR, [(i, i ^ d) for i in range(N_FAR)]) for d in range(1, N_FAR)]
    chunk, total_stats, loss = combine_far(who, own, far, w, q)

    other_chunk = lax.ppermute(chunk, "yl", swap)
    key_part = key_grads(who, index, main_target, total_stats, q, weighted, index_keys)
    other_key_part = lax.ppermute(key_part, "yh", swap)
    other_chunk, _ = lax.optimization_barrier((other_chunk, key_part))
    mine = lax.all_to_all(spread(who, chunk, other_chunk), PLANE, 0, 0, tiled=True)
    half = N_PLANE // 2
    other = [lax.ppermute(x, "c", swap) for x in (mine[:half], mine[half:])]
    grad_queries, grad_weights = place_other(who, mine, other, place_mine(who, mine))
    grad_weights, key_part = lax.optimization_barrier((grad_weights, key_part))
    return grad_queries, grad_weights.T, key_part[:S] + other_key_part[:S], loss[0, :T]


def solution(mesh):
    fine = Mesh(mesh.devices.reshape(N_FAR, 2, 2, 4, 2, 2), CTX + ("yh",))
    return jax.shard_map(
        on_device,
        mesh=fine,
        in_specs=(P(None, "yh", None), P(None, "yh"), P(CTX, None), P(None, CTX)),
        out_specs=(P(None, "yh", None), P(None, "yh"), P(CTX, None), P()),
        check_vma=False,
    )
```

time: 1800 us -> 86 us (0.05)
  blocking collectives: 1100 us -> 22.8 us
  waiting for transfers between devices: 612 us -> 12.8 us
  matrix products: 52.7 us -> 0 us
  starting transfers between devices: 0.12 us -> 24.8 us
  Pallas kernels: 0 us -> 20.1 us
    psum x2 -> x0, blocking collectives: 823 us -> none  [the longest x1 543 us: on_device(): lax.psum((partial_queries, partial_weights), 'ctx')]
    psum x3 -> x0, waiting for transfers between devices: 612 us -> none  [the longest x1 572 us: on_device(): lax.psum((partial_queries, partial_weights), 'ctx')]
    pmax x1 -> x0, blocking collectives: 276 us -> none  [on_device(): row_max = lax.pmax(local_max, 'ctx')]
    dot_general x24 -> x0, matrix products: 52.7 us -> none  [the longest x4 17.4 us: back_step(): jnp.einsum('ts,tjs->tj', grad_index, jnp.maximum(logits, 0.0), precision=...]
    all_to_all x0 -> x1, blocking collectives: none -> 22.8 us  [on_device(): near = lax.all_to_all(pack(keep, recv), NEAR, 0, 0, tiled=True)]
    ppermute x0 -> x9, starting transfers between devices: none -> 21.3 us  [the longest x3 7.39 us: on_device(): lax.ppermute(own, FAR, [(i, i ^ d) for i in range(N_FAR)])]
    pallas_call x0 -> x12, Pallas kernels: none -> 20.1 us  [the longest x1 4.13 us: score(): pl.pallas_call(score_kernel, in_specs=[IN_HBM, IN_VMEM, IN_HBM], out_spec...]
  transfers between devices with their start and end apart: 3 -> 10, of which waited for: 2 -> 6; matrix products, arithmetic and copies ran while one was open for 0% -> 1% of each run, Pallas kernels for 0% -> 11%
where the time goes in v2:
time: 86 us; the launch traced here: 85.7 us
  starting transfers between devices  24.8 us (29%)
  blocking collectives  22.8 us (27%)
  Pallas kernels  20.1 us (23%)
  waiting for transfers between devices  12.8 us (15%)
  local copies, waits for them, and re-layouts  3.28 us (4%)
  other arithmetic  0.94 us (1%)
    all_to_all x1, blocking collectives, on_device(): near = lax.all_to_all(pack(keep, recv), NEAR, 0, 0, tiled=True)  22.8 us
    ppermute x3, starting transfers between devices, on_device(): lax.ppermute(own, FAR, [(i, i ^ d) for i in range(N_FAR)])  7.39 us
    ppermute x3, waiting for transfers between devices, on_device(): lax.ppermute(own, FAR, [(i, i ^ d) for i in range(N_FAR)])  6.32 us
    ppermute x2, starting transfers between devices, on_device(): other = [lax.ppermute(x, 'c', swap) for x in (mine[:half], mine[half:])]  4.74 us
    all_to_all x1, waiting for transfers between devices, on_device(): lax.all_to_all(spread(who, chunk, other_chunk), PLANE, 0, 0, tiled=True)  4.62 us
    pallas_call x1, Pallas kernels, score(): pl.pallas_call(score_kernel, in_specs=[IN_HBM, IN_VMEM, IN_HBM], out_spec...  4.13 us
    ppermute x1, starting transfers between devices, on_device(): other_index = lax.ppermute(partial_index, 'yh', swap)  3.83 us
    pallas_call x2, Pallas kernels, query_sums(): pl.pallas_call(query_kernel, in_specs=[IN_SMEM] + [IN_VMEM] * 4, out_spec...  3.62 us
  transfers between devices with their start and end apart: 10, of which 6 were waited for; matrix products, arithmetic and copies ran while one was open for 1% of the time, Pallas kernels for 11%

profile of v2, /device:TPU:1, one launch (start us, length us, event | category | flops | bytes accessed | tf_op | source)
XLA Modules:
  0.0 85.7 jit_solution(1252944785459644989)
XLA Ops:
  0.7 4.1 %score.1 = (f32[64,1024]{1,0:T(8,128)}, bf16[2048,128]{1,0:T(8,128)(2,1)}) custom-call(bf16[64,32,128]{2,1,0:T(8,128)(2,1)} %q_hbm.1, f32[32,64]{1,0:T(8,128)} %bitcast.8, bf16[1024,128]{1,0:T(8,128)(2,1)} %k_ref.5), custom_call_target="tpu_custom_call" | custom-call | tf_op jit(solution)/shard_map/score/pallas_call | solution.py:94
  4.8 3.8 %collective-permute-start = (f32[64,1024]{1,0:T(8,128)}, f32[64,1024]{1,0:T(8,128)S(1)}, u32[]{:S(2)}, u32[]{:S(2)}) collective-permute-start(f32[64,1024]{1,0:T(8,128)} %get-tuple-element.21.index_ref), channel_id=1, source_target_pairs={{0,1},{1,0},{2,3},{3,2},{4,5},{5,4},{6,7},{7,6},{8,9},{9,8},{10,11... | collective-permute-start | bytes 786440 | tf_op jit(solution)/shard_map/ppermute | solution.py:431
  8.7 1.0 %copy-done = bf16[2048,128]{1,0:T(8,128)(2,1)S(1)} copy-done((bf16[2048,128]{1,0:T(8,128)(2,1)S(1)}, bf16[2048,128]{1,0:T(8,128)(2,1)}, u32[]{:S(2)}) %copy-start) | copy-done | bytes 524312
  9.7 0.9 %copy-done.4 = f32[64,1024]{1,0:T(8,128)S(1)} copy-done((f32[64,1024]{1,0:T(8,128)S(1)}, f32[64,1024]{1,0:T(8,128)}, u32[]{:S(2)}) %copy-start.4) | copy-done | bytes 262168
  11.4 1.1 %target.1 = (f32[64,1024]{1,0:T(8,128)S(1)}, f32[64,128]{1,0:T(8,128)S(1)}, f32[64,1024]{1,0:T(8,128)S(1)}, bf16[2048,128]{1,0:T(8,128)(2,1)S(1)}) custom-call(s32[4]{0:T(128)S(1)} %pad_add_fusion.who_ref, f32[64,1024]{1,0:T(8,128)S(1)} %copy-done.3, f32[64,1024]{1,0:T(8,128)S(1)} %copy-done.4, f32[32,64]{1,0:T(8,128)S(1)} %bitcast.9, ...), custom_call_target="tpu_custom_call" | custom-call | tf_op jit(solution)/shard_map/target/pallas_call | solution.py:133
  12.5 1.4 %collective-permute-done.other_ref = f32[64,1024]{1,0:T(8,128)S(1)} collective-permute-done((f32[64,1024]{1,0:T(8,128)}, f32[64,1024]{1,0:T(8,128)S(1)}, u32[]{:S(2)}, u32[]{:S(2)}) %collective-permute-start) | collective-permute-done | bytes 262176 | tf_op jit(solution)/shard_map/ppermute | solution.py:431
  13.9 1.0 %stats.1 = (f32[64,1024]{1,0:T(8,128)S(1)}, f32[8,128]{1,0:T(8,128)S(1)}, bf16[2,64,1024]{2,1,0:T(8,128)(2,1)S(1)}) custom-call(s32[4]{0:T(128)S(1)} %pad_add_fusion.who_ref, f32[64,1024]{1,0:T(8,128)S(1)} %get-tuple-element.23.mine_ref, f32[64,1024]{1,0:T(8,128)S(1)} %collective-permute-done.other_ref, f32[64,1024]{1,0:T(8,128)S(1)} %get-tuple-element.24.target_ref, ...), custom_call_target="tpu_custom_call" | custom-call | tf_op jit(solution)/shard_map/stats/pallas_call | solution.py:167
  14.9 1.8 %query_sums_send.1 = f32[2056,128]{1,0:T(8,128)S(1)} custom-call(s32[1]{0:T(128)S(6)} %sub.3.who_ref, bf16[2,64,1024]{2,1,0:T(8,128)(2,1)S(1)} %get-tuple-element.26.parts_ref, f32[8,128]{1,0:T(8,128)S(1)} %get-tuple-element.27.stats_ref, bf16[2048,128]{1,0:T(8,128)(2,1)S(1)} %copy-done.1, bf16[1024,128]{1,0:T(8,128)(2,1)S(1)} %copy-done.2), custom_call_target="tpu_custom_call" | custom-call | flops 805306368 | bytes 4194304 | tf_op jit(solution)/shard_map/query_sums_send/pallas_call | solution.py:194
  16.7 2.4 %collective-permute-start.1 = (f32[2056,128]{1,0:T(8,128)S(1)}, f32[2056,128]{1,0:T(8,128)S(1)}, u32[]{:S(2)}, u32[]{:S(2)}) collective-permute-start(f32[2056,128]{1,0:T(8,128)S(1)} %query_sums_send.1), channel_id=1, source_target_pairs={{0,2},{2,0},{1,3},{3,1},{4,6},{6,4},{5,7},{7,5},{8,10},{10,8},{9,1... | collective-permute-start | bytes 3158024 | tf_op jit(solution)/shard_map/ppermute | solution.py:436
  19.1 1.8 %query_sums_keep.1.keep_ref = f32[2056,128]{1,0:T(8,128)S(1)} custom-call(s32[1]{0:T(128)} %bitcast.1.who_ref, bf16[2,64,1024]{2,1,0:T(8,128)(2,1)S(1)} %get-tuple-element.26.parts_ref, f32[8,128]{1,0:T(8,128)S(1)} %get-tuple-element.27.stats_ref, bf16[2048,128]{1,0:T(8,128)(2,1)S(1)} %copy-done.1, bf16[1024,128]{1,0:T(8,128)(2,1)S(1)} %copy-done.2), custom_call_target="tpu_custom_call" | custom-call | flops 805306368 | bytes 4194304 | tf_op jit(solution)/shard_map/query_sums_keep/pallas_call | solution.py:194
  21.9 22.8 %all_to_all.10.in_ref = f32[16,136,128]{2,1,0:T(8,128)S(1)} all-to-all(f32[16,136,128]{2,1,0:T(8,128)S(1)} %pack.1), channel_id=1, replica_groups=mesh['zh'=4,'zl'=2,'yl'=2,'x'=4,'c'=2,'yh'=2] {'zl','yl','x'}, dimensions={0} | all-to-all | bytes 2228224 | tf_op jit(solution)/shard_map/all_to_all | solution.py:438
  45.4 5.2 %collective-permute-start.4 = (f32[136,128]{1,0:T(8,128)S(1)}, f32[136,128]{1,0:T(8,128)S(1)}, u32[]{:S(2)}, u32[]{:S(2)}) collective-permute-start(f32[136,128]{1,0:T(8,128)S(1)} %combine_near.1.a_ref), channel_id=1, source_target_pairs={{0,192},{64,128},{128,64},{192,0},{1,193},{65,129},{129,65},{193,1... | collective-permute-start | bytes 208904 | tf_op jit(solution)/shard_map/ppermute | solution.py:440
  50.7 1.2 %collective-permute-start.3 = (f32[136,128]{1,0:T(8,128)S(1)}, f32[136,128]{1,0:T(8,128)S(1)}, u32[]{:S(2)}, u32[]{:S(2)}) collective-permute-start(f32[136,128]{1,0:T(8,128)S(1)} %combine_near.1.a_ref), channel_id=1, source_target_pairs={{0,128},{64,192},{128,0},{192,64},{1,129},{65,193},{129,1},{193,65... | collective-permute-start | bytes 208904 | tf_op jit(solution)/shard_map/ppermute | solution.py:440
  51.8 1.0 %collective-permute-start.2 = (f32[136,128]{1,0:T(8,128)S(1)}, f32[136,128]{1,0:T(8,128)S(1)}, u32[]{:S(2)}, u32[]{:S(2)}) collective-permute-start(f32[136,128]{1,0:T(8,128)S(1)} %combine_near.1.a_ref), channel_id=1, source_target_pairs={{0,64},{64,0},{128,192},{192,128},{1,65},{65,1},{129,193},{193,129... | collective-permute-start | bytes 208904 | tf_op jit(solution)/shard_map/ppermute | solution.py:440
  53.4 5.7 %collective-permute-done.3.c_ref = f32[136,128]{1,0:T(8,128)S(1)} collective-permute-done((f32[136,128]{1,0:T(8,128)S(1)}, f32[136,128]{1,0:T(8,128)S(1)}, u32[]{:S(2)}, u32[]{:S(2)}) %collective-permute-start.3) | collective-permute-done | bytes 69664 | tf_op jit(solution)/shard_map/ppermute | solution.py:440
  59.2 1.0 %combine_far.1 = (f32[72,128]{1,0:T(8,128)S(1)}, f32[8,128]{1,0:T(8,128)S(1)}, f32[8,128]{1,0:T(8,128)S(1)}) custom-call(s32[4]{0:T(128)S(1)} %pad_add_fusion.who_ref, f32[136,128]{1,0:T(8,128)S(1)} %combine_near.1.a_ref, f32[136,128]{1,0:T(8,128)S(1)} %collective-permute-done.2.b_ref, f32[136,128]{1,0:T(8,128)S(1)} %collective-permute-done.3.c_ref, ...), custom_call_target="tpu_custom_call" | custom-call | tf_op jit(solution)/shard_map/combine_far/pallas_call | solution.py:294
  60.5 2.9 %key_grads.1 = f32[1024,128]{1,0:T(8,128)S(1)} custom-call(s32[4]{0:T(128)S(1)} %pad_add_fusion.who_ref, f32[64,1024]{1,0:T(8,128)S(1)} %get-tuple-element.29.index_ref, f32[64,1024]{1,0:T(8,128)S(1)} %copy-done.3, f32[8,128]{1,0:T(8,128)S(1)} %get-tuple-element.30.stats_ref, bf16[2048,128]{1,0:T(8,128)(2,1)S(1)} %copy-done.1, ...), custom_call_target="tpu_custom_call" | custom-call | flops 1073741824 | bytes 4194304 | tf_op jit(solution)/shard_map/key_grads/pallas_call | solution.py:413
  63.4 1.4 %spread.1 = f32[8,144,128]{2,1,0:T(8,128)} custom-call(s32[4]{0:T(128)S(1)} %pad_add_fusion.who_ref, f32[72,128]{1,0:T(8,128)S(1)} %get-tuple-element.28.mine_ref, f32[72,128]{1,0:T(8,128)S(1)} %collective-permute-done.5.other_ref), custom_call_target="tpu_custom_call" | custom-call | tf_op jit(solution)/shard_map/spread/pallas_call | solution.py:313
  64.8 3.5 %all-to-all-start.1 = ((f32[8,144,128]{2,1,0:T(8,128)}), f32[8,144,128]{2,1,0:T(8,128)S(1)}, u32[]{:S(2)}, u32[]{:S(2)}) async-start(f32[8,144,128]{2,1,0:T(8,128)} %spread.1), calls=%async_computation.1 | async-start | bytes 1179648 | tf_op jit(solution)/shard_map/all_to_all | solution.py:447
  68.4 2.7 %collective-permute-start.8 = (f32[1024,128]{1,0:T(8,128)S(1)}, f32[1024,128]{1,0:T(8,128)S(1)}, u32[]{:S(2)}, u32[]{:S(2)}) collective-permute-start(f32[1024,128]{1,0:T(8,128)S(1)} %key_grads.1), channel_id=1, source_target_pairs={{0,1},{1,0},{2,3},{3,2},{4,5},{5,4},{6,7},{7,6},{8,9},{9,8},{10,11... | collective-permute-start | bytes 1572872 | tf_op jit(solution)/shard_map/ppermute | solution.py:445
  71.1 4.6 %all-to-all-done.1.mine_ref = f32[8,144,128]{2,1,0:T(8,128)S(1)} async-done(((f32[8,144,128]{2,1,0:T(8,128)}), f32[8,144,128]{2,1,0:T(8,128)S(1)}, u32[]{:S(2)}, u32[]{:S(2)}) %all-to-all-start.1) | async-done | bytes 589856 | tf_op jit(solution)/shard_map/all_to_all | solution.py:447
  75.7 4.6 %collective-permute-start.7 = (f32[4,144,128]{2,1,0:T(8,128)S(1)}, f32[4,144,128]{2,1,0:T(8,128)S(1)}, u32[]{:S(2)}, u32[]{:S(2)}) collective-permute-start(f32[4,144,128]{2,1,0:T(8,128)S(1)} %get-tuple-element.38), channel_id=1, source_target_pairs={{0,2},{2,0},{1,3},{3,1},{4,6},{6,4},{5,7},{7,5},{8,10},{10,8},{9,1... | collective-permute-start | bytes 884744 | tf_op jit(solution)/shard_map/ppermute | solution.py:449
  81.0 1.6 %place_mine.1.begun_hbm = f32[64,32,128]{2,1,0:T(8,128)} custom-call(s32[4]{0:T(128)S(1)} %pad_add_fusion.who_ref, f32[8,144,128]{2,1,0:T(8,128)S(1)} %all-to-all-done.1.mine_ref), custom_call_target="tpu_custom_call" | custom-call | tf_op jit(solution)/shard_map/place_mine/pallas_call | solution.py:368
  82.6 2.2 %place_other.1 = (f32[64,32,128]{2,1,0:T(8,128)}, f32[32,64]{1,0:T(8,128)}) custom-call(s32[4]{0:T(128)S(1)} %pad_add_fusion.who_ref, f32[8,144,128]{2,1,0:T(8,128)S(1)} %all-to-all-done.1.mine_ref, f32[4,144,128]{2,1,0:T(8,128)S(1)} %collective-permute-done.6.lower_ref, ...), custom_call_target="tpu_custom_call", output_to_operand_aliasing={{0}: (4, {})} | custom-call | tf_op jit(solution)/shard_map/place_other/pallas_call | solution.py:380
  (27 shorter events, 4.9 us)
Async XLA Ops:
  0.6 8.1 %copy-start.3 = (f32[64,1024]{1,0:T(8,128)S(1)}, f32[64,1024]{1,0:T(8,128)}, u32[]{:S(2)}) copy-start(f32[64,1024]{1,0:T(8,128)} %target_ref.3) | copy-start | bytes 786436
  0.6 14.2 %copy-start.2 = (bf16[1024,128]{1,0:T(8,128)(2,1)S(1)}, bf16[1024,128]{1,0:T(8,128)(2,1)}, u32[]{:S(2)}) copy-start(bf16[1024,128]{1,0:T(8,128)(2,1)} %k_ref.5) | copy-start | bytes 786436
  4.8 9.1 %collective-permute-start = (f32[64,1024]{1,0:T(8,128)}, f32[64,1024]{1,0:T(8,128)S(1)}, u32[]{:S(2)}, u32[]{:S(2)}) collective-permute-start(f32[64,1024]{1,0:T(8,128)} %get-tuple-element.21.index_ref), channel_id=1, source_target_pairs={{0,1},{1,0},{2,3},{3,2},{4,5},{5,4},{6,7},{7,6},{8,9},{9,8},{10,11... | collective-permute-start | bytes 786440 | tf_op jit(solution)/shard_map/ppermute | solution.py:431
  8.7 1.0 %copy-start = (bf16[2048,128]{1,0:T(8,128)(2,1)S(1)}, bf16[2048,128]{1,0:T(8,128)(2,1)}, u32[]{:S(2)}) copy-start(bf16[2048,128]{1,0:T(8,128)(2,1)} %get-tuple-element.22.q_ref) | copy-start | bytes 1572868
  9.7 0.9 %copy-start.4 = (f32[64,1024]{1,0:T(8,128)S(1)}, f32[64,1024]{1,0:T(8,128)}, u32[]{:S(2)}) copy-start(f32[64,1024]{1,0:T(8,128)} %get-tuple-element.21.index_ref) | copy-start | bytes 786436
  10.7 0.7 copy-start.5
  11.4 3.5 %copy-start.1 = (bf16[2048,128]{1,0:T(8,128)(2,1)S(1)}, bf16[2048,128]{1,0:T(8,128)(2,1)}, u32[]{:S(2)}) copy-start(bf16[2048,128]{1,0:T(8,128)(2,1)} %get-tuple-element.22.q_ref) | copy-start | bytes 1572868
  16.7 4.7 %collective-permute-start.1 = (f32[2056,128]{1,0:T(8,128)S(1)}, f32[2056,128]{1,0:T(8,128)S(1)}, u32[]{:S(2)}, u32[]{:S(2)}) collective-permute-start(f32[2056,128]{1,0:T(8,128)S(1)} %query_sums_send.1), channel_id=1, source_target_pairs={{0,2},{2,0},{1,3},{3,1},{4,6},{6,4},{5,7},{7,5},{8,10},{10,8},{9,1... | collective-permute-start | bytes 3158024 | tf_op jit(solution)/shard_map/ppermute | solution.py:436
  44.7 14.4 %copy-start.6 = (f32[64,32]{0,1:T(8,128)S(1)}, f32[64,32]{0,1:T(8,128)}, u32[]{:S(2)}) copy-start(f32[64,32]{0,1:T(8,128)} %param.5) | copy-start | bytes 24580
  45.4 8.0 %collective-permute-start.4 = (f32[136,128]{1,0:T(8,128)S(1)}, f32[136,128]{1,0:T(8,128)S(1)}, u32[]{:S(2)}, u32[]{:S(2)}) collective-permute-start(f32[136,128]{1,0:T(8,128)S(1)} %combine_near.1.a_ref), channel_id=1, source_target_pairs={{0,192},{64,128},{128,64},{192,0},{1,193},{65,129},{129,65},{193,1... | collective-permute-start | bytes 208904 | tf_op jit(solution)/shard_map/ppermute | solution.py:440
  50.7 8.4 %collective-permute-start.3 = (f32[136,128]{1,0:T(8,128)S(1)}, f32[136,128]{1,0:T(8,128)S(1)}, u32[]{:S(2)}, u32[]{:S(2)}) collective-permute-start(f32[136,128]{1,0:T(8,128)S(1)} %combine_near.1.a_ref), channel_id=1, source_target_pairs={{0,128},{64,192},{128,0},{192,64},{1,129},{65,193},{129,1},{193,65... | collective-permute-start | bytes 208904 | tf_op jit(solution)/shard_map/ppermute | solution.py:440
  51.8 7.3 %collective-permute-start.2 = (f32[136,128]{1,0:T(8,128)S(1)}, f32[136,128]{1,0:T(8,128)S(1)}, u32[]{:S(2)}, u32[]{:S(2)}) collective-permute-start(f32[136,128]{1,0:T(8,128)S(1)} %combine_near.1.a_ref), channel_id=1, source_target_pairs={{0,64},{64,0},{128,192},{192,128},{1,65},{65,1},{129,193},{193,129... | collective-permute-start | bytes 208904 | tf_op jit(solution)/shard_map/ppermute | solution.py:440
  60.2 3.2 %collective-permute-start.5 = (f32[72,128]{1,0:T(8,128)S(1)}, f32[72,128]{1,0:T(8,128)S(1)}, u32[]{:S(2)}, u32[]{:S(2)}) collective-permute-start(f32[72,128]{1,0:T(8,128)S(1)} %get-tuple-element.28.mine_ref), channel_id=1, source_target_pairs={{0,16},{16,0},{1,17},{17,1},{2,18},{18,2},{3,19},{19,3},{4,20},{20... | collective-permute-start | bytes 110600 | tf_op jit(solution)/shard_map/ppermute | solution.py:443
  64.8 10.9 %all-to-all-start.1 = ((f32[8,144,128]{2,1,0:T(8,128)}), f32[8,144,128]{2,1,0:T(8,128)S(1)}, u32[]{:S(2)}, u32[]{:S(2)}) async-start(f32[8,144,128]{2,1,0:T(8,128)} %spread.1), calls=%async_computation.1 | async-start | bytes 1179648 | tf_op jit(solution)/shard_map/all_to_all | solution.py:447
  68.4 16.4 %collective-permute-start.8 = (f32[1024,128]{1,0:T(8,128)S(1)}, f32[1024,128]{1,0:T(8,128)S(1)}, u32[]{:S(2)}, u32[]{:S(2)}) collective-permute-start(f32[1024,128]{1,0:T(8,128)S(1)} %key_grads.1), channel_id=1, source_target_pairs={{0,1},{1,0},{2,3},{3,2},{4,5},{5,4},{6,7},{7,6},{8,9},{9,8},{10,11... | collective-permute-start | bytes 1572872 | tf_op jit(solution)/shard_map/ppermute | solution.py:445
  75.7 6.8 %collective-permute-start.7 = (f32[4,144,128]{2,1,0:T(8,128)S(1)}, f32[4,144,128]{2,1,0:T(8,128)S(1)}, u32[]{:S(2)}, u32[]{:S(2)}) collective-permute-start(f32[4,144,128]{2,1,0:T(8,128)S(1)} %get-tuple-element.38), channel_id=1, source_target_pairs={{0,2},{2,0},{1,3},{3,1},{4,6},{6,4},{5,7},{7,5},{8,10},{10,8},{9,1... | collective-permute-start | bytes 884744 | tf_op jit(solution)/shard_map/ppermute | solution.py:449
  80.4 2.2 %collective-permute-start.6 = (f32[4,144,128]{2,1,0:T(8,128)S(1)}, f32[4,144,128]{2,1,0:T(8,128)S(1)}, u32[]{:S(2)}, u32[]{:S(2)}) collective-permute-start(f32[4,144,128]{2,1,0:T(8,128)S(1)} %get-tuple-element.39), channel_id=1, source_target_pairs={{0,2},{2,0},{1,3},{3,1},{4,6},{6,4},{5,7},{7,5},{8,10},{10,8},{9,1... | collective-permute-start | bytes 884744 | tf_op jit(solution)/shard_map/ppermute | solution.py:449

commit v3 on v2

--- a/solution.py
+++ b/solution.py
@@ -16,11 +16,8 @@
 SCALE = (D**-0.5) * (H**-0.5)
 CTX = ("zh", "zl", "yl", "x", "c")
 NEAR = ("zl", "yl", "x")
-PLANE = ("zl", "x")
 FAR = "zh"
 N_NEAR = 16
-N_PLANE = 8
-N_X = 4
 N_FAR = 4
 CHUNK = HALF // N_NEAR
 KEY_ROWS = S
@@ -113,12 +110,16 @@
     return key <= query
 
 
-def target_kernel(who_ref, target_ref, index_ref, w_ref, q_ref, normal_ref, sums_ref, held_ref, weighted_ref):
+def target_kernel(who_ref, target_ref, index_ref, w_ref, q_ref, normal_ref, sums_ref, held_ref, weighted_ref, payload_ref):
     held_ref[...] = index_ref[...]
     w = columns_of([w_ref[j : j + 1, :] for j in range(JL)])
     for j in range(JL):
         at = slice(j * T, (j + 1) * T)
         weighted_ref[at, :] = (q_ref[at, :].astype(jnp.float32) * w[j]).astype(jnp.bfloat16)
+    core = who_ref[1]
+    payload_ref[:HALF, :] = q_ref[pl.ds(pl.multiple_of(core * HALF, HALF), HALF), :].astype(jnp.float32)
+    part = w_ref[pl.ds(pl.multiple_of(core * N_NEAR, N_NEAR), N_NEAR), :]
+    payload_ref[HALF:, :] = jnp.concatenate([part, jnp.zeros((N_NEAR, 128 - T), jnp.float32)], axis=1)
     valid = valid_mask(who_ref[0])
     target = target_ref[...]
     masked = jnp.where(valid, target, 0.0)
@@ -133,8 +134,14 @@
     return pl.pallas_call(
         target_kernel,
         in_specs=[IN_SMEM] + [IN_VMEM] * 4,
-        out_specs=[IN_VMEM] * 4,
-        out_shape=[f32(T, S), f32(T, 128), f32(T, S), jax.ShapeDtypeStruct((ROWS, D), jnp.bfloat16)],
+        out_specs=[IN_VMEM] * 5,
+        out_shape=[
+            f32(T, S),
+            f32(T, 128),
+            f32(T, S),
+            jax.ShapeDtypeStruct((ROWS, D), jnp.bfloat16),
+            f32(HALF + N_NEAR, D),
+        ],
         compiler_params=params(),
         name="target",
     )(who, target, partial_index, w, q)
@@ -286,8 +293,9 @@
     q = q_ref[pl.ds(pl.multiple_of(head * T, T), T), :].astype(jnp.float32)
     grads = jnp.broadcast_to(jnp.sum(gap_sum * q, axis=1, keepdims=True), (T, 128))
     grads = jnp.transpose(jnp.concatenate([grads, grads], axis=0))[:8]
-    out_ref[:CHUNK, :] = scaled
-    out_ref[CHUNK:, :] = grads
+    for p in range(N_NEAR):
+        out_ref[p, :CHUNK, :] = scaled
+        out_ref[p, CHUNK:, :] = grads
 
 
 def combine_far(who, own, far, w, q):
@@ -295,73 +303,51 @@
         far_kernel,
         in_specs=[IN_SMEM] + [IN_VMEM] * 6,
         out_specs=[IN_VMEM] * 3,
-        out_shape=[f32(CHUNK + 8, D), f32(8, 128), f32(8, 128)],
+        out_shape=[f32(N_NEAR, CHUNK + 8, D), f32(8, 128), f32(8, 128)],
         compiler_params=params(),
         name="combine_far",
     )(who, own, *far, w, q)
 
 
-def spread_kernel(who_ref, mine_ref, other_ref, out_ref):
-    size = CHUNK + 8
-    first = who_ref[3] == 0
-    for p in range(N_PLANE):
-        out_ref[p, :size, :] = jnp.where(first, mine_ref[...], other_ref[...])
-        out_ref[p, size:, :] = jnp.where(first, other_ref[...], mine_ref[...])
-
-
-def spread(who, mine, other):
-    return pl.pallas_call(
-        spread_kernel,
-        in_specs=[IN_SMEM] + [IN_VMEM] * 2,
-        out_specs=IN_VMEM,
-        out_shape=f32(N_PLANE, 2 * (CHUNK + 8), D),
-        compiler_params=params(),
-        name="spread",
-    )(who, mine, other)
-
-
-def chunks_of():
-    for p in range(N_PLANE):
-        for y in range(2):
-            yield (p // N_X * 2 + y) * N_X + p % N_X, p, y * (CHUNK + 8)
-
-
-def place_half(half, at, out_hbm, rows_ref, sem):
-    for j, p, r in chunks_of():
+def place_half(half, at, out_hbm, sem):
+    copies = []
+    for p in range(N_NEAR):
         ref, i = at(p)
-        rows_ref[pl.ds(j, T, stride=N_NEAR), :] = ref[i, r : r + CHUNK, :]
-    to = out_hbm.at[:, pl.ds(pl.multiple_of(half * N_NEAR, N_NEAR), N_NEAR), :]
-    copy = pltpu.make_async_copy(rows_ref.reshape(T, N_NEAR, D), to, sem)
-    copy.start()
-    return copy
-
-
-def first_kernel(who_ref, mine_ref, out_hbm, rows_ref, sem):
-    place_half(who_ref[1], lambda p: (mine_ref, p), out_hbm, rows_ref, sem).wait()
-
-
-def last_kernel(who_ref, mine_ref, lower_ref, upper_ref, begun_hbm, out_hbm, weights_ref, rows_ref, sem):
+        to = out_hbm.at[:, half * N_NEAR + p, :]
+        copies.append(pltpu.make_async_copy(ref.at[i, :CHUNK, :], to, sem.at[p]))
+    for copy in copies:
+        copy.start()
+    return copies
+
+
+def first_kernel(who_ref, mine_ref, out_hbm, sem):
+    for copy in place_half(who_ref[1], lambda p: (mine_ref, p), out_hbm, sem):
+        copy.wait()
+
+
+def last_kernel(who_ref, mine_ref, lower_ref, upper_ref, begun_hbm, out_hbm, weights_ref, sem):
     def mine_at(p):
         return mine_ref, p
 
     def other_at(p):
-        return (lower_ref, p) if p < N_PLANE // 2 else (upper_ref, p - N_PLANE // 2)
-
-    copy = place_half(1 - who_ref[1], other_at, out_hbm, rows_ref, sem)
+        return (lower_ref, p) if p < N_NEAR // 2 else (upper_ref, p - N_NEAR // 2)
+
+    copies = place_half(1 - who_ref[1], other_at, out_hbm, sem)
 
     def emit(first, second):
         for half, at in enumerate((first, second)):
-            for j, p, r in chunks_of():
+            for p in range(N_NEAR):
                 ref, i = at(p)
-                row = half * N_NEAR + j
-                weights_ref[row : row + 1, :] = ref[i, r + CHUNK : r + CHUNK + 1, :T]
+                row = half * N_NEAR + p
+                weights_ref[row : row + 1, :] = ref[i, CHUNK : CHUNK + 1, :T]
 
     pl.when(who_ref[1] == 0)(lambda: emit(mine_at, other_at))
     pl.when(who_ref[1] == 1)(lambda: emit(other_at, mine_at))
-    copy.wait()
-
-
-HALF_SCRATCH = [pltpu.VMEM((HALF, D), jnp.float32), pltpu.SemaphoreType.DMA(())]
+    for copy in copies:
+        copy.wait()
+
+
+HALF_SCRATCH = [pltpu.SemaphoreType.DMA((N_NEAR,))]
 
 
 def place_mine(who, mine):
@@ -389,47 +375,95 @@
     )(who, mine, *other, begun)
 
 
-def key_kernel(who_ref, index_ref, target_ref, stats_ref, q_ref, weighted_ref, k_ref, out_ref):
+def unpack_kernel(payload_ref, q_ref, weighted_ref):
+    w = columns_of([payload_ref[HALF + j : HALF + j + 1, :] for j in range(N_NEAR)])
+    for j in range(N_NEAR):
+        at = slice(j * T, (j + 1) * T)
+        q = payload_ref[at, :]
+        q_ref[at, :] = q.astype(jnp.bfloat16)
+        weighted_ref[at, :] = (q * w[j]).astype(jnp.bfloat16)
+
+
+KEY_TILE = 256
+
+
+def key_sums(gap, k, q_ref, weighted_ref):
+    span = 1024
+    gap = jnp.concatenate([gap] * (span // 128), axis=1)
+    acc = jnp.zeros((KEY_TILE, D), jnp.float32)
+    for r in range(0, q_ref.shape[0], span):
+        logits = lax.dot_general(k, q_ref[r : r + span, :], NT, preferred_element_type=jnp.float32)
+        picked = jnp.where(logits > 0.0, gap, 0.0).astype(jnp.bfloat16)
+        acc = acc + jnp.dot(picked, weighted_ref[r : r + span, :], preferred_element_type=jnp.float32)
+    return acc
+
+
+def own_kernel(who_ref, index_ref, target_ref, stats_ref, q_ref, weighted_ref, k_ref, out_ref, gap_ref):
     row_max, denom, mass = columns_of([stats_ref[i : i + 1, :] for i in range(3)])
     gap = jnp.exp(index_ref[...] - row_max) * (1.0 / denom) - target_ref[...] * (1.0 / mass)
     gap = jnp.where(valid_mask(who_ref[0]), gap, 0.0) * (SCALE / T)
-    tile, span = 256, 1024
-    for s in range(0, S, tile):
-        g = gap[:, s : s + tile]
-        g = jnp.transpose(jnp.concatenate([g, g], axis=0))
-        acc = jnp.zeros((tile, D), jnp.float32)
-        for r in range(0, ROWS, span):
-            logits = lax.dot_general(
-                k_ref[s : s + tile, :], q_ref[r : r + span, :], NT, preferred_element_type=jnp.float32
-            )
-            picked = jnp.where(logits > 0.0, jnp.concatenate([g] * (span // 128), axis=1), 0.0)
-            acc = acc + jnp.dot(
-                picked.astype(jnp.bfloat16), weighted_ref[r : r + span, :], preferred_element_type=jnp.float32
-            )
-        out_ref[s : s + tile, :] = acc
-
-
-def key_grads(who, index, target, stats, q, weighted, k):
-    return pl.pallas_call(
-        key_kernel,
+    for s in range(0, S, KEY_TILE):
+        at = slice(s, s + KEY_TILE)
+        turned = jnp.transpose(jnp.concatenate([gap[:, at]] * 2, axis=0))
+        gap_ref[at, :] = turned
+        out_ref[at, :] = key_sums(turned, k_ref[at, :], q_ref, weighted_ref)
+
+
+def own_key_grads(who, index, target, stats, q, weighted, k):
+    return pl.pallas_call(
+        own_kernel,
         in_specs=[IN_SMEM] + [IN_VMEM] * 6,
-        out_specs=IN_VMEM,
-        out_shape=f32(KEY_ROWS, D),
+        out_specs=[IN_VMEM] * 2,
+        out_shape=[f32(S, D)] * 2,
+        compiler_params=params(),
+        cost_estimate=cost(4 * ROWS * S * D, 4 << 20),
+        name="own_key_grads",
+    )(who, index, target, stats, q, weighted, k)
+
+
+def other_kernel(
+    own_ref, gap_ref, k_ref, payload_a_ref, payload_b_ref, out_hbm,
+    q_a_ref, weighted_a_ref, q_b_ref, weighted_b_ref, out_ref, sems,
+):
+    unpack_kernel(payload_a_ref, q_a_ref, weighted_a_ref)
+    unpack_kernel(payload_b_ref, q_b_ref, weighted_b_ref)
+    copies = []
+    for s in range(0, S, KEY_TILE):
+        at = slice(s, s + KEY_TILE)
+        gap, k = gap_ref[at, :], k_ref[at, :]
+        both = key_sums(gap, k, q_a_ref, weighted_a_ref) + key_sums(gap, k, q_b_ref, weighted_b_ref)
+        out_ref[at, :] = own_ref[at, :] + both
+        copies.append(pltpu.make_async_copy(out_ref.at[at], out_hbm.at[at], sems.at[s // KEY_TILE]))
+        copies[-1].start()
+    for copy in copies:
+        copy.wait()
+
+
+def key_grads(own, gap, k, *heads):
+    return pl.pallas_call(
+        other_kernel,
+        in_specs=[IN_VMEM] * 5,
+        out_specs=IN_HBM,
+        out_shape=f32(S, D),
+        scratch_shapes=[pltpu.VMEM((HALF, D), jnp.bfloat16)] * 4
+        + [pltpu.VMEM((S, D), jnp.float32), pltpu.SemaphoreType.DMA((S // KEY_TILE,))],
         compiler_params=params(),
         cost_estimate=cost(4 * ROWS * S * D, 4 << 20),
         name="key_grads",
-    )(who, index, target, stats, q, weighted, k)
+    )(own, gap, k, *heads)
 
 
 def on_device(index_queries, head_weights, index_keys, main_target):
     swap = [(0, 1), (1, 0)]
     core = lax.axis_index("c")
     head = core * N_NEAR + lax.axis_index(NEAR)
-    who = jnp.stack([lax.axis_index(CTX), core, head, lax.axis_index("yl")]).astype(jnp.int32)
+    who = jnp.stack([lax.axis_index(CTX), core, head]).astype(jnp.int32)
     w = head_weights.T
     partial_index, q = score(index_queries, w, index_keys)
     other_index = lax.ppermute(partial_index, "yh", swap)
-    target, target_sum, held_index, weighted = target_sums(who, main_target, partial_index, w, q)
+    target, target_sum, held_index, weighted, payload = target_sums(who, main_target, partial_index, w, q)
+    payload = lax.ppermute(payload, "yh", swap)
+    payloads = [payload, lax.ppermute(payload, "c", swap)]
     index, stats, parts = local_stats(who, held_index, other_index, target, target_sum)
 
     send = query_sums(1 - who[1:2], parts, stats, q, index_keys, "query_sums_send")
@@ -440,16 +474,14 @@
     far = [lax.ppermute(own, FAR, [(i, i ^ d) for i in range(N_FAR)]) for d in range(1, N_FAR)]
     chunk, total_stats, loss = combine_far(who, own, far, w, q)
 
-    other_chunk = lax.ppermute(chunk, "yl", swap)
-    key_part = key_grads(who, index, main_target, total_stats, q, weighted, index_keys)
-    other_key_part = lax.ppermute(key_part, "yh", swap)
-    other_chunk, _ = lax.optimization_barrier((other_chunk, key_part))
-    mine = lax.all_to_all(spread(who, chunk, other_chunk), PLANE, 0, 0, tiled=True)
-    half = N_PLANE // 2
+    mine = lax.all_to_all(chunk, NEAR, 0, 0, tiled=True)
+    own, gap = own_key_grads(who, index, main_target, total_stats, q, weighted, index_keys)
+    grad_keys = key_grads(own, gap, index_keys, *payloads)
+    mine, grad_keys = lax.optimization_barrier((mine, grad_keys))
+    half = N_NEAR // 2
     other = [lax.ppermute(x, "c", swap) for x in (mine[:half], mine[half:])]
     grad_queries, grad_weights = place_other(who, mine, other, place_mine(who, mine))
-    grad_weights, key_part = lax.optimization_barrier((grad_weights, key_part))
-    return grad_queries, grad_weights.T, key_part[:S] + other_key_part[:S], loss[0, :T]
+    return grad_queries, grad_weights.T, grad_keys, loss[0, :T]
 
 
 def solution(mesh):

time: 86 us -> 82.1 us (0.955)
  waiting for transfers between devices: 12.8 us -> 6.3 us
  Pallas kernels: 20.1 us -> 22.7 us
  other arithmetic: 0.94 us -> 0.08 us
    all_to_all x1, waiting for transfers between devices: 4.62 us -> 0.01 us  [on_device(): mine = lax.all_to_all(chunk, NEAR, 0, 0, tiled=True)]
    ppermute x2, starting transfers between devices: 2.95 us -> 6.42 us  [the longest x1 3.8 us: on_device(): payloads = [payload, lax.ppermute(payload, 'c', swap)]]
    ppermute x3, waiting for transfers between devices: 6.32 us -> 3.38 us  [on_device(): lax.ppermute(own, FAR, [(i, i ^ d) for i in range(N_FAR)])]
    ppermute x2, starting transfers between devices: 4.74 us -> 1.88 us  [on_device(): other = [lax.ppermute(x, 'c', swap) for x in (mine[:half], mine[half:])]]
    pallas_call x2, Pallas kernels: 4.33 us -> 6.29 us  [the longest x1 3.37 us: key_grads(): pl.pallas_call(other_kernel, in_specs=[IN_VMEM] * 5, out_specs=IN_HBM, ou...]
    ppermute x2, waiting for transfers between devices: 0.01 us -> 1.05 us  [the longest x1 1.05 us: on_device(): payload = lax.ppermute(payload, 'yh', swap)]
    add x1 -> x0, other arithmetic: 0.86 us -> none  [on_device(): key_part[:S] + other_key_part[:S]]
  transfers between devices with their start and end apart: 10 -> 10, of which waited for: 6 -> 5; matrix products, arithmetic and copies ran while one was open for 1% -> 1% of each run, Pallas kernels for 11% -> 15%
where the time goes in v3:
time: 82.1 us; the launch traced here: 81.7 us
  starting transfers between devices  25.6 us (31%)
  blocking collectives  22.8 us (28%)
  Pallas kernels  22.7 us (28%)
  waiting for transfers between devices  6.3 us (8%)
  local copies, waits for them, and re-layouts  3.28 us (4%)
  between operations  0.93 us (1%)
    all_to_all x1, blocking collectives, on_device(): near = lax.all_to_all(pack(keep, recv), NEAR, 0, 0, tiled=True)  22.8 us
    ppermute x3, starting transfers between devices, on_device(): lax.ppermute(own, FAR, [(i, i ^ d) for i in range(N_FAR)])  7.29 us
    pallas_call x1, Pallas kernels, score(): pl.pallas_call(score_kernel, in_specs=[IN_HBM, IN_VMEM, IN_HBM], out_spec...  4.13 us
    ppermute x1, starting transfers between devices, on_device(): other_index = lax.ppermute(partial_index, 'yh', swap)  3.83 us
    ppermute x1, starting transfers between devices, on_device(): payloads = [payload, lax.ppermute(payload, 'c', swap)]  3.8 us
    all_to_all x1, starting transfers between devices, on_device(): mine = lax.all_to_all(chunk, NEAR, 0, 0, tiled=True)  3.78 us
    pallas_call x2, Pallas kernels, query_sums(): pl.pallas_call(query_kernel, in_specs=[IN_SMEM] + [IN_VMEM] * 4, out_spec...  3.62 us
    ppermute x3, waiting for transfers between devices, on_device(): lax.ppermute(own, FAR, [(i, i ^ d) for i in range(N_FAR)])  3.38 us
  transfers between devices with their start and end apart: 10, of which 5 were waited for; matrix products, arithmetic and copies ran while one was open for 1% of the time, Pallas kernels for 15%

profile of v3, /device:TPU:1, one launch (start us, length us, event | category | flops | bytes accessed | tf_op | source)
XLA Modules:
  0.0 81.7 jit_solution(13576277352246074499)
XLA Ops:
  0.7 4.1 %score.1 = (f32[64,1024]{1,0:T(8,128)}, bf16[2048,128]{1,0:T(8,128)(2,1)}) custom-call(bf16[64,32,128]{2,1,0:T(8,128)(2,1)} %q_hbm.1, f32[32,64]{1,0:T(8,128)} %bitcast.7, bf16[1024,128]{1,0:T(8,128)(2,1)} %k_ref.7), custom_call_target="tpu_custom_call" | custom-call | tf_op jit(solution)/shard_map/score/pallas_call | solution.py:91
  4.8 3.8 %collective-permute-start = (f32[64,1024]{1,0:T(8,128)}, f32[64,1024]{1,0:T(8,128)S(1)}, u32[]{:S(2)}, u32[]{:S(2)}) collective-permute-start(f32[64,1024]{1,0:T(8,128)} %get-tuple-element.23.index_ref), channel_id=1, source_target_pairs={{0,1},{1,0},{2,3},{3,2},{4,5},{5,4},{6,7},{7,6},{8,9},{9,8},{10,11... | collective-permute-start | bytes 786440 | tf_op jit(solution)/shard_map/ppermute | solution.py:463
  8.7 1.0 %copy-done = bf16[2048,128]{1,0:T(8,128)(2,1)S(1)} copy-done((bf16[2048,128]{1,0:T(8,128)(2,1)S(1)}, bf16[2048,128]{1,0:T(8,128)(2,1)}, u32[]{:S(2)}) %copy-start) | copy-done | bytes 524312
  9.7 0.9 %copy-done.4 = f32[64,1024]{1,0:T(8,128)S(1)} copy-done((f32[64,1024]{1,0:T(8,128)S(1)}, f32[64,1024]{1,0:T(8,128)}, u32[]{:S(2)}) %copy-start.4) | copy-done | bytes 262168
  11.4 1.1 %target.1 = (f32[64,1024]{1,0:T(8,128)S(1)}, f32[64,128]{1,0:T(8,128)S(1)}, f32[64,1024]{1,0:T(8,128)S(1)}, bf16[2048,128]{1,0:T(8,128)(2,1)S(1)}, f32[1040,128]{1,0:T(8,128)S(1)}) custom-call(s32[3]{0:T(128)S(1)} %pad_add_fusion.who_ref, f32[64,1024]{1,0:T(8,128)S(1)} %copy-done.3, f32[64,1024]{1,0:T(8,128)S(1)} %copy-done.4, f32[32,64]{1,0:T(8,128)S(1)} %bitcast.8, ...), custom_call_target="tpu_custom_call" | custom-call | tf_op jit(solution)/shard_map/target/pallas_call | solution.py:134
  12.5 1.4 %collective-permute-done.other_ref = f32[64,1024]{1,0:T(8,128)S(1)} collective-permute-done((f32[64,1024]{1,0:T(8,128)}, f32[64,1024]{1,0:T(8,128)S(1)}, u32[]{:S(2)}, u32[]{:S(2)}) %collective-permute-start) | collective-permute-done | bytes 262176 | tf_op jit(solution)/shard_map/ppermute | solution.py:463
  13.9 0.9 %stats.1 = (f32[64,1024]{1,0:T(8,128)S(1)}, f32[8,128]{1,0:T(8,128)S(1)}, bf16[2,64,1024]{2,1,0:T(8,128)(2,1)S(1)}) custom-call(s32[3]{0:T(128)S(1)} %pad_add_fusion.who_ref, f32[64,1024]{1,0:T(8,128)S(1)} %get-tuple-element.25.mine_ref, f32[64,1024]{1,0:T(8,128)S(1)} %collective-permute-done.other_ref, f32[64,1024]{1,0:T(8,128)S(1)} %get-tuple-element.26.target_ref, ...), custom_call_target="tpu_custom_call" | custom-call | tf_op jit(solution)/shard_map/stats/pallas_call | solution.py:174
  14.9 1.8 %query_sums_send.1 = f32[2056,128]{1,0:T(8,128)S(1)} custom-call(s32[1]{0:T(128)S(6)} %sub.3.who_ref, bf16[2,64,1024]{2,1,0:T(8,128)(2,1)S(1)} %get-tuple-element.28.parts_ref, f32[8,128]{1,0:T(8,128)S(1)} %get-tuple-element.29.stats_ref, bf16[2048,128]{1,0:T(8,128)(2,1)S(1)} %copy-done.1, bf16[1024,128]{1,0:T(8,128)(2,1)S(1)} %copy-done.2), custom_call_target="tpu_custom_call" | custom-call | flops 805306368 | bytes 4194304 | tf_op jit(solution)/shard_map/query_sums_send/pallas_call | solution.py:201
  16.7 2.4 %collective-permute-start.1 = (f32[2056,128]{1,0:T(8,128)S(1)}, f32[2056,128]{1,0:T(8,128)S(1)}, u32[]{:S(2)}, u32[]{:S(2)}) collective-permute-start(f32[2056,128]{1,0:T(8,128)S(1)} %query_sums_send.1), channel_id=1, source_target_pairs={{0,2},{2,0},{1,3},{3,1},{4,6},{6,4},{5,7},{7,5},{8,10},{10,8},{9,1... | collective-permute-start | bytes 3158024 | tf_op jit(solution)/shard_map/ppermute | solution.py:470
  19.1 1.8 %query_sums_keep.1.keep_ref = f32[2056,128]{1,0:T(8,128)S(1)} custom-call(s32[1]{0:T(128)} %bitcast.1.who_ref, bf16[2,64,1024]{2,1,0:T(8,128)(2,1)S(1)} %get-tuple-element.28.parts_ref, f32[8,128]{1,0:T(8,128)S(1)} %get-tuple-element.29.stats_ref, bf16[2048,128]{1,0:T(8,128)(2,1)S(1)} %copy-done.1, bf16[1024,128]{1,0:T(8,128)(2,1)S(1)} %copy-done.2), custom_call_target="tpu_custom_call" | custom-call | flops 805306368 | bytes 4194304 | tf_op jit(solution)/shard_map/query_sums_keep/pallas_call | solution.py:201
  21.9 22.8 %all_to_all.10.in_ref = f32[16,136,128]{2,1,0:T(8,128)S(1)} all-to-all(f32[16,136,128]{2,1,0:T(8,128)S(1)} %pack.1), channel_id=1, replica_groups=mesh['zh'=4,'zl'=2,'yl'=2,'x'=4,'c'=2,'yh'=2] {'zl','yl','x'}, dimensions={0} | all-to-all | bytes 2228224 | tf_op jit(solution)/shard_map/all_to_all | solution.py:472
  45.4 3.1 %collective-permute-start.2 = (f32[136,128]{1,0:T(8,128)S(1)}, f32[136,128]{1,0:T(8,128)S(1)}, u32[]{:S(2)}, u32[]{:S(2)}) collective-permute-start(f32[136,128]{1,0:T(8,128)S(1)} %combine_near.1.a_ref), channel_id=1, source_target_pairs={{0,64},{64,0},{128,192},{192,128},{1,65},{65,1},{129,193},{193,129... | collective-permute-start | bytes 208904 | tf_op jit(solution)/shard_map/ppermute | solution.py:474
  48.5 4.2 %collective-permute-start.3 = (f32[136,128]{1,0:T(8,128)S(1)}, f32[136,128]{1,0:T(8,128)S(1)}, u32[]{:S(2)}, u32[]{:S(2)}) collective-permute-start(f32[136,128]{1,0:T(8,128)S(1)} %combine_near.1.a_ref), channel_id=1, source_target_pairs={{0,128},{64,192},{128,0},{192,64},{1,129},{65,193},{129,1},{193,65... | collective-permute-start | bytes 208904 | tf_op jit(solution)/shard_map/ppermute | solution.py:474
  52.7 2.6 %collective-permute-start.5 = (f32[1040,128]{1,0:T(8,128)S(1)}, f32[1040,128]{1,0:T(8,128)S(1)}, u32[]{:S(2)}, u32[]{:S(2)}) collective-permute-start(f32[1040,128]{1,0:T(8,128)S(1)} %get-tuple-element.36), channel_id=1, source_target_pairs={{0,1},{1,0},{2,3},{3,2},{4,5},{5,4},{6,7},{7,6},{8,9},{9,8},{10,11... | collective-permute-start | bytes 1597448 | tf_op jit(solution)/shard_map/ppermute | solution.py:465
  55.7 3.0 %collective-permute-done.4.d_ref = f32[136,128]{1,0:T(8,128)S(1)} collective-permute-done((f32[136,128]{1,0:T(8,128)S(1)}, f32[136,128]{1,0:T(8,128)S(1)}, u32[]{:S(2)}, u32[]{:S(2)}) %collective-permute-start.4) | collective-permute-done | bytes 69664 | tf_op jit(solution)/shard_map/ppermute | solution.py:474
  58.7 1.9 %combine_far.1 = (f32[16,72,128]{2,1,0:T(8,128)}, f32[8,128]{1,0:T(8,128)S(1)}, f32[8,128]{1,0:T(8,128)S(1)}) custom-call(s32[3]{0:T(128)S(1)} %pad_add_fusion.who_ref, f32[136,128]{1,0:T(8,128)S(1)} %combine_near.1.a_ref, f32[136,128]{1,0:T(8,128)S(1)} %collective-permute-done.2.b_ref, f32[136,128]{1,0:T(8,128)S(1)} %collective-permute-done.3.c_ref, ...), custom_call_target="tpu_custom_call" | custom-call | tf_op jit(solution)/shard_map/combine_far/pallas_call | solution.py:302
  60.6 3.8 %all-to-all-start.1 = ((f32[16,72,128]{2,1,0:T(8,128)}), f32[16,72,128]{2,1,0:T(8,128)S(1)}, u32[]{:S(2)}, u32[]{:S(2)}) async-start(f32[16,72,128]{2,1,0:T(8,128)} %get-tuple-element.30), calls=%async_computation.1 | async-start | bytes 1179648 | tf_op jit(solution)/shard_map/all_to_all | solution.py:477
  64.4 1.0 %collective-permute-done.5.payload_a_ref = f32[1040,128]{1,0:T(8,128)S(1)} collective-permute-done((f32[1040,128]{1,0:T(8,128)S(1)}, f32[1040,128]{1,0:T(8,128)S(1)}, u32[]{:S(2)}, u32[]{:S(2)}) %collective-permute-start.5) | collective-permute-done | bytes 532512 | tf_op jit(solution)/shard_map/ppermute | solution.py:465
  65.5 3.8 %collective-permute-start.6 = (f32[1040,128]{1,0:T(8,128)S(1)}, f32[1040,128]{1,0:T(8,128)S(1)}, u32[]{:S(2)}, u32[]{:S(2)}) collective-permute-start(f32[1040,128]{1,0:T(8,128)S(1)} %collective-permute-done.5.payload_a_ref), channel_id=1, source_target_pairs={{0,2},{2,0},{1,3},{3,1},{4,6},{6,4},{5,7},{7,5},{8,10},{10,8},{9,1... | collective-permute-start | bytes 1597448 | tf_op jit(solution)/shard_map/ppermute | solution.py:466
  69.3 2.9 %own_key_grads.1 = (f32[1024,128]{1,0:T(8,128)S(1)}, f32[1024,128]{1,0:T(8,128)S(1)}) custom-call(s32[3]{0:T(128)S(1)} %pad_add_fusion.who_ref, f32[64,1024]{1,0:T(8,128)S(1)} %get-tuple-element.31.index_ref, f32[64,1024]{1,0:T(8,128)S(1)} %copy-done.3, f32[8,128]{1,0:T(8,128)S(1)} %get-tuple-element.32.stats_ref, bf16[2048,128]{1,0:T(8,128)(2,1)S(1)} %copy-done.1, ...), custom_call_target="tpu_custom_call" | custom-call | flops 1073741824 | bytes 4194304 | tf_op jit(solution)/shard_map/own_key_grads/pallas_call | solution.py:413
  72.2 3.4 %key_grads.1 = f32[1024,128]{1,0:T(8,128)} custom-call(f32[1024,128]{1,0:T(8,128)S(1)} %get-tuple-element.34.own_ref, f32[1024,128]{1,0:T(8,128)S(1)} %get-tuple-element.35.gap_ref, bf16[1024,128]{1,0:T(8,128)(2,1)S(1)} %copy-done.2, f32[1040,128]{1,0:T(8,128)S(1)} %collective-permute-done.5.payload_a_ref, f32[1040,128]{1,0:T(8,128)S(1)} %collective-permute-done.6.payload_b_ref), custom_call_target="tpu_custom_call" | custom-call | flops 1073741824 | bytes 4194304 | tf_op jit(solution)/shard_map/key_grads/pallas_call | solution.py:443
  75.6 1.8 %collective-permute-start.7 = (f32[8,72,128]{2,1,0:T(8,128)S(1)}, f32[8,72,128]{2,1,0:T(8,128)S(1)}, u32[]{:S(2)}, u32[]{:S(2)}) collective-permute-start(f32[8,72,128]{2,1,0:T(8,128)S(1)} %get-tuple-element.43), channel_id=1, source_target_pairs={{0,2},{2,0},{1,3},{3,1},{4,6},{6,4},{5,7},{7,5},{8,10},{10,8},{9,1... | collective-permute-start | bytes 884744 | tf_op jit(solution)/shard_map/ppermute | solution.py:482
  78.0 1.5 %place_mine.1.begun_hbm = f32[64,32,128]{2,1,0:T(8,128)} custom-call(s32[3]{0:T(128)S(1)} %pad_add_fusion.who_ref, f32[16,72,128]{2,1,0:T(8,128)S(1)} %all-to-all-done.1.mine_ref), custom_call_target="tpu_custom_call" | custom-call | tf_op jit(solution)/shard_map/place_mine/pallas_call | solution.py:354
  79.5 2.1 %place_other.1 = (f32[64,32,128]{2,1,0:T(8,128)}, f32[32,64]{1,0:T(8,128)}) custom-call(s32[3]{0:T(128)S(1)} %pad_add_fusion.who_ref, f32[16,72,128]{2,1,0:T(8,128)S(1)} %all-to-all-done.1.mine_ref, f32[8,72,128]{2,1,0:T(8,128)S(1)} %collective-permute-done.7.lower_ref, ...), custom_call_target="tpu_custom_call", output_to_operand_aliasing={{0}: (4, {})} | custom-call | tf_op jit(solution)/shard_map/place_other/pallas_call | solution.py:366
  (26 shorter events, 3.5 us)
Async XLA Ops:
  0.6 8.1 %copy-start.3 = (f32[64,1024]{1,0:T(8,128)S(1)}, f32[64,1024]{1,0:T(8,128)}, u32[]{:S(2)}) copy-start(f32[64,1024]{1,0:T(8,128)} %target_ref.3) | copy-start | bytes 786436
  0.6 14.2 %copy-start.2 = (bf16[1024,128]{1,0:T(8,128)(2,1)S(1)}, bf16[1024,128]{1,0:T(8,128)(2,1)}, u32[]{:S(2)}) copy-start(bf16[1024,128]{1,0:T(8,128)(2,1)} %k_ref.7) | copy-start | bytes 786436
  4.8 9.1 %collective-permute-start = (f32[64,1024]{1,0:T(8,128)}, f32[64,1024]{1,0:T(8,128)S(1)}, u32[]{:S(2)}, u32[]{:S(2)}) collective-permute-start(f32[64,1024]{1,0:T(8,128)} %get-tuple-element.23.index_ref), channel_id=1, source_target_pairs={{0,1},{1,0},{2,3},{3,2},{4,5},{5,4},{6,7},{7,6},{8,9},{9,8},{10,11... | collective-permute-start | bytes 786440 | tf_op jit(solution)/shard_map/ppermute | solution.py:463
  8.7 1.0 %copy-start = (bf16[2048,128]{1,0:T(8,128)(2,1)S(1)}, bf16[2048,128]{1,0:T(8,128)(2,1)}, u32[]{:S(2)}) copy-start(bf16[2048,128]{1,0:T(8,128)(2,1)} %get-tuple-element.24.q_ref) | copy-start | bytes 1572868
  9.7 0.9 %copy-start.4 = (f32[64,1024]{1,0:T(8,128)S(1)}, f32[64,1024]{1,0:T(8,128)}, u32[]{:S(2)}) copy-start(f32[64,1024]{1,0:T(8,128)} %get-tuple-element.23.index_ref) | copy-start | bytes 786436
  10.7 0.7 copy-start.5
  11.4 3.4 %copy-start.1 = (bf16[2048,128]{1,0:T(8,128)(2,1)S(1)}, bf16[2048,128]{1,0:T(8,128)(2,1)}, u32[]{:S(2)}) copy-start(bf16[2048,128]{1,0:T(8,128)(2,1)} %get-tuple-element.24.q_ref) | copy-start | bytes 1572868
  16.7 4.7 %collective-permute-start.1 = (f32[2056,128]{1,0:T(8,128)S(1)}, f32[2056,128]{1,0:T(8,128)S(1)}, u32[]{:S(2)}, u32[]{:S(2)}) collective-permute-start(f32[2056,128]{1,0:T(8,128)S(1)} %query_sums_send.1), channel_id=1, source_target_pairs={{0,2},{2,0},{1,3},{3,1},{4,6},{6,4},{5,7},{7,5},{8,10},{10,8},{9,1... | collective-permute-start | bytes 3158024 | tf_op jit(solution)/shard_map/ppermute | solution.py:470
  44.7 14.0 %copy-start.6 = (f32[64,32]{0,1:T(8,128)S(1)}, f32[64,32]{0,1:T(8,128)}, u32[]{:S(2)}) copy-start(f32[64,32]{0,1:T(8,128)} %param.5) | copy-start | bytes 24580
  45.4 9.9 %collective-permute-start.2 = (f32[136,128]{1,0:T(8,128)S(1)}, f32[136,128]{1,0:T(8,128)S(1)}, u32[]{:S(2)}, u32[]{:S(2)}) collective-permute-start(f32[136,128]{1,0:T(8,128)S(1)} %combine_near.1.a_ref), channel_id=1, source_target_pairs={{0,64},{64,0},{128,192},{192,128},{1,65},{65,1},{129,193},{193,129... | collective-permute-start | bytes 208904 | tf_op jit(solution)/shard_map/ppermute | solution.py:474
  48.5 7.2 %collective-permute-start.3 = (f32[136,128]{1,0:T(8,128)S(1)}, f32[136,128]{1,0:T(8,128)S(1)}, u32[]{:S(2)}, u32[]{:S(2)}) collective-permute-start(f32[136,128]{1,0:T(8,128)S(1)} %combine_near.1.a_ref), channel_id=1, source_target_pairs={{0,128},{64,192},{128,0},{192,64},{1,129},{65,193},{129,1},{193,65... | collective-permute-start | bytes 208904 | tf_op jit(solution)/shard_map/ppermute | solution.py:474
  52.7 6.0 %collective-permute-start.4 = (f32[136,128]{1,0:T(8,128)S(1)}, f32[136,128]{1,0:T(8,128)S(1)}, u32[]{:S(2)}, u32[]{:S(2)}) collective-permute-start(f32[136,128]{1,0:T(8,128)S(1)} %combine_near.1.a_ref), channel_id=1, source_target_pairs={{0,192},{64,128},{128,64},{192,0},{1,193},{65,129},{129,65},{193,1... | collective-permute-start | bytes 208904 | tf_op jit(solution)/shard_map/ppermute | solution.py:474
  52.7 12.7 %collective-permute-start.5 = (f32[1040,128]{1,0:T(8,128)S(1)}, f32[1040,128]{1,0:T(8,128)S(1)}, u32[]{:S(2)}, u32[]{:S(2)}) collective-permute-start(f32[1040,128]{1,0:T(8,128)S(1)} %get-tuple-element.36), channel_id=1, source_target_pairs={{0,1},{1,0},{2,3},{3,2},{4,5},{5,4},{6,7},{7,6},{8,9},{9,8},{10,11... | collective-permute-start | bytes 1597448 | tf_op jit(solution)/shard_map/ppermute | solution.py:465
  60.6 15.0 %all-to-all-start.1 = ((f32[16,72,128]{2,1,0:T(8,128)}), f32[16,72,128]{2,1,0:T(8,128)S(1)}, u32[]{:S(2)}, u32[]{:S(2)}) async-start(f32[16,72,128]{2,1,0:T(8,128)} %get-tuple-element.30), calls=%async_computation.1 | async-start | bytes 1179648 | tf_op jit(solution)/shard_map/all_to_all | solution.py:477
  65.5 6.7 %collective-permute-start.6 = (f32[1040,128]{1,0:T(8,128)S(1)}, f32[1040,128]{1,0:T(8,128)S(1)}, u32[]{:S(2)}, u32[]{:S(2)}) collective-permute-start(f32[1040,128]{1,0:T(8,128)S(1)} %collective-permute-done.5.payload_a_ref), channel_id=1, source_target_pairs={{0,2},{2,0},{1,3},{3,1},{4,6},{6,4},{5,7},{7,5},{8,10},{10,8},{9,1... | collective-permute-start | bytes 1597448 | tf_op jit(solution)/shard_map/ppermute | solution.py:466
  75.6 3.9 %collective-permute-start.7 = (f32[8,72,128]{2,1,0:T(8,128)S(1)}, f32[8,72,128]{2,1,0:T(8,128)S(1)}, u32[]{:S(2)}, u32[]{:S(2)}) collective-permute-start(f32[8,72,128]{2,1,0:T(8,128)S(1)} %get-tuple-element.43), channel_id=1, source_target_pairs={{0,2},{2,0},{1,3},{3,1},{4,6},{6,4},{5,7},{7,5},{8,10},{10,8},{9,1... | collective-permute-start | bytes 884744 | tf_op jit(solution)/shard_map/ppermute | solution.py:482
  77.4 2.1 %collective-permute-start.8 = (f32[8,72,128]{2,1,0:T(8,128)S(1)}, f32[8,72,128]{2,1,0:T(8,128)S(1)}, u32[]{:S(2)}, u32[]{:S(2)}) collective-permute-start(f32[8,72,128]{2,1,0:T(8,128)S(1)} %get-tuple-element.42), channel_id=1, source_target_pairs={{0,2},{2,0},{1,3},{3,1},{4,6},{6,4},{5,7},{7,5},{8,10},{10,8},{9,1... | collective-permute-start | bytes 884744 | tf_op jit(solution)/shard_map/ppermute | solution.py:482

commit v4 on v3

--- a/solution.py
+++ b/solution.py
@@ -286,7 +286,7 @@
     row_max, denom, mass, entropy, cross = (total[i : i + 1] for i in range(5))
     stats_ref[...] = total
     loss = entropy / mass - jnp.log(mass) - cross / mass + row_max + jnp.log(denom)
-    loss_ref[...] = jnp.broadcast_to(loss, loss_ref.shape)
+    loss_ref[...] = loss[0, :T]
     gap_sum = gap_sum * (SCALE / T)
     head = who_ref[2]
     scaled = gap_sum * columns_of([w_ref[pl.ds(head, 1), :]])[0]
@@ -303,7 +303,7 @@
         far_kernel,
         in_specs=[IN_SMEM] + [IN_VMEM] * 6,
         out_specs=[IN_VMEM] * 3,
-        out_shape=[f32(N_NEAR, CHUNK + 8, D), f32(8, 128), f32(8, 128)],
+        out_shape=[f32(N_NEAR, CHUNK + 8, D), f32(8, 128), f32(T)],
         compiler_params=params(),
         name="combine_far",
     )(who, own, *far, w, q)
@@ -325,7 +325,7 @@
         copy.wait()
 
 
-def last_kernel(who_ref, mine_ref, lower_ref, upper_ref, begun_hbm, out_hbm, weights_ref, sem):
+def last_kernel(who_ref, mine_ref, lower_ref, upper_ref, begun_hbm, out_hbm, weights_hbm, sem, weights_ref, weights_sem):
     def mine_at(p):
         return mine_ref, p
 
@@ -343,6 +343,8 @@
 
     pl.when(who_ref[1] == 0)(lambda: emit(mine_at, other_at))
     pl.when(who_ref[1] == 1)(lambda: emit(other_at, mine_at))
+    copies.append(pltpu.make_async_copy(weights_ref, weights_hbm, weights_sem))
+    copies[-1].start()
     for copy in copies:
         copy.wait()
 
@@ -366,9 +368,9 @@
     return pl.pallas_call(
         last_kernel,
         in_specs=[IN_SMEM, IN_VMEM, IN_VMEM, IN_VMEM, IN_HBM],
-        out_specs=[IN_HBM, IN_VMEM],
+        out_specs=[IN_HBM] * 2,
         out_shape=[f32(T, JL, D), f32(JL, T)],
-        scratch_shapes=HALF_SCRATCH,
+        scratch_shapes=HALF_SCRATCH + [pltpu.VMEM((JL, T), jnp.float32), pltpu.SemaphoreType.DMA(())],
         input_output_aliases={4: 0},
         compiler_params=params(),
         name="place_other",
@@ -481,7 +483,7 @@
     half = N_NEAR // 2
     other = [lax.ppermute(x, "c", swap) for x in (mine[:half], mine[half:])]
     grad_queries, grad_weights = place_other(who, mine, other, place_mine(who, mine))
-    return grad_queries, grad_weights.T, grad_keys, loss[0, :T]
+    return grad_queries, grad_weights.T, grad_keys, loss
 
 
 def solution(mesh):

time: 82.1 us -> 81.1 us (0.988)
  transfers between devices with their start and end apart: 10 -> 10, of which waited for: 5 -> 6; matrix products, arithmetic and copies ran while one was open for 1% -> 0% of each run, Pallas kernels for 15% -> 16%
where the time goes in v4:
time: 81.1 us; the launch traced here: 80.7 us
  starting transfers between devices  25.6 us (32%)
  blocking collectives  22.8 us (28%)
  Pallas kernels  22.1 us (27%)
  waiting for transfers between devices  6.35 us (8%)
  local copies, waits for them, and re-layouts  2.77 us (3%)
  between operations  0.92 us (1%)
    all_to_all x1, blocking collectives, on_device(): near = lax.all_to_all(pack(keep, recv), NEAR, 0, 0, tiled=True)  22.8 us
    ppermute x3, starting transfers between devices, on_device(): lax.ppermute(own, FAR, [(i, i ^ d) for i in range(N_FAR)])  7.29 us
    pallas_call x1, Pallas kernels, score(): pl.pallas_call(score_kernel, in_specs=[IN_HBM, IN_VMEM, IN_HBM], out_spec...  4.13 us
    ppermute x1, starting transfers between devices, on_device(): other_index = lax.ppermute(partial_index, 'yh', swap)  3.83 us
    ppermute x1, starting transfers between devices, on_device(): payloads = [payload, lax.ppermute(payload, 'c', swap)]  3.8 us
    all_to_all x1, starting transfers between devices, on_device(): mine = lax.all_to_all(chunk, NEAR, 0, 0, tiled=True)  3.78 us
    pallas_call x2, Pallas kernels, query_sums(): pl.pallas_call(query_kernel, in_specs=[IN_SMEM] + [IN_VMEM] * 4, out_spec...  3.62 us
    ppermute x3, waiting for transfers between devices, on_device(): lax.ppermute(own, FAR, [(i, i ^ d) for i in range(N_FAR)])  3.38 us
  transfers between devices with their start and end apart: 10, of which 6 were waited for; matrix products, arithmetic and copies ran while one was open for 0% of the time, Pallas kernels for 16%

profile of v4, /device:TPU:1, one launch (start us, length us, event | category | flops | bytes accessed | tf_op | source)
XLA Modules:
  0.0 80.7 jit_solution(14135652334363392827)
XLA Ops:
  0.7 4.1 %score.1 = (f32[64,1024]{1,0:T(8,128)}, bf16[2048,128]{1,0:T(8,128)(2,1)}) custom-call(bf16[64,32,128]{2,1,0:T(8,128)(2,1)} %q_hbm.1, f32[32,64]{1,0:T(8,128)} %bitcast.5, bf16[1024,128]{1,0:T(8,128)(2,1)} %k_ref.7), custom_call_target="tpu_custom_call" | custom-call | tf_op jit(solution)/shard_map/score/pallas_call | solution.py:91
  4.8 3.8 %collective-permute-start = (f32[64,1024]{1,0:T(8,128)}, f32[64,1024]{1,0:T(8,128)S(1)}, u32[]{:S(2)}, u32[]{:S(2)}) collective-permute-start(f32[64,1024]{1,0:T(8,128)} %get-tuple-element.23.index_ref), channel_id=1, source_target_pairs={{0,1},{1,0},{2,3},{3,2},{4,5},{5,4},{6,7},{7,6},{8,9},{9,8},{10,11... | collective-permute-start | bytes 786440 | tf_op jit(solution)/shard_map/ppermute | solution.py:465
  8.7 1.0 %copy-done = bf16[2048,128]{1,0:T(8,128)(2,1)S(1)} copy-done((bf16[2048,128]{1,0:T(8,128)(2,1)S(1)}, bf16[2048,128]{1,0:T(8,128)(2,1)}, u32[]{:S(2)}) %copy-start) | copy-done | bytes 524312
  9.7 0.9 %copy-done.4 = f32[64,1024]{1,0:T(8,128)S(1)} copy-done((f32[64,1024]{1,0:T(8,128)S(1)}, f32[64,1024]{1,0:T(8,128)}, u32[]{:S(2)}) %copy-start.4) | copy-done | bytes 262168
  11.4 1.1 %target.1 = (f32[64,1024]{1,0:T(8,128)S(1)}, f32[64,128]{1,0:T(8,128)S(1)}, f32[64,1024]{1,0:T(8,128)S(1)}, bf16[2048,128]{1,0:T(8,128)(2,1)S(1)}, f32[1040,128]{1,0:T(8,128)S(1)}) custom-call(s32[3]{0:T(128)S(1)} %pad_add_fusion.who_ref, f32[64,1024]{1,0:T(8,128)S(1)} %copy-done.3, f32[64,1024]{1,0:T(8,128)S(1)} %copy-done.4, f32[32,64]{1,0:T(8,128)S(1)} %bitcast.6, ...), custom_call_target="tpu_custom_call" | custom-call | tf_op jit(solution)/shard_map/target/pallas_call | solution.py:134
  12.5 1.4 %collective-permute-done.other_ref = f32[64,1024]{1,0:T(8,128)S(1)} collective-permute-done((f32[64,1024]{1,0:T(8,128)}, f32[64,1024]{1,0:T(8,128)S(1)}, u32[]{:S(2)}, u32[]{:S(2)}) %collective-permute-start) | collective-permute-done | bytes 262176 | tf_op jit(solution)/shard_map/ppermute | solution.py:465
  13.9 0.9 %stats.1 = (f32[64,1024]{1,0:T(8,128)S(1)}, f32[8,128]{1,0:T(8,128)S(1)}, bf16[2,64,1024]{2,1,0:T(8,128)(2,1)S(1)}) custom-call(s32[3]{0:T(128)S(1)} %pad_add_fusion.who_ref, f32[64,1024]{1,0:T(8,128)S(1)} %get-tuple-element.25.mine_ref, f32[64,1024]{1,0:T(8,128)S(1)} %collective-permute-done.other_ref, f32[64,1024]{1,0:T(8,128)S(1)} %get-tuple-element.26.target_ref, ...), custom_call_target="tpu_custom_call" | custom-call | tf_op jit(solution)/shard_map/stats/pallas_call | solution.py:174
  14.9 1.8 %query_sums_send.1 = f32[2056,128]{1,0:T(8,128)S(1)} custom-call(s32[1]{0:T(128)S(6)} %sub.3.who_ref, bf16[2,64,1024]{2,1,0:T(8,128)(2,1)S(1)} %get-tuple-element.28.parts_ref, f32[8,128]{1,0:T(8,128)S(1)} %get-tuple-element.29.stats_ref, bf16[2048,128]{1,0:T(8,128)(2,1)S(1)} %copy-done.1, bf16[1024,128]{1,0:T(8,128)(2,1)S(1)} %copy-done.2), custom_call_target="tpu_custom_call" | custom-call | flops 805306368 | bytes 4194304 | tf_op jit(solution)/shard_map/query_sums_send/pallas_call | solution.py:201
  16.7 2.4 %collective-permute-start.1 = (f32[2056,128]{1,0:T(8,128)S(1)}, f32[2056,128]{1,0:T(8,128)S(1)}, u32[]{:S(2)}, u32[]{:S(2)}) collective-permute-start(f32[2056,128]{1,0:T(8,128)S(1)} %query_sums_send.1), channel_id=1, source_target_pairs={{0,2},{2,0},{1,3},{3,1},{4,6},{6,4},{5,7},{7,5},{8,10},{10,8},{9,1... | collective-permute-start | bytes 3158024 | tf_op jit(solution)/shard_map/ppermute | solution.py:472
  19.1 1.8 %query_sums_keep.1.keep_ref = f32[2056,128]{1,0:T(8,128)S(1)} custom-call(s32[1]{0:T(128)} %bitcast.1.who_ref, bf16[2,64,1024]{2,1,0:T(8,128)(2,1)S(1)} %get-tuple-element.28.parts_ref, f32[8,128]{1,0:T(8,128)S(1)} %get-tuple-element.29.stats_ref, bf16[2048,128]{1,0:T(8,128)(2,1)S(1)} %copy-done.1, bf16[1024,128]{1,0:T(8,128)(2,1)S(1)} %copy-done.2), custom_call_target="tpu_custom_call" | custom-call | flops 805306368 | bytes 4194304 | tf_op jit(solution)/shard_map/query_sums_keep/pallas_call | solution.py:201
  21.9 22.8 %all_to_all.10.in_ref = f32[16,136,128]{2,1,0:T(8,128)S(1)} all-to-all(f32[16,136,128]{2,1,0:T(8,128)S(1)} %pack.1), channel_id=1, replica_groups=mesh['zh'=4,'zl'=2,'yl'=2,'x'=4,'c'=2,'yh'=2] {'zl','yl','x'}, dimensions={0} | all-to-all | bytes 2228224 | tf_op jit(solution)/shard_map/all_to_all | solution.py:474
  45.4 3.1 %collective-permute-start.2 = (f32[136,128]{1,0:T(8,128)S(1)}, f32[136,128]{1,0:T(8,128)S(1)}, u32[]{:S(2)}, u32[]{:S(2)}) collective-permute-start(f32[136,128]{1,0:T(8,128)S(1)} %combine_near.1.a_ref), channel_id=1, source_target_pairs={{0,64},{64,0},{128,192},{192,128},{1,65},{65,1},{129,193},{193,129... | collective-permute-start | bytes 208904 | tf_op jit(solution)/shard_map/ppermute | solution.py:476
  48.5 4.2 %collective-permute-start.3 = (f32[136,128]{1,0:T(8,128)S(1)}, f32[136,128]{1,0:T(8,128)S(1)}, u32[]{:S(2)}, u32[]{:S(2)}) collective-permute-start(f32[136,128]{1,0:T(8,128)S(1)} %combine_near.1.a_ref), channel_id=1, source_target_pairs={{0,128},{64,192},{128,0},{192,64},{1,129},{65,193},{129,1},{193,65... | collective-permute-start | bytes 208904 | tf_op jit(solution)/shard_map/ppermute | solution.py:476
  52.7 2.6 %collective-permute-start.5 = (f32[1040,128]{1,0:T(8,128)S(1)}, f32[1040,128]{1,0:T(8,128)S(1)}, u32[]{:S(2)}, u32[]{:S(2)}) collective-permute-start(f32[1040,128]{1,0:T(8,128)S(1)} %get-tuple-element.36), channel_id=1, source_target_pairs={{0,1},{1,0},{2,3},{3,2},{4,5},{5,4},{6,7},{7,6},{8,9},{9,8},{10,11... | collective-permute-start | bytes 1597448 | tf_op jit(solution)/shard_map/ppermute | solution.py:467
  55.7 3.0 %collective-permute-done.4.d_ref = f32[136,128]{1,0:T(8,128)S(1)} collective-permute-done((f32[136,128]{1,0:T(8,128)S(1)}, f32[136,128]{1,0:T(8,128)S(1)}, u32[]{:S(2)}, u32[]{:S(2)}) %collective-permute-start.4) | collective-permute-done | bytes 69664 | tf_op jit(solution)/shard_map/ppermute | solution.py:476
  58.7 1.9 %combine_far.1 = (f32[16,72,128]{2,1,0:T(8,128)}, f32[8,128]{1,0:T(8,128)S(1)}, f32[64]{0:T(128)}) custom-call(s32[3]{0:T(128)S(1)} %pad_add_fusion.who_ref, f32[136,128]{1,0:T(8,128)S(1)} %combine_near.1.a_ref, f32[136,128]{1,0:T(8,128)S(1)} %collective-permute-done.2.b_ref, f32[136,128]{1,0:T(8,128)S(1)} %collective-permute-done.3.c_ref, ...), custom_call_target="tpu_custom_call" | custom-call | tf_op jit(solution)/shard_map/combine_far/pallas_call | solution.py:302
  60.6 3.8 %all-to-all-start.1 = ((f32[16,72,128]{2,1,0:T(8,128)}), f32[16,72,128]{2,1,0:T(8,128)S(1)}, u32[]{:S(2)}, u32[]{:S(2)}) async-start(f32[16,72,128]{2,1,0:T(8,128)} %get-tuple-element.30), calls=%async_computation.1 | async-start | bytes 1179648 | tf_op jit(solution)/shard_map/all_to_all | solution.py:479
  64.4 1.0 %collective-permute-done.5.payload_a_ref = f32[1040,128]{1,0:T(8,128)S(1)} collective-permute-done((f32[1040,128]{1,0:T(8,128)S(1)}, f32[1040,128]{1,0:T(8,128)S(1)}, u32[]{:S(2)}, u32[]{:S(2)}) %collective-permute-start.5) | collective-permute-done | bytes 532512 | tf_op jit(solution)/shard_map/ppermute | solution.py:467
  65.5 3.8 %collective-permute-start.6 = (f32[1040,128]{1,0:T(8,128)S(1)}, f32[1040,128]{1,0:T(8,128)S(1)}, u32[]{:S(2)}, u32[]{:S(2)}) collective-permute-start(f32[1040,128]{1,0:T(8,128)S(1)} %collective-permute-done.5.payload_a_ref), channel_id=1, source_target_pairs={{0,2},{2,0},{1,3},{3,1},{4,6},{6,4},{5,7},{7,5},{8,10},{10,8},{9,1... | collective-permute-start | bytes 1597448 | tf_op jit(solution)/shard_map/ppermute | solution.py:468
  69.3 2.9 %own_key_grads.1 = (f32[1024,128]{1,0:T(8,128)S(1)}, f32[1024,128]{1,0:T(8,128)S(1)}) custom-call(s32[3]{0:T(128)S(1)} %pad_add_fusion.who_ref, f32[64,1024]{1,0:T(8,128)S(1)} %get-tuple-element.31.index_ref, f32[64,1024]{1,0:T(8,128)S(1)} %copy-done.3, f32[8,128]{1,0:T(8,128)S(1)} %get-tuple-element.32.stats_ref, bf16[2048,128]{1,0:T(8,128)(2,1)S(1)} %copy-done.1, ...), custom_call_target="tpu_custom_call" | custom-call | flops 1073741824 | bytes 4194304 | tf_op jit(solution)/shard_map/own_key_grads/pallas_call | solution.py:415
  72.2 3.4 %key_grads.1 = f32[1024,128]{1,0:T(8,128)} custom-call(f32[1024,128]{1,0:T(8,128)S(1)} %get-tuple-element.34.own_ref, f32[1024,128]{1,0:T(8,128)S(1)} %get-tuple-element.35.gap_ref, bf16[1024,128]{1,0:T(8,128)(2,1)S(1)} %copy-done.2, f32[1040,128]{1,0:T(8,128)S(1)} %collective-permute-done.5.payload_a_ref, f32[1040,128]{1,0:T(8,128)S(1)} %collective-permute-done.6.payload_b_ref), custom_call_target="tpu_custom_call" | custom-call | flops 1073741824 | bytes 4194304 | tf_op jit(solution)/shard_map/key_grads/pallas_call | solution.py:445
  75.6 1.8 %collective-permute-start.7 = (f32[8,72,128]{2,1,0:T(8,128)S(1)}, f32[8,72,128]{2,1,0:T(8,128)S(1)}, u32[]{:S(2)}, u32[]{:S(2)}) collective-permute-start(f32[8,72,128]{2,1,0:T(8,128)S(1)} %get-tuple-element.43), channel_id=1, source_target_pairs={{0,2},{2,0},{1,3},{3,1},{4,6},{6,4},{5,7},{7,5},{8,10},{10,8},{9,1... | collective-permute-start | bytes 884744 | tf_op jit(solution)/shard_map/ppermute | solution.py:484
  77.5 1.5 %place_mine.1.begun_hbm = f32[64,32,128]{2,1,0:T(8,128)} custom-call(s32[3]{0:T(128)S(1)} %pad_add_fusion.who_ref, f32[16,72,128]{2,1,0:T(8,128)S(1)} %all-to-all-done.1.mine_ref), custom_call_target="tpu_custom_call" | custom-call | tf_op jit(solution)/shard_map/place_mine/pallas_call | solution.py:356
  79.1 1.5 %place_other.1 = (f32[64,32,128]{2,1,0:T(8,128)}, f32[32,64]{1,0:T(8,128)}) custom-call(s32[3]{0:T(128)S(1)} %pad_add_fusion.who_ref, f32[16,72,128]{2,1,0:T(8,128)S(1)} %all-to-all-done.1.mine_ref, f32[8,72,128]{2,1,0:T(8,128)S(1)} %collective-permute-done.7.lower_ref, ...), custom_call_target="tpu_custom_call", output_to_operand_aliasing={{0}: (4, {})} | custom-call | tf_op jit(solution)/shard_map/place_other/pallas_call | solution.py:368
  (25 shorter events, 3.0 us)
Async XLA Ops:
  0.6 8.1 %copy-start.3 = (f32[64,1024]{1,0:T(8,128)S(1)}, f32[64,1024]{1,0:T(8,128)}, u32[]{:S(2)}) copy-start(f32[64,1024]{1,0:T(8,128)} %target_ref.3) | copy-start | bytes 786436
  0.6 14.2 %copy-start.2 = (bf16[1024,128]{1,0:T(8,128)(2,1)S(1)}, bf16[1024,128]{1,0:T(8,128)(2,1)}, u32[]{:S(2)}) copy-start(bf16[1024,128]{1,0:T(8,128)(2,1)} %k_ref.7) | copy-start | bytes 786436
  4.8 9.1 %collective-permute-start = (f32[64,1024]{1,0:T(8,128)}, f32[64,1024]{1,0:T(8,128)S(1)}, u32[]{:S(2)}, u32[]{:S(2)}) collective-permute-start(f32[64,1024]{1,0:T(8,128)} %get-tuple-element.23.index_ref), channel_id=1, source_target_pairs={{0,1},{1,0},{2,3},{3,2},{4,5},{5,4},{6,7},{7,6},{8,9},{9,8},{10,11... | collective-permute-start | bytes 786440 | tf_op jit(solution)/shard_map/ppermute | solution.py:465
  8.7 1.0 %copy-start = (bf16[2048,128]{1,0:T(8,128)(2,1)S(1)}, bf16[2048,128]{1,0:T(8,128)(2,1)}, u32[]{:S(2)}) copy-start(bf16[2048,128]{1,0:T(8,128)(2,1)} %get-tuple-element.24.q_ref) | copy-start | bytes 1572868
  9.7 0.9 %copy-start.4 = (f32[64,1024]{1,0:T(8,128)S(1)}, f32[64,1024]{1,0:T(8,128)}, u32[]{:S(2)}) copy-start(f32[64,1024]{1,0:T(8,128)} %get-tuple-element.23.index_ref) | copy-start | bytes 786436
  10.7 0.7 copy-start.5
  11.4 3.4 %copy-start.1 = (bf16[2048,128]{1,0:T(8,128)(2,1)S(1)}, bf16[2048,128]{1,0:T(8,128)(2,1)}, u32[]{:S(2)}) copy-start(bf16[2048,128]{1,0:T(8,128)(2,1)} %get-tuple-element.24.q_ref) | copy-start | bytes 1572868
  16.7 4.7 %collective-permute-start.1 = (f32[2056,128]{1,0:T(8,128)S(1)}, f32[2056,128]{1,0:T(8,128)S(1)}, u32[]{:S(2)}, u32[]{:S(2)}) collective-permute-start(f32[2056,128]{1,0:T(8,128)S(1)} %query_sums_send.1), channel_id=1, source_target_pairs={{0,2},{2,0},{1,3},{3,1},{4,6},{6,4},{5,7},{7,5},{8,10},{10,8},{9,1... | collective-permute-start | bytes 3158024 | tf_op jit(solution)/shard_map/ppermute | solution.py:472
  44.7 14.0 %copy-start.6 = (f32[64,32]{0,1:T(8,128)S(1)}, f32[64,32]{0,1:T(8,128)}, u32[]{:S(2)}) copy-start(f32[64,32]{0,1:T(8,128)} %param.5) | copy-start | bytes 24580
  45.4 9.9 %collective-permute-start.2 = (f32[136,128]{1,0:T(8,128)S(1)}, f32[136,128]{1,0:T(8,128)S(1)}, u32[]{:S(2)}, u32[]{:S(2)}) collective-permute-start(f32[136,128]{1,0:T(8,128)S(1)} %combine_near.1.a_ref), channel_id=1, source_target_pairs={{0,64},{64,0},{128,192},{192,128},{1,65},{65,1},{129,193},{193,129... | collective-permute-start | bytes 208904 | tf_op jit(solution)/shard_map/ppermute | solution.py:476
  48.5 7.2 %collective-permute-start.3 = (f32[136,128]{1,0:T(8,128)S(1)}, f32[136,128]{1,0:T(8,128)S(1)}, u32[]{:S(2)}, u32[]{:S(2)}) collective-permute-start(f32[136,128]{1,0:T(8,128)S(1)} %combine_near.1.a_ref), channel_id=1, source_target_pairs={{0,128},{64,192},{128,0},{192,64},{1,129},{65,193},{129,1},{193,65... | collective-permute-start | bytes 208904 | tf_op jit(solution)/shard_map/ppermute | solution.py:476
  52.7 6.0 %collective-permute-start.4 = (f32[136,128]{1,0:T(8,128)S(1)}, f32[136,128]{1,0:T(8,128)S(1)}, u32[]{:S(2)}, u32[]{:S(2)}) collective-permute-start(f32[136,128]{1,0:T(8,128)S(1)} %combine_near.1.a_ref), channel_id=1, source_target_pairs={{0,192},{64,128},{128,64},{192,0},{1,193},{65,129},{129,65},{193,1... | collective-permute-start | bytes 208904 | tf_op jit(solution)/shard_map/ppermute | solution.py:476
  52.7 12.7 %collective-permute-start.5 = (f32[1040,128]{1,0:T(8,128)S(1)}, f32[1040,128]{1,0:T(8,128)S(1)}, u32[]{:S(2)}, u32[]{:S(2)}) collective-permute-start(f32[1040,128]{1,0:T(8,128)S(1)} %get-tuple-element.36), channel_id=1, source_target_pairs={{0,1},{1,0},{2,3},{3,2},{4,5},{5,4},{6,7},{7,6},{8,9},{9,8},{10,11... | collective-permute-start | bytes 1597448 | tf_op jit(solution)/shard_map/ppermute | solution.py:467
  60.6 14.9 %all-to-all-start.1 = ((f32[16,72,128]{2,1,0:T(8,128)}), f32[16,72,128]{2,1,0:T(8,128)S(1)}, u32[]{:S(2)}, u32[]{:S(2)}) async-start(f32[16,72,128]{2,1,0:T(8,128)} %get-tuple-element.30), calls=%async_computation.1 | async-start | bytes 1179648 | tf_op jit(solution)/shard_map/all_to_all | solution.py:479
  65.5 6.7 %collective-permute-start.6 = (f32[1040,128]{1,0:T(8,128)S(1)}, f32[1040,128]{1,0:T(8,128)S(1)}, u32[]{:S(2)}, u32[]{:S(2)}) collective-permute-start(f32[1040,128]{1,0:T(8,128)S(1)} %collective-permute-done.5.payload_a_ref), channel_id=1, source_target_pairs={{0,2},{2,0},{1,3},{3,1},{4,6},{6,4},{5,7},{7,5},{8,10},{10,8},{9,1... | collective-permute-start | bytes 1597448 | tf_op jit(solution)/shard_map/ppermute | solution.py:468
  75.6 3.4 %collective-permute-start.7 = (f32[8,72,128]{2,1,0:T(8,128)S(1)}, f32[8,72,128]{2,1,0:T(8,128)S(1)}, u32[]{:S(2)}, u32[]{:S(2)}) collective-permute-start(f32[8,72,128]{2,1,0:T(8,128)S(1)} %get-tuple-element.43), channel_id=1, source_target_pairs={{0,2},{2,0},{1,3},{3,1},{4,6},{6,4},{5,7},{7,5},{8,10},{10,8},{9,1... | collective-permute-start | bytes 884744 | tf_op jit(solution)/shard_map/ppermute | solution.py:484
  77.4 1.6 %collective-permute-start.8 = (f32[8,72,128]{2,1,0:T(8,128)S(1)}, f32[8,72,128]{2,1,0:T(8,128)S(1)}, u32[]{:S(2)}, u32[]{:S(2)}) collective-permute-start(f32[8,72,128]{2,1,0:T(8,128)S(1)} %get-tuple-element.42), channel_id=1, source_target_pairs={{0,2},{2,0},{1,3},{3,1},{4,6},{6,4},{5,7},{7,5},{8,10},{10,8},{9,1... | collective-permute-start | bytes 884744 | tf_op jit(solution)/shard_map/ppermute | solution.py:484

commit v5 on v4

--- a/solution.py
+++ b/solution.py
@@ -15,7 +15,7 @@
 POS = 131072 - T
 SCALE = (D**-0.5) * (H**-0.5)
 CTX = ("zh", "zl", "yl", "x", "c")
-NEAR = ("zl", "yl", "x")
+NEAR = ("x", "yl", "zl")
 FAR = "zh"
 N_NEAR = 16
 N_FAR = 4
@@ -325,12 +325,12 @@
         copy.wait()
 
 
-def last_kernel(who_ref, mine_ref, lower_ref, upper_ref, begun_hbm, out_hbm, weights_hbm, sem, weights_ref, weights_sem):
+def last_kernel(who_ref, mine_ref, other_ref, begun_hbm, out_hbm, weights_hbm, sem, weights_ref, weights_sem):
     def mine_at(p):
         return mine_ref, p
 
     def other_at(p):
-        return (lower_ref, p) if p < N_NEAR // 2 else (upper_ref, p - N_NEAR // 2)
+        return other_ref, p
 
     copies = place_half(1 - who_ref[1], other_at, out_hbm, sem)
 
@@ -367,11 +367,11 @@
 def place_other(who, mine, other, begun):
     return pl.pallas_call(
         last_kernel,
-        in_specs=[IN_SMEM, IN_VMEM, IN_VMEM, IN_VMEM, IN_HBM],
+        in_specs=[IN_SMEM, IN_VMEM, IN_VMEM, IN_HBM],
         out_specs=[IN_HBM] * 2,
         out_shape=[f32(T, JL, D), f32(JL, T)],
         scratch_shapes=HALF_SCRATCH + [pltpu.VMEM((JL, T), jnp.float32), pltpu.SemaphoreType.DMA(())],
-        input_output_aliases={4: 0},
+        input_output_aliases={3: 0},
         compiler_params=params(),
         name="place_other",
     )(who, mine, *other, begun)
@@ -480,8 +480,7 @@
     own, gap = own_key_grads(who, index, main_target, total_stats, q, weighted, index_keys)
     grad_keys = key_grads(own, gap, index_keys, *payloads)
     mine, grad_keys = lax.optimization_barrier((mine, grad_keys))
-    half = N_NEAR // 2
-    other = [lax.ppermute(x, "c", swap) for x in (mine[:half], mine[half:])]
+    other = [lax.ppermute(mine, "c", swap)]
     grad_queries, grad_weights = place_other(who, mine, other, place_mine(who, mine))
     return grad_queries, grad_weights.T, grad_keys, loss
 

time: 81.1 us -> 80.3 us (level)
  starting transfers between devices: 25.6 us -> 24.5 us
    ppermute x2 -> x1, starting transfers between devices: 1.89 us -> 0.65 us  [on_device(): other = [lax.ppermute(mine, 'c', swap)]]
  transfers between devices with their start and end apart: 10 -> 9, of which waited for: 6 -> 6; matrix products, arithmetic and copies ran while one was open for 0% -> 0% of each run, Pallas kernels for 16% -> 16%
where the time goes in v5:
time: 80.3 us; the launch traced here: 79.1 us
  starting transfers between devices  24.5 us (31%)
  blocking collectives  22.5 us (28%)
  Pallas kernels  22.1 us (28%)
  waiting for transfers between devices  6.28 us (8%)
  local copies, waits for them, and re-layouts  2.73 us (3%)
  between operations  0.9 us (1%)
    all_to_all x1, blocking collectives, on_device(): near = lax.all_to_all(pack(keep, recv), NEAR, 0, 0, tiled=True)  22.5 us
    ppermute x3, starting transfers between devices, on_device(): lax.ppermute(own, FAR, [(i, i ^ d) for i in range(N_FAR)])  7.29 us
    pallas_call x1, Pallas kernels, score(): pl.pallas_call(score_kernel, in_specs=[IN_HBM, IN_VMEM, IN_HBM], out_spec...  4.13 us
    ppermute x1, starting transfers between devices, on_device(): payloads = [payload, lax.ppermute(payload, 'c', swap)]  3.97 us
    ppermute x1, starting transfers between devices, on_device(): other_index = lax.ppermute(partial_index, 'yh', swap)  3.83 us
    all_to_all x1, starting transfers between devices, on_device(): mine = lax.all_to_all(chunk, NEAR, 0, 0, tiled=True)  3.78 us
    pallas_call x2, Pallas kernels, query_sums(): pl.pallas_call(query_kernel, in_specs=[IN_SMEM] + [IN_VMEM] * 4, out_spec...  3.62 us
    ppermute x3, waiting for transfers between devices, on_device(): lax.ppermute(own, FAR, [(i, i ^ d) for i in range(N_FAR)])  3.38 us
  transfers between devices with their start and end apart: 9, of which 6 were waited for; matrix products, arithmetic and copies ran while one was open for 0% of the time, Pallas kernels for 16%

profile of v5, /device:TPU:1, one launch (start us, length us, event | category | flops | bytes accessed | tf_op | source)
XLA Modules:
  0.0 79.1 jit_solution(1950667326615762967)
XLA Ops:
  0.7 4.1 %score.1 = (f32[64,1024]{1,0:T(8,128)}, bf16[2048,128]{1,0:T(8,128)(2,1)}) custom-call(bf16[64,32,128]{2,1,0:T(8,128)(2,1)} %q_hbm.1, f32[32,64]{1,0:T(8,128)} %bitcast.5, bf16[1024,128]{1,0:T(8,128)(2,1)} %k_ref.7), custom_call_target="tpu_custom_call" | custom-call | tf_op jit(solution)/shard_map/score/pallas_call | solution.py:91
  4.8 3.8 %collective-permute-start = (f32[64,1024]{1,0:T(8,128)}, f32[64,1024]{1,0:T(8,128)S(1)}, u32[]{:S(2)}, u32[]{:S(2)}) collective-permute-start(f32[64,1024]{1,0:T(8,128)} %get-tuple-element.23.index_ref), channel_id=1, source_target_pairs={{0,1},{1,0},{2,3},{3,2},{4,5},{5,4},{6,7},{7,6},{8,9},{9,8},{10,11... | collective-permute-start | bytes 786440 | tf_op jit(solution)/shard_map/ppermute | solution.py:465
  8.7 1.0 %copy-done = bf16[2048,128]{1,0:T(8,128)(2,1)S(1)} copy-done((bf16[2048,128]{1,0:T(8,128)(2,1)S(1)}, bf16[2048,128]{1,0:T(8,128)(2,1)}, u32[]{:S(2)}) %copy-start) | copy-done | bytes 524312
  9.7 0.9 %copy-done.4 = f32[64,1024]{1,0:T(8,128)S(1)} copy-done((f32[64,1024]{1,0:T(8,128)S(1)}, f32[64,1024]{1,0:T(8,128)}, u32[]{:S(2)}) %copy-start.4) | copy-done | bytes 262168
  11.4 1.1 %target.1 = (f32[64,1024]{1,0:T(8,128)S(1)}, f32[64,128]{1,0:T(8,128)S(1)}, f32[64,1024]{1,0:T(8,128)S(1)}, bf16[2048,128]{1,0:T(8,128)(2,1)S(1)}, f32[1040,128]{1,0:T(8,128)S(1)}) custom-call(s32[3]{0:T(128)S(1)} %pad_add_fusion.who_ref, f32[64,1024]{1,0:T(8,128)S(1)} %copy-done.3, f32[64,1024]{1,0:T(8,128)S(1)} %copy-done.4, f32[32,64]{1,0:T(8,128)S(1)} %bitcast.6, ...), custom_call_target="tpu_custom_call" | custom-call | tf_op jit(solution)/shard_map/target/pallas_call | solution.py:134
  12.5 1.4 %collective-permute-done.other_ref = f32[64,1024]{1,0:T(8,128)S(1)} collective-permute-done((f32[64,1024]{1,0:T(8,128)}, f32[64,1024]{1,0:T(8,128)S(1)}, u32[]{:S(2)}, u32[]{:S(2)}) %collective-permute-start) | collective-permute-done | bytes 262176 | tf_op jit(solution)/shard_map/ppermute | solution.py:465
  13.9 0.9 %stats.1 = (f32[64,1024]{1,0:T(8,128)S(1)}, f32[8,128]{1,0:T(8,128)S(1)}, bf16[2,64,1024]{2,1,0:T(8,128)(2,1)S(1)}) custom-call(s32[3]{0:T(128)S(1)} %pad_add_fusion.who_ref, f32[64,1024]{1,0:T(8,128)S(1)} %get-tuple-element.25.mine_ref, f32[64,1024]{1,0:T(8,128)S(1)} %collective-permute-done.other_ref, f32[64,1024]{1,0:T(8,128)S(1)} %get-tuple-element.26.target_ref, ...), custom_call_target="tpu_custom_call" | custom-call | tf_op jit(solution)/shard_map/stats/pallas_call | solution.py:174
  14.9 1.8 %query_sums_send.1 = f32[2056,128]{1,0:T(8,128)S(1)} custom-call(s32[1]{0:T(128)S(6)} %sub.3.who_ref, bf16[2,64,1024]{2,1,0:T(8,128)(2,1)S(1)} %get-tuple-element.28.parts_ref, f32[8,128]{1,0:T(8,128)S(1)} %get-tuple-element.29.stats_ref, bf16[2048,128]{1,0:T(8,128)(2,1)S(1)} %copy-done.1, bf16[1024,128]{1,0:T(8,128)(2,1)S(1)} %copy-done.2), custom_call_target="tpu_custom_call" | custom-call | flops 805306368 | bytes 4194304 | tf_op jit(solution)/shard_map/query_sums_send/pallas_call | solution.py:201
  16.7 2.4 %collective-permute-start.1 = (f32[2056,128]{1,0:T(8,128)S(1)}, f32[2056,128]{1,0:T(8,128)S(1)}, u32[]{:S(2)}, u32[]{:S(2)}) collective-permute-start(f32[2056,128]{1,0:T(8,128)S(1)} %query_sums_send.1), channel_id=1, source_target_pairs={{0,2},{2,0},{1,3},{3,1},{4,6},{6,4},{5,7},{7,5},{8,10},{10,8},{9,1... | collective-permute-start | bytes 3158024 | tf_op jit(solution)/shard_map/ppermute | solution.py:472
  19.1 1.8 %query_sums_keep.1.keep_ref = f32[2056,128]{1,0:T(8,128)S(1)} custom-call(s32[1]{0:T(128)} %bitcast.1.who_ref, bf16[2,64,1024]{2,1,0:T(8,128)(2,1)S(1)} %get-tuple-element.28.parts_ref, f32[8,128]{1,0:T(8,128)S(1)} %get-tuple-element.29.stats_ref, bf16[2048,128]{1,0:T(8,128)(2,1)S(1)} %copy-done.1, bf16[1024,128]{1,0:T(8,128)(2,1)S(1)} %copy-done.2), custom_call_target="tpu_custom_call" | custom-call | flops 805306368 | bytes 4194304 | tf_op jit(solution)/shard_map/query_sums_keep/pallas_call | solution.py:201
  21.9 22.5 %all_to_all.10.in_ref = f32[16,136,128]{2,1,0:T(8,128)S(1)} all-to-all(f32[16,136,128]{2,1,0:T(8,128)S(1)} %pack.1), channel_id=1, replica_groups=mesh['zh'=4,'zl'=2,'yl'=2,'x'=4,'c'=2,'yh'=2] {'x','yl','zl'}, dimensions={0} | all-to-all | bytes 2228224 | tf_op jit(solution)/shard_map/all_to_all | solution.py:474
  44.4 0.7 combine_near.1.a_ref
  45.1 3.1 %collective-permute-start.2 = (f32[136,128]{1,0:T(8,128)S(1)}, f32[136,128]{1,0:T(8,128)S(1)}, u32[]{:S(2)}, u32[]{:S(2)}) collective-permute-start(f32[136,128]{1,0:T(8,128)S(1)} %combine_near.1.a_ref), channel_id=1, source_target_pairs={{0,64},{64,0},{128,192},{192,128},{1,65},{65,1},{129,193},{193,129... | collective-permute-start | bytes 208904 | tf_op jit(solution)/shard_map/ppermute | solution.py:476
  48.2 4.2 %collective-permute-start.3 = (f32[136,128]{1,0:T(8,128)S(1)}, f32[136,128]{1,0:T(8,128)S(1)}, u32[]{:S(2)}, u32[]{:S(2)}) collective-permute-start(f32[136,128]{1,0:T(8,128)S(1)} %combine_near.1.a_ref), channel_id=1, source_target_pairs={{0,128},{64,192},{128,0},{192,64},{1,129},{65,193},{129,1},{193,65... | collective-permute-start | bytes 208904 | tf_op jit(solution)/shard_map/ppermute | solution.py:476
  52.4 2.6 %collective-permute-start.5 = (f32[1040,128]{1,0:T(8,128)S(1)}, f32[1040,128]{1,0:T(8,128)S(1)}, u32[]{:S(2)}, u32[]{:S(2)}) collective-permute-start(f32[1040,128]{1,0:T(8,128)S(1)} %get-tuple-element.36), channel_id=1, source_target_pairs={{0,1},{1,0},{2,3},{3,2},{4,5},{5,4},{6,7},{7,6},{8,9},{9,8},{10,11... | collective-permute-start | bytes 1597448 | tf_op jit(solution)/shard_map/ppermute | solution.py:467
  55.3 3.1 %collective-permute-done.4.d_ref = f32[136,128]{1,0:T(8,128)S(1)} collective-permute-done((f32[136,128]{1,0:T(8,128)S(1)}, f32[136,128]{1,0:T(8,128)S(1)}, u32[]{:S(2)}, u32[]{:S(2)}) %collective-permute-start.4) | collective-permute-done | bytes 69664 | tf_op jit(solution)/shard_map/ppermute | solution.py:476
  58.4 1.9 %combine_far.1 = (f32[16,72,128]{2,1,0:T(8,128)}, f32[8,128]{1,0:T(8,128)S(1)}, f32[64]{0:T(128)}) custom-call(s32[3]{0:T(128)S(1)} %pad_add_fusion.who_ref, f32[136,128]{1,0:T(8,128)S(1)} %combine_near.1.a_ref, f32[136,128]{1,0:T(8,128)S(1)} %collective-permute-done.2.b_ref, f32[136,128]{1,0:T(8,128)S(1)} %collective-permute-done.3.c_ref, ...), custom_call_target="tpu_custom_call" | custom-call | tf_op jit(solution)/shard_map/combine_far/pallas_call | solution.py:302
  60.3 3.8 %all-to-all-start.1 = ((f32[16,72,128]{2,1,0:T(8,128)}), f32[16,72,128]{2,1,0:T(8,128)S(1)}, u32[]{:S(2)}, u32[]{:S(2)}) async-start(f32[16,72,128]{2,1,0:T(8,128)} %get-tuple-element.30), calls=%async_computation.1 | async-start | bytes 1179648 | tf_op jit(solution)/shard_map/all_to_all | solution.py:479
  64.1 0.9 %collective-permute-done.5.payload_a_ref = f32[1040,128]{1,0:T(8,128)S(1)} collective-permute-done((f32[1040,128]{1,0:T(8,128)S(1)}, f32[1040,128]{1,0:T(8,128)S(1)}, u32[]{:S(2)}, u32[]{:S(2)}) %collective-permute-start.5) | collective-permute-done | bytes 532512 | tf_op jit(solution)/shard_map/ppermute | solution.py:467
  64.9 4.0 %collective-permute-start.6 = (f32[1040,128]{1,0:T(8,128)S(1)}, f32[1040,128]{1,0:T(8,128)S(1)}, u32[]{:S(2)}, u32[]{:S(2)}) collective-permute-start(f32[1040,128]{1,0:T(8,128)S(1)} %collective-permute-done.5.payload_a_ref), channel_id=1, source_target_pairs={{0,2},{2,0},{1,3},{3,1},{4,6},{6,4},{5,7},{7,5},{8,10},{10,8},{9,1... | collective-permute-start | bytes 1597448 | tf_op jit(solution)/shard_map/ppermute | solution.py:468
  68.9 2.9 %own_key_grads.1 = (f32[1024,128]{1,0:T(8,128)S(1)}, f32[1024,128]{1,0:T(8,128)S(1)}) custom-call(s32[3]{0:T(128)S(1)} %pad_add_fusion.who_ref, f32[64,1024]{1,0:T(8,128)S(1)} %get-tuple-element.31.index_ref, f32[64,1024]{1,0:T(8,128)S(1)} %copy-done.3, f32[8,128]{1,0:T(8,128)S(1)} %get-tuple-element.32.stats_ref, bf16[2048,128]{1,0:T(8,128)(2,1)S(1)} %copy-done.1, ...), custom_call_target="tpu_custom_call" | custom-call | flops 1073741824 | bytes 4194304 | tf_op jit(solution)/shard_map/own_key_grads/pallas_call | solution.py:415
  71.9 3.4 %key_grads.1 = f32[1024,128]{1,0:T(8,128)} custom-call(f32[1024,128]{1,0:T(8,128)S(1)} %get-tuple-element.34.own_ref, f32[1024,128]{1,0:T(8,128)S(1)} %get-tuple-element.35.gap_ref, bf16[1024,128]{1,0:T(8,128)(2,1)S(1)} %copy-done.2, f32[1040,128]{1,0:T(8,128)S(1)} %collective-permute-done.5.payload_a_ref, f32[1040,128]{1,0:T(8,128)S(1)} %collective-permute-done.6.payload_b_ref), custom_call_target="tpu_custom_call" | custom-call | flops 1073741824 | bytes 4194304 | tf_op jit(solution)/shard_map/key_grads/pallas_call | solution.py:445
  75.9 1.5 %place_mine.1.begun_hbm = f32[64,32,128]{2,1,0:T(8,128)} custom-call(s32[3]{0:T(128)S(1)} %pad_add_fusion.who_ref, f32[16,72,128]{2,1,0:T(8,128)S(1)} %all-to-all-done.1.mine_ref), custom_call_target="tpu_custom_call" | custom-call | tf_op jit(solution)/shard_map/place_mine/pallas_call | solution.py:356
  77.5 1.5 %place_other.1 = (f32[64,32,128]{2,1,0:T(8,128)}, f32[32,64]{1,0:T(8,128)}) custom-call(s32[3]{0:T(128)S(1)} %pad_add_fusion.who_ref, f32[16,72,128]{2,1,0:T(8,128)S(1)} %all-to-all-done.1.mine_ref, f32[16,72,128]{2,1,0:T(8,128)S(1)} %collective-permute-done.7.other_ref, f32[64,32,128]{2,1,0:T(8,128)} %place_mine.1.begun_hbm), custom_call_target="tpu_custom_call", output_to_operand_aliasing={{0}: (3, {})} | custom-call | tf_op jit(solution)/shard_map/place_other/pallas_call | solution.py:368
  (22 shorter events, 2.9 us)
Async XLA Ops:
  0.6 8.1 %copy-start.3 = (f32[64,1024]{1,0:T(8,128)S(1)}, f32[64,1024]{1,0:T(8,128)}, u32[]{:S(2)}) copy-start(f32[64,1024]{1,0:T(8,128)} %target_ref.3) | copy-start | bytes 786436
  0.6 14.2 %copy-start.2 = (bf16[1024,128]{1,0:T(8,128)(2,1)S(1)}, bf16[1024,128]{1,0:T(8,128)(2,1)}, u32[]{:S(2)}) copy-start(bf16[1024,128]{1,0:T(8,128)(2,1)} %k_ref.7) | copy-start | bytes 786436
  4.8 9.1 %collective-permute-start = (f32[64,1024]{1,0:T(8,128)}, f32[64,1024]{1,0:T(8,128)S(1)}, u32[]{:S(2)}, u32[]{:S(2)}) collective-permute-start(f32[64,1024]{1,0:T(8,128)} %get-tuple-element.23.index_ref), channel_id=1, source_target_pairs={{0,1},{1,0},{2,3},{3,2},{4,5},{5,4},{6,7},{7,6},{8,9},{9,8},{10,11... | collective-permute-start | bytes 786440 | tf_op jit(solution)/shard_map/ppermute | solution.py:465
  8.7 1.0 %copy-start = (bf16[2048,128]{1,0:T(8,128)(2,1)S(1)}, bf16[2048,128]{1,0:T(8,128)(2,1)}, u32[]{:S(2)}) copy-start(bf16[2048,128]{1,0:T(8,128)(2,1)} %get-tuple-element.24.q_ref) | copy-start | bytes 1572868
  9.7 0.9 %copy-start.4 = (f32[64,1024]{1,0:T(8,128)S(1)}, f32[64,1024]{1,0:T(8,128)}, u32[]{:S(2)}) copy-start(f32[64,1024]{1,0:T(8,128)} %get-tuple-element.23.index_ref) | copy-start | bytes 786436
  10.7 0.7 copy-start.5
  11.4 3.4 %copy-start.1 = (bf16[2048,128]{1,0:T(8,128)(2,1)S(1)}, bf16[2048,128]{1,0:T(8,128)(2,1)}, u32[]{:S(2)}) copy-start(bf16[2048,128]{1,0:T(8,128)(2,1)} %get-tuple-element.24.q_ref) | copy-start | bytes 1572868
  16.7 4.7 %collective-permute-start.1 = (f32[2056,128]{1,0:T(8,128)S(1)}, f32[2056,128]{1,0:T(8,128)S(1)}, u32[]{:S(2)}, u32[]{:S(2)}) collective-permute-start(f32[2056,128]{1,0:T(8,128)S(1)} %query_sums_send.1), channel_id=1, source_target_pairs={{0,2},{2,0},{1,3},{3,1},{4,6},{6,4},{5,7},{7,5},{8,10},{10,8},{9,1... | collective-permute-start | bytes 3158024 | tf_op jit(solution)/shard_map/ppermute | solution.py:472
  44.4 14.0 %copy-start.6 = (f32[64,32]{0,1:T(8,128)S(1)}, f32[64,32]{0,1:T(8,128)}, u32[]{:S(2)}) copy-start(f32[64,32]{0,1:T(8,128)} %param.5) | copy-start | bytes 24580
  45.1 9.9 %collective-permute-start.2 = (f32[136,128]{1,0:T(8,128)S(1)}, f32[136,128]{1,0:T(8,128)S(1)}, u32[]{:S(2)}, u32[]{:S(2)}) collective-permute-start(f32[136,128]{1,0:T(8,128)S(1)} %combine_near.1.a_ref), channel_id=1, source_target_pairs={{0,64},{64,0},{128,192},{192,128},{1,65},{65,1},{129,193},{193,129... | collective-permute-start | bytes 208904 | tf_op jit(solution)/shard_map/ppermute | solution.py:476
  48.2 7.1 %collective-permute-start.3 = (f32[136,128]{1,0:T(8,128)S(1)}, f32[136,128]{1,0:T(8,128)S(1)}, u32[]{:S(2)}, u32[]{:S(2)}) collective-permute-start(f32[136,128]{1,0:T(8,128)S(1)} %combine_near.1.a_ref), channel_id=1, source_target_pairs={{0,128},{64,192},{128,0},{192,64},{1,129},{65,193},{129,1},{193,65... | collective-permute-start | bytes 208904 | tf_op jit(solution)/shard_map/ppermute | solution.py:476
  52.4 6.0 %collective-permute-start.4 = (f32[136,128]{1,0:T(8,128)S(1)}, f32[136,128]{1,0:T(8,128)S(1)}, u32[]{:S(2)}, u32[]{:S(2)}) collective-permute-start(f32[136,128]{1,0:T(8,128)S(1)} %combine_near.1.a_ref), channel_id=1, source_target_pairs={{0,192},{64,128},{128,64},{192,0},{1,193},{65,129},{129,65},{193,1... | collective-permute-start | bytes 208904 | tf_op jit(solution)/shard_map/ppermute | solution.py:476
  52.4 12.5 %collective-permute-start.5 = (f32[1040,128]{1,0:T(8,128)S(1)}, f32[1040,128]{1,0:T(8,128)S(1)}, u32[]{:S(2)}, u32[]{:S(2)}) collective-permute-start(f32[1040,128]{1,0:T(8,128)S(1)} %get-tuple-element.36), channel_id=1, source_target_pairs={{0,1},{1,0},{2,3},{3,2},{4,5},{5,4},{6,7},{7,6},{8,9},{9,8},{10,11... | collective-permute-start | bytes 1597448 | tf_op jit(solution)/shard_map/ppermute | solution.py:467
  60.3 14.9 %all-to-all-start.1 = ((f32[16,72,128]{2,1,0:T(8,128)}), f32[16,72,128]{2,1,0:T(8,128)S(1)}, u32[]{:S(2)}, u32[]{:S(2)}) async-start(f32[16,72,128]{2,1,0:T(8,128)} %get-tuple-element.30), calls=%async_computation.1 | async-start | bytes 1179648 | tf_op jit(solution)/shard_map/all_to_all | solution.py:479
  64.9 6.9 %collective-permute-start.6 = (f32[1040,128]{1,0:T(8,128)S(1)}, f32[1040,128]{1,0:T(8,128)S(1)}, u32[]{:S(2)}, u32[]{:S(2)}) collective-permute-start(f32[1040,128]{1,0:T(8,128)S(1)} %collective-permute-done.5.payload_a_ref), channel_id=1, source_target_pairs={{0,2},{2,0},{1,3},{3,1},{4,6},{6,4},{5,7},{7,5},{8,10},{10,8},{9,1... | collective-permute-start | bytes 1597448 | tf_op jit(solution)/shard_map/ppermute | solution.py:468
  75.2 2.3 %collective-permute-start.7 = (f32[16,72,128]{2,1,0:T(8,128)S(1)}, f32[16,72,128]{2,1,0:T(8,128)S(1)}, u32[]{:S(2)}, u32[]{:S(2)}) collective-permute-start(f32[16,72,128]{2,1,0:T(8,128)S(1)} %all-to-all-done.1.mine_ref), channel_id=1, source_target_pairs={{0,2},{2,0},{1,3},{3,1},{4,6},{6,4},{5,7},{7,5},{8,10},{10,8},{9,1... | collective-permute-start | bytes 1769480 | tf_op jit(solution)/shard_map/ppermute | solution.py:483

commit v6 on v5

--- a/solution.py
+++ b/solution.py
@@ -15,7 +15,7 @@
 POS = 131072 - T
 SCALE = (D**-0.5) * (H**-0.5)
 CTX = ("zh", "zl", "yl", "x", "c")
-NEAR = ("x", "yl", "zl")
+NEAR = ("x", "zl", "yl")
 FAR = "zh"
 N_NEAR = 16
 N_FAR = 4

time: 80.3 us -> 80.9 us (level)
  starting transfers between devices: 24.5 us -> 25.6 us
    ppermute x1, starting transfers between devices: 0.65 us -> 2.07 us  [on_device(): other = [lax.ppermute(mine, 'c', swap)]]
    ppermute x1, starting transfers between devices: 3.97 us -> 3.11 us  [on_device(): payloads = [payload, lax.ppermute(payload, 'c', swap)]]
where the time goes in v6:
time: 80.9 us; the launch traced here: 80.5 us
  starting transfers between devices  25.6 us (32%)
  blocking collectives  22.9 us (28%)
  Pallas kernels  22.1 us (27%)
  waiting for transfers between devices  6.1 us (8%)
  local copies, waits for them, and re-layouts  2.73 us (3%)
  between operations  0.9 us (1%)
    all_to_all x1, blocking collectives, on_device(): near = lax.all_to_all(pack(keep, recv), NEAR, 0, 0, tiled=True)  22.9 us
    ppermute x3, starting transfers between devices, on_device(): lax.ppermute(own, FAR, [(i, i ^ d) for i in range(N_FAR)])  7.29 us
    all_to_all x1, starting transfers between devices, on_device(): mine = lax.all_to_all(chunk, NEAR, 0, 0, tiled=True)  4.33 us
    pallas_call x1, Pallas kernels, score(): pl.pallas_call(score_kernel, in_specs=[IN_HBM, IN_VMEM, IN_HBM], out_spec...  4.13 us
    ppermute x1, starting transfers between devices, on_device(): other_index = lax.ppermute(partial_index, 'yh', swap)  3.83 us
    pallas_call x2, Pallas kernels, query_sums(): pl.pallas_call(query_kernel, in_specs=[IN_SMEM] + [IN_VMEM] * 4, out_spec...  3.62 us
    ppermute x3, waiting for transfers between devices, on_device(): lax.ppermute(own, FAR, [(i, i ^ d) for i in range(N_FAR)])  3.45 us
    pallas_call x1, Pallas kernels, key_grads(): pl.pallas_call(other_kernel, in_specs=[IN_VMEM] * 5, out_specs=IN_HBM, ou...  3.37 us
  transfers between devices with their start and end apart: 9, of which 6 were waited for; matrix products, arithmetic and copies ran while one was open for 0% of the time, Pallas kernels for 16%

profile of v6, /device:TPU:1, one launch (start us, length us, event | category | flops | bytes accessed | tf_op | source)
XLA Modules:
  0.0 80.5 jit_solution(3999023262170483830)
XLA Ops:
  0.7 4.1 %score.1 = (f32[64,1024]{1,0:T(8,128)}, bf16[2048,128]{1,0:T(8,128)(2,1)}) custom-call(bf16[64,32,128]{2,1,0:T(8,128)(2,1)} %q_hbm.1, f32[32,64]{1,0:T(8,128)} %bitcast.5, bf16[1024,128]{1,0:T(8,128)(2,1)} %k_ref.7), custom_call_target="tpu_custom_call" | custom-call | tf_op jit(solution)/shard_map/score/pallas_call | solution.py:91
  4.8 3.8 %collective-permute-start = (f32[64,1024]{1,0:T(8,128)}, f32[64,1024]{1,0:T(8,128)S(1)}, u32[]{:S(2)}, u32[]{:S(2)}) collective-permute-start(f32[64,1024]{1,0:T(8,128)} %get-tuple-element.23.index_ref), channel_id=1, source_target_pairs={{0,1},{1,0},{2,3},{3,2},{4,5},{5,4},{6,7},{7,6},{8,9},{9,8},{10,11... | collective-permute-start | bytes 786440 | tf_op jit(solution)/shard_map/ppermute | solution.py:465
  8.7 1.0 %copy-done = bf16[2048,128]{1,0:T(8,128)(2,1)S(1)} copy-done((bf16[2048,128]{1,0:T(8,128)(2,1)S(1)}, bf16[2048,128]{1,0:T(8,128)(2,1)}, u32[]{:S(2)}) %copy-start) | copy-done | bytes 524312
  9.7 0.9 %copy-done.4 = f32[64,1024]{1,0:T(8,128)S(1)} copy-done((f32[64,1024]{1,0:T(8,128)S(1)}, f32[64,1024]{1,0:T(8,128)}, u32[]{:S(2)}) %copy-start.4) | copy-done | bytes 262168
  11.4 1.1 %target.1 = (f32[64,1024]{1,0:T(8,128)S(1)}, f32[64,128]{1,0:T(8,128)S(1)}, f32[64,1024]{1,0:T(8,128)S(1)}, bf16[2048,128]{1,0:T(8,128)(2,1)S(1)}, f32[1040,128]{1,0:T(8,128)S(1)}) custom-call(s32[3]{0:T(128)S(1)} %pad_add_fusion.who_ref, f32[64,1024]{1,0:T(8,128)S(1)} %copy-done.3, f32[64,1024]{1,0:T(8,128)S(1)} %copy-done.4, f32[32,64]{1,0:T(8,128)S(1)} %bitcast.6, ...), custom_call_target="tpu_custom_call" | custom-call | tf_op jit(solution)/shard_map/target/pallas_call | solution.py:134
  12.5 1.4 %collective-permute-done.other_ref = f32[64,1024]{1,0:T(8,128)S(1)} collective-permute-done((f32[64,1024]{1,0:T(8,128)}, f32[64,1024]{1,0:T(8,128)S(1)}, u32[]{:S(2)}, u32[]{:S(2)}) %collective-permute-start) | collective-permute-done | bytes 262176 | tf_op jit(solution)/shard_map/ppermute | solution.py:465
  13.9 0.9 %stats.1 = (f32[64,1024]{1,0:T(8,128)S(1)}, f32[8,128]{1,0:T(8,128)S(1)}, bf16[2,64,1024]{2,1,0:T(8,128)(2,1)S(1)}) custom-call(s32[3]{0:T(128)S(1)} %pad_add_fusion.who_ref, f32[64,1024]{1,0:T(8,128)S(1)} %get-tuple-element.25.mine_ref, f32[64,1024]{1,0:T(8,128)S(1)} %collective-permute-done.other_ref, f32[64,1024]{1,0:T(8,128)S(1)} %get-tuple-element.26.target_ref, ...), custom_call_target="tpu_custom_call" | custom-call | tf_op jit(solution)/shard_map/stats/pallas_call | solution.py:174
  14.9 1.8 %query_sums_send.1 = f32[2056,128]{1,0:T(8,128)S(1)} custom-call(s32[1]{0:T(128)S(6)} %sub.3.who_ref, bf16[2,64,1024]{2,1,0:T(8,128)(2,1)S(1)} %get-tuple-element.28.parts_ref, f32[8,128]{1,0:T(8,128)S(1)} %get-tuple-element.29.stats_ref, bf16[2048,128]{1,0:T(8,128)(2,1)S(1)} %copy-done.1, bf16[1024,128]{1,0:T(8,128)(2,1)S(1)} %copy-done.2), custom_call_target="tpu_custom_call" | custom-call | flops 805306368 | bytes 4194304 | tf_op jit(solution)/shard_map/query_sums_send/pallas_call | solution.py:201
  16.7 2.4 %collective-permute-start.1 = (f32[2056,128]{1,0:T(8,128)S(1)}, f32[2056,128]{1,0:T(8,128)S(1)}, u32[]{:S(2)}, u32[]{:S(2)}) collective-permute-start(f32[2056,128]{1,0:T(8,128)S(1)} %query_sums_send.1), channel_id=1, source_target_pairs={{0,2},{2,0},{1,3},{3,1},{4,6},{6,4},{5,7},{7,5},{8,10},{10,8},{9,1... | collective-permute-start | bytes 3158024 | tf_op jit(solution)/shard_map/ppermute | solution.py:472
  19.1 1.8 %query_sums_keep.1.keep_ref = f32[2056,128]{1,0:T(8,128)S(1)} custom-call(s32[1]{0:T(128)} %bitcast.1.who_ref, bf16[2,64,1024]{2,1,0:T(8,128)(2,1)S(1)} %get-tuple-element.28.parts_ref, f32[8,128]{1,0:T(8,128)S(1)} %get-tuple-element.29.stats_ref, bf16[2048,128]{1,0:T(8,128)(2,1)S(1)} %copy-done.1, bf16[1024,128]{1,0:T(8,128)(2,1)S(1)} %copy-done.2), custom_call_target="tpu_custom_call" | custom-call | flops 805306368 | bytes 4194304 | tf_op jit(solution)/shard_map/query_sums_keep/pallas_call | solution.py:201
  21.9 22.9 %all_to_all.10.in_ref = f32[16,136,128]{2,1,0:T(8,128)S(1)} all-to-all(f32[16,136,128]{2,1,0:T(8,128)S(1)} %pack.1), channel_id=1, replica_groups=mesh['zh'=4,'zl'=2,'yl'=2,'x'=4,'c'=2,'yh'=2] {'x','zl','yl'}, dimensions={0} | all-to-all | bytes 2228224 | tf_op jit(solution)/shard_map/all_to_all | solution.py:474
  44.8 0.7 combine_near.1.a_ref
  45.5 3.1 %collective-permute-start.2 = (f32[136,128]{1,0:T(8,128)S(1)}, f32[136,128]{1,0:T(8,128)S(1)}, u32[]{:S(2)}, u32[]{:S(2)}) collective-permute-start(f32[136,128]{1,0:T(8,128)S(1)} %combine_near.1.a_ref), channel_id=1, source_target_pairs={{0,64},{64,0},{128,192},{192,128},{1,65},{65,1},{129,193},{193,129... | collective-permute-start | bytes 208904 | tf_op jit(solution)/shard_map/ppermute | solution.py:476
  48.6 4.2 %collective-permute-start.3 = (f32[136,128]{1,0:T(8,128)S(1)}, f32[136,128]{1,0:T(8,128)S(1)}, u32[]{:S(2)}, u32[]{:S(2)}) collective-permute-start(f32[136,128]{1,0:T(8,128)S(1)} %combine_near.1.a_ref), channel_id=1, source_target_pairs={{0,128},{64,192},{128,0},{192,64},{1,129},{65,193},{129,1},{193,65... | collective-permute-start | bytes 208904 | tf_op jit(solution)/shard_map/ppermute | solution.py:476
  52.8 2.6 %collective-permute-start.5 = (f32[1040,128]{1,0:T(8,128)S(1)}, f32[1040,128]{1,0:T(8,128)S(1)}, u32[]{:S(2)}, u32[]{:S(2)}) collective-permute-start(f32[1040,128]{1,0:T(8,128)S(1)} %get-tuple-element.36), channel_id=1, source_target_pairs={{0,1},{1,0},{2,3},{3,2},{4,5},{5,4},{6,7},{7,6},{8,9},{9,8},{10,11... | collective-permute-start | bytes 1597448 | tf_op jit(solution)/shard_map/ppermute | solution.py:467
  55.7 3.2 %collective-permute-done.4.d_ref = f32[136,128]{1,0:T(8,128)S(1)} collective-permute-done((f32[136,128]{1,0:T(8,128)S(1)}, f32[136,128]{1,0:T(8,128)S(1)}, u32[]{:S(2)}, u32[]{:S(2)}) %collective-permute-start.4) | collective-permute-done | bytes 69664 | tf_op jit(solution)/shard_map/ppermute | solution.py:476
  58.9 1.9 %combine_far.1 = (f32[16,72,128]{2,1,0:T(8,128)}, f32[8,128]{1,0:T(8,128)S(1)}, f32[64]{0:T(128)}) custom-call(s32[3]{0:T(128)S(1)} %pad_add_fusion.who_ref, f32[136,128]{1,0:T(8,128)S(1)} %combine_near.1.a_ref, f32[136,128]{1,0:T(8,128)S(1)} %collective-permute-done.2.b_ref, f32[136,128]{1,0:T(8,128)S(1)} %collective-permute-done.3.c_ref, ...), custom_call_target="tpu_custom_call" | custom-call | tf_op jit(solution)/shard_map/combine_far/pallas_call | solution.py:302
  60.8 4.3 %all-to-all-start.1 = ((f32[16,72,128]{2,1,0:T(8,128)}), f32[16,72,128]{2,1,0:T(8,128)S(1)}, u32[]{:S(2)}, u32[]{:S(2)}) async-start(f32[16,72,128]{2,1,0:T(8,128)} %get-tuple-element.30), calls=%async_computation.1 | async-start | bytes 1179648 | tf_op jit(solution)/shard_map/all_to_all | solution.py:479
  65.7 3.1 %collective-permute-start.6 = (f32[1040,128]{1,0:T(8,128)S(1)}, f32[1040,128]{1,0:T(8,128)S(1)}, u32[]{:S(2)}, u32[]{:S(2)}) collective-permute-start(f32[1040,128]{1,0:T(8,128)S(1)} %collective-permute-done.5.payload_a_ref), channel_id=1, source_target_pairs={{0,2},{2,0},{1,3},{3,1},{4,6},{6,4},{5,7},{7,5},{8,10},{10,8},{9,1... | collective-permute-start | bytes 1597448 | tf_op jit(solution)/shard_map/ppermute | solution.py:468
  68.8 2.9 %own_key_grads.1 = (f32[1024,128]{1,0:T(8,128)S(1)}, f32[1024,128]{1,0:T(8,128)S(1)}) custom-call(s32[3]{0:T(128)S(1)} %pad_add_fusion.who_ref, f32[64,1024]{1,0:T(8,128)S(1)} %get-tuple-element.31.index_ref, f32[64,1024]{1,0:T(8,128)S(1)} %copy-done.3, f32[8,128]{1,0:T(8,128)S(1)} %get-tuple-element.32.stats_ref, bf16[2048,128]{1,0:T(8,128)(2,1)S(1)} %copy-done.1, ...), custom_call_target="tpu_custom_call" | custom-call | flops 1073741824 | bytes 4194304 | tf_op jit(solution)/shard_map/own_key_grads/pallas_call | solution.py:415
  71.8 3.4 %key_grads.1 = f32[1024,128]{1,0:T(8,128)} custom-call(f32[1024,128]{1,0:T(8,128)S(1)} %get-tuple-element.34.own_ref, f32[1024,128]{1,0:T(8,128)S(1)} %get-tuple-element.35.gap_ref, bf16[1024,128]{1,0:T(8,128)(2,1)S(1)} %copy-done.2, f32[1040,128]{1,0:T(8,128)S(1)} %collective-permute-done.5.payload_a_ref, f32[1040,128]{1,0:T(8,128)S(1)} %collective-permute-done.6.payload_b_ref), custom_call_target="tpu_custom_call" | custom-call | flops 1073741824 | bytes 4194304 | tf_op jit(solution)/shard_map/key_grads/pallas_call | solution.py:445
  75.1 2.1 %collective-permute-start.7 = (f32[16,72,128]{2,1,0:T(8,128)S(1)}, f32[16,72,128]{2,1,0:T(8,128)S(1)}, u32[]{:S(2)}, u32[]{:S(2)}) collective-permute-start(f32[16,72,128]{2,1,0:T(8,128)S(1)} %all-to-all-done.1.mine_ref), channel_id=1, source_target_pairs={{0,2},{2,0},{1,3},{3,1},{4,6},{6,4},{5,7},{7,5},{8,10},{10,8},{9,1... | collective-permute-start | bytes 1769480 | tf_op jit(solution)/shard_map/ppermute | solution.py:483
  77.2 1.5 %place_mine.1.begun_hbm = f32[64,32,128]{2,1,0:T(8,128)} custom-call(s32[3]{0:T(128)S(1)} %pad_add_fusion.who_ref, f32[16,72,128]{2,1,0:T(8,128)S(1)} %all-to-all-done.1.mine_ref), custom_call_target="tpu_custom_call" | custom-call | tf_op jit(solution)/shard_map/place_mine/pallas_call | solution.py:356
  78.8 1.5 %place_other.1 = (f32[64,32,128]{2,1,0:T(8,128)}, f32[32,64]{1,0:T(8,128)}) custom-call(s32[3]{0:T(128)S(1)} %pad_add_fusion.who_ref, f32[16,72,128]{2,1,0:T(8,128)S(1)} %all-to-all-done.1.mine_ref, f32[16,72,128]{2,1,0:T(8,128)S(1)} %collective-permute-done.7.other_ref, f32[64,32,128]{2,1,0:T(8,128)} %place_mine.1.begun_hbm), custom_call_target="tpu_custom_call", output_to_operand_aliasing={{0}: (3, {})} | custom-call | tf_op jit(solution)/shard_map/place_other/pallas_call | solution.py:368
  (22 shorter events, 2.9 us)
Async XLA Ops:
  0.6 8.1 %copy-start.3 = (f32[64,1024]{1,0:T(8,128)S(1)}, f32[64,1024]{1,0:T(8,128)}, u32[]{:S(2)}) copy-start(f32[64,1024]{1,0:T(8,128)} %target_ref.3) | copy-start | bytes 786436
  0.6 14.2 %copy-start.2 = (bf16[1024,128]{1,0:T(8,128)(2,1)S(1)}, bf16[1024,128]{1,0:T(8,128)(2,1)}, u32[]{:S(2)}) copy-start(bf16[1024,128]{1,0:T(8,128)(2,1)} %k_ref.7) | copy-start | bytes 786436
  4.8 9.1 %collective-permute-start = (f32[64,1024]{1,0:T(8,128)}, f32[64,1024]{1,0:T(8,128)S(1)}, u32[]{:S(2)}, u32[]{:S(2)}) collective-permute-start(f32[64,1024]{1,0:T(8,128)} %get-tuple-element.23.index_ref), channel_id=1, source_target_pairs={{0,1},{1,0},{2,3},{3,2},{4,5},{5,4},{6,7},{7,6},{8,9},{9,8},{10,11... | collective-permute-start | bytes 786440 | tf_op jit(solution)/shard_map/ppermute | solution.py:465
  8.7 1.0 %copy-start = (bf16[2048,128]{1,0:T(8,128)(2,1)S(1)}, bf16[2048,128]{1,0:T(8,128)(2,1)}, u32[]{:S(2)}) copy-start(bf16[2048,128]{1,0:T(8,128)(2,1)} %get-tuple-element.24.q_ref) | copy-start | bytes 1572868
  9.7 0.9 %copy-start.4 = (f32[64,1024]{1,0:T(8,128)S(1)}, f32[64,1024]{1,0:T(8,128)}, u32[]{:S(2)}) copy-start(f32[64,1024]{1,0:T(8,128)} %get-tuple-element.23.index_ref) | copy-start | bytes 786436
  10.7 0.7 copy-start.5
  11.4 3.4 %copy-start.1 = (bf16[2048,128]{1,0:T(8,128)(2,1)S(1)}, bf16[2048,128]{1,0:T(8,128)(2,1)}, u32[]{:S(2)}) copy-start(bf16[2048,128]{1,0:T(8,128)(2,1)} %get-tuple-element.24.q_ref) | copy-start | bytes 1572868
  16.7 4.7 %collective-permute-start.1 = (f32[2056,128]{1,0:T(8,128)S(1)}, f32[2056,128]{1,0:T(8,128)S(1)}, u32[]{:S(2)}, u32[]{:S(2)}) collective-permute-start(f32[2056,128]{1,0:T(8,128)S(1)} %query_sums_send.1), channel_id=1, source_target_pairs={{0,2},{2,0},{1,3},{3,1},{4,6},{6,4},{5,7},{7,5},{8,10},{10,8},{9,1... | collective-permute-start | bytes 3158024 | tf_op jit(solution)/shard_map/ppermute | solution.py:472
  44.8 14.1 %copy-start.6 = (f32[64,32]{0,1:T(8,128)S(1)}, f32[64,32]{0,1:T(8,128)}, u32[]{:S(2)}) copy-start(f32[64,32]{0,1:T(8,128)} %param.5) | copy-start | bytes 24580
  45.5 9.9 %collective-permute-start.2 = (f32[136,128]{1,0:T(8,128)S(1)}, f32[136,128]{1,0:T(8,128)S(1)}, u32[]{:S(2)}, u32[]{:S(2)}) collective-permute-start(f32[136,128]{1,0:T(8,128)S(1)} %combine_near.1.a_ref), channel_id=1, source_target_pairs={{0,64},{64,0},{128,192},{192,128},{1,65},{65,1},{129,193},{193,129... | collective-permute-start | bytes 208904 | tf_op jit(solution)/shard_map/ppermute | solution.py:476
  48.6 7.1 %collective-permute-start.3 = (f32[136,128]{1,0:T(8,128)S(1)}, f32[136,128]{1,0:T(8,128)S(1)}, u32[]{:S(2)}, u32[]{:S(2)}) collective-permute-start(f32[136,128]{1,0:T(8,128)S(1)} %combine_near.1.a_ref), channel_id=1, source_target_pairs={{0,128},{64,192},{128,0},{192,64},{1,129},{65,193},{129,1},{193,65... | collective-permute-start | bytes 208904 | tf_op jit(solution)/shard_map/ppermute | solution.py:476
  52.8 6.1 %collective-permute-start.4 = (f32[136,128]{1,0:T(8,128)S(1)}, f32[136,128]{1,0:T(8,128)S(1)}, u32[]{:S(2)}, u32[]{:S(2)}) collective-permute-start(f32[136,128]{1,0:T(8,128)S(1)} %combine_near.1.a_ref), channel_id=1, source_target_pairs={{0,192},{64,128},{128,64},{192,0},{1,193},{65,129},{129,65},{193,1... | collective-permute-start | bytes 208904 | tf_op jit(solution)/shard_map/ppermute | solution.py:476
  52.8 12.9 %collective-permute-start.5 = (f32[1040,128]{1,0:T(8,128)S(1)}, f32[1040,128]{1,0:T(8,128)S(1)}, u32[]{:S(2)}, u32[]{:S(2)}) collective-permute-start(f32[1040,128]{1,0:T(8,128)S(1)} %get-tuple-element.36), channel_id=1, source_target_pairs={{0,1},{1,0},{2,3},{3,2},{4,5},{5,4},{6,7},{7,6},{8,9},{9,8},{10,11... | collective-permute-start | bytes 1597448 | tf_op jit(solution)/shard_map/ppermute | solution.py:467
  60.8 14.4 %all-to-all-start.1 = ((f32[16,72,128]{2,1,0:T(8,128)}), f32[16,72,128]{2,1,0:T(8,128)S(1)}, u32[]{:S(2)}, u32[]{:S(2)}) async-start(f32[16,72,128]{2,1,0:T(8,128)} %get-tuple-element.30), calls=%async_computation.1 | async-start | bytes 1179648 | tf_op jit(solution)/shard_map/all_to_all | solution.py:479
  65.7 6.0 %collective-permute-start.6 = (f32[1040,128]{1,0:T(8,128)S(1)}, f32[1040,128]{1,0:T(8,128)S(1)}, u32[]{:S(2)}, u32[]{:S(2)}) collective-permute-start(f32[1040,128]{1,0:T(8,128)S(1)} %collective-permute-done.5.payload_a_ref), channel_id=1, source_target_pairs={{0,2},{2,0},{1,3},{3,1},{4,6},{6,4},{5,7},{7,5},{8,10},{10,8},{9,1... | collective-permute-start | bytes 1597448 | tf_op jit(solution)/shard_map/ppermute | solution.py:468
  75.1 3.7 %collective-permute-start.7 = (f32[16,72,128]{2,1,0:T(8,128)S(1)}, f32[16,72,128]{2,1,0:T(8,128)S(1)}, u32[]{:S(2)}, u32[]{:S(2)}) collective-permute-start(f32[16,72,128]{2,1,0:T(8,128)S(1)} %all-to-all-done.1.mine_ref), channel_id=1, source_target_pairs={{0,2},{2,0},{1,3},{3,1},{4,6},{6,4},{5,7},{7,5},{8,10},{10,8},{9,1... | collective-permute-start | bytes 1769480 | tf_op jit(solution)/shard_map/ppermute | solution.py:483
